TPU v7x, 32 devices: a whole 2x2x4 slice. The times are simulated.
32 devices in a mesh: dp: 8 (over z, x), tensor: 4 (over y, core).
Axes of the slice: x: 2, y: 2, z: 4, core: 2. Of those that a mesh axis runs over, the one named last changes fastest.
Arguments:
- hidden_states: bfloat16 [1024, 6144], P('dp', 'tensor'), may hold values from -9 to 9
- expert_ids: int32 [1024, 2], P('dp'), may hold values from 0 to 7, as said below
- route_gates: float32 [1024, 2], P('dp'), may hold values from 0.1 to 0.9
- gate_weight: bfloat16 [6144, 16384], P('tensor', 'dp'), may hold values from -0.078125 to 0.078125
- up_weight: bfloat16 [6144, 16384], P('tensor', 'dp'), may hold values from -0.078125 to 0.078125
Outputs:
- covariance: float32 [16384, 16384], P('tensor', 'dp')
Inputs may be any that keep to these rules, and one draw needn't show every extreme that they name: `expert_ids`: each row names two different experts. Among the 128 rows of one device (aligned blocks), expert 0 is named by at most 32 rows, by exactly 32 rows in at least one block, and by at least one row in every block.
All inputs are finite; a program needn't handle non-finite values.
Results may differ from a plain program's by a relative error of at most 0.0057.
Values may be sent and summed in bfloat16 or wider, within the bound.
No kernel may reach another device: no remote copies, remote signals or barrier semaphores. Data moves between devices by JAX's collectives and lax.ppermute only.
A program may use at most 128 MiB of HBM per device.

v0:
```python
import jax
import jax.numpy as jnp
from jax import lax
from jax.sharding import PartitionSpec as P

CAP = 32


def pack_rows(token_blocks, weight_blocks):
    member = (weight_blocks > 0).astype(jnp.int32)
    position = jnp.cumsum(member, axis=1) - 1
    slot_index = lax.broadcasted_iota(jnp.int32, (1, CAP, 1), 1)
    picked = (position[:, None, :] == slot_index) & (member[:, None, :] > 0)
    selector = picked.astype(jnp.bfloat16)
    packed = jnp.einsum(
        "sct,std->scd", selector, token_blocks, preferred_element_type=jnp.float32
    ).astype(jnp.bfloat16)
    packed_weight = jnp.einsum(
        "sct,st->sc", selector, weight_blocks, preferred_element_type=jnp.float32
    ).astype(jnp.bfloat16)
    return (packed.reshape(-1, token_blocks.shape[2]), packed_weight.reshape(-1))


def shards(hidden_states, expert_ids, route_gates, gate_weight, up_weight):
    route_weight = jnp.sum(
        jnp.where(expert_ids == 0, route_gates, jnp.zeros_like(route_gates)), axis=1
    ).astype(jnp.bfloat16)
    own_rows, own_weight = pack_rows(hidden_states[None], route_weight[None])
    packed_rows, packed_weight = (
        lax.all_gather(own_rows, "dp", axis=0, tiled=True),
        lax.all_gather(own_weight, "dp", axis=0, tiled=True),
    )
    weight_total = jnp.sum(packed_weight.astype(jnp.float32))
    gate_part = jnp.dot(packed_rows, gate_weight, preferred_element_type=jnp.float32)
    up_part = jnp.dot(packed_rows, up_weight, preferred_element_type=jnp.float32)
    summed = lax.psum_scatter(
        jnp.concatenate([gate_part, up_part], axis=1), "tensor", scatter_dimension=0, tiled=True
    )
    unit_width = gate_weight.shape[1]
    local_keys = (jax.nn.silu(summed[:, :unit_width]) * summed[:, unit_width:]).astype(jnp.bfloat16)
    column_keys = lax.all_gather(local_keys, "tensor", axis=0, tiled=True)
    weighted = (
        packed_weight.astype(jnp.float32)[:, None] * column_keys.astype(jnp.float32)
    ).astype(jnp.bfloat16)
    spread_keys = lax.all_gather(local_keys, "dp", axis=1, tiled=True)
    row_keys = lax.all_to_all(spread_keys, "tensor", split_axis=1, concat_axis=0, tiled=True)
    covariance = lax.dot_general(
        row_keys, weighted, (((0,), (0,)), ((), ())), preferred_element_type=jnp.float32
    )
    return covariance / weight_total


def solution(mesh):
    placed = (P("dp", "tensor"), P("dp", None), P("dp", None), P("tensor", "dp"), P("tensor", "dp"))
    return jax.shard_map(
        shards, mesh=mesh, in_specs=placed, out_specs=P("tensor", "dp"), check_vma=False
    )
```

profile of v0, /device:TPU:12, one launch (start us, length us, event | category | flops | bytes accessed | tf_op | source)
XLA Modules:
  0.0 206.2 jit_solution(15877365630926725277)
XLA Ops:
  6.5 0.0 copy-start
  6.5 0.0 reduce-scatter.2.cloned.1.call-start
  6.5 0.8 fusion.10
  7.3 0.1 copy.7
  7.4 0.2 reduce-window.7
  7.6 0.1 add_reduce_fusion
  7.7 0.0 copy-done
  7.7 0.2 convolution_convert_fusion
  7.9 0.0 slice-start
  7.9 29.9 %all_gather.12 = bf16[256,1536]{1,0:T(8,128)(2,1)S(1)} all-gather(bf16[32,1536]{1,0:T(8,128)(2,1)S(1)} %convolution_convert_fusion), channel_id=1, replica_groups=mesh['dp'=8,'tensor'=4] {'dp'}, dimensions={0}, use_global_device_ids=true | all-gather | bytes 884736 | tf_op jit(solution)/shard_map/all_gather | solution.py:30
  37.8 4.8 %fusion.14 = f32[256,2048]{1,0:T(8,128)S(1)} fusion(bf16[256,1536]{1,0:T(8,128)(2,1)S(1)} %all_gather.12, bf16[1536,2048]{1,0:T(8,128)(2,1)} %param.9), kind=kOutput, calls=%fused_computation.25 | convolution fusion | flops 1610612736 | bytes 9175040 | tf_op jit(solution)/shard_map/dot_general | solution.py:35
  42.6 0.0 slice-done
  42.7 0.0 slice-done.1
  42.7 1.8 fusion.13
  44.5 2.5 %pad_maximum_fusion = f32[256,4096]{1,0:T(8,128)} fusion(f32[256,2048]{1,0:T(8,128)S(1)} %fusion.14, f32[256,2048]{1,0:T(8,128)S(1)} %fusion.13), kind=kLoop, calls=%fused_computation.1 | loop fusion | flops 1048576 | bytes 8388608 | tf_op jit(solution)/shard_map/concatenate | solution.py:37
  46.9 0.0 reduce-scatter.2.cloned.1.call-update
  47.0 0.0 all-gather.3.cloned.1.call-start
  47.0 47.1 %reduce-scatter.2.cloned.1.call-done = f32[64,4096]{1,0:T(8,128)} async-done(((f32[256,4096]{1,0:T(8,128)}), f32[64,4096]{1,0:T(8,128)}) %reduce-scatter.2.cloned.1.call-update) | async-done | bytes 1048592 | tf_op jit(solution)/shard_map/reduce_scatter | solution.py:36
  94.2 2.1 fusion.2
  96.2 0.0 all-gather.3.cloned.1.call-update
  96.2 0.0 all-gather.5.cloned.1.call-start
  96.3 0.7 all-gather.5.cloned.1.call-update
  97.0 49.8 %all-gather.3.cloned.1.call-done = bf16[64,16384]{1,0:T(8,128)(2,1)} async-done(((bf16[64,2048]{1,0:T(8,128)(2,1)}), bf16[64,16384]{1,0:T(8,128)(2,1)}) %all-gather.3.cloned.1.call-update) | async-done | bytes 2097168 | tf_op jit(solution)/shard_map/all_gather | solution.py:45
  146.8 3.1 %copy.11 = bf16[8,4,8,4096]{3,2,0,1:T(8,128)(2,1)} copy(bf16[8,4,8,4096]{3,2,1,0:T(8,128)(2,1)} %bitcast.24) | data formatting | bytes 4194304 | tf_op jit(solution)/shard_map/all_to_all | solution.py:46
  149.9 4.1 %all-to-all-start = ((bf16[64,4,4096]{2,0,1:T(8,128)(2,1)}), bf16[64,4,4096]{2,0,1:T(8,128)(2,1)S(1)}, u32[]{:S(2)}, u32[]{:S(2)}) async-start(bf16[64,4,4096]{2,0,1:T(8,128)(2,1)} %bitcast.22), calls=%async_computation.1 | async-start | bytes 4194304 | tf_op jit(solution)/shard_map/all_to_all | solution.py:46
  154.1 0.6 dynamic-slice
  155.2 0.1 fusion
  155.3 0.2 dynamic-update-slice
  155.5 16.2 %all-reduce = bf16[256]{0:T(256)(128)(2,1)S(1)} all-reduce(bf16[256]{0:T(256)(128)(2,1)S(1)} %dynamic-update-slice), channel_id=1, replica_groups=mesh['dp'=8,'tensor'=4] {'dp'}, use_global_device_ids=true, to_apply=%add | all-reduce | flops 256 | bytes 1024
  171.7 0.6 convert_reduce_fusion
  172.3 11.4 %all-to-all-done = bf16[64,4,4096]{2,0,1:T(8,128)(2,1)S(1)} async-done(((bf16[64,4,4096]{2,0,1:T(8,128)(2,1)}), bf16[64,4,4096]{2,0,1:T(8,128)(2,1)S(1)}, u32[]{:S(2)}, u32[]{:S(2)}) %all-to-all-start) | async-done | bytes 2097184 | tf_op jit(solution)/shard_map/all_to_all | solution.py:46
  183.7 16.0 %broadcast_divide_fusion = f32[4096,2048]{1,0:T(8,128)} fusion(f32[]{:T(128)} %convert_reduce_fusion, bf16[256,4096]{1,0:T(8,128)(2,1)S(1)} %bitcast.23, bf16[256,2048]{1,0:T(8,128)(2,1)} %all-gather.5.cloned.1.call-done, f32[256]{0:T(256)S(1)} %convert_element_type.72), kind=kOutput, calls=%fused_computation | convolution fusion | flops 4304928768 | bytes 36701188 | tf_op jit(solution)/shard_map/dot_general | solution.py:47
  (8 shorter events, 0.0 us)
Async XLA Ops:
  6.5 1.2 copy-start
  6.5 87.6 %reduce-scatter.2.cloned.1.call-start = ((), (), s32[]{:S(2)}) async-start(), calls=%async_computation.2 | async-start | bytes 5242880 | tf_op jit(solution)/shard_map/reduce_scatter | solution.py:36
  7.9 34.8 %slice-start = ((s8[6291456]{0:T(1024)(128)(4,1)}), s8[4194304]{0:T(1024)(128)(4,1)S(1)}, s32[]{:S(2)}) async-start(s8[6291456]{0:T(1024)(128)(4,1)} %bitcast.25), calls=%async_computation.5 | async-start | bytes 8388608
  37.8 4.8 %slice-start.1 = ((s8[6291456]{0:T(1024)(128)(4,1)}), s8[2097152]{0:T(1024)(128)(4,1)S(1)}, s32[]{:S(2)}) async-start(s8[6291456]{0:T(1024)(128)(4,1)} %bitcast.25), calls=%async_computation.6 | async-start | bytes 4194304
  47.0 99.8 %all-gather.3.cloned.1.call-start = ((), (), s32[]{:S(2)}) async-start(), calls=%async_computation.3 | async-start | bytes 2359296 | tf_op jit(solution)/shard_map/all_gather | solution.py:45
  96.2 76.1 %all-gather.5.cloned.1.call-start = ((), (), s32[]{:S(2)}) async-start(), calls=%async_computation.4 | async-start | bytes 1310720 | tf_op jit(solution)/shard_map/all_gather | solution.py:41
  146.8 7.3 %copy-start.1 = (u32[32]{0:T(128)S(1)}, u32[32]{0:T(128)}, u32[]{:S(2)}) copy-start(u32[32]{0:T(128)} %constant.19) | copy-start | bytes 388
  149.9 33.8 %all-to-all-start = ((bf16[64,4,4096]{2,0,1:T(8,128)(2,1)}), bf16[64,4,4096]{2,0,1:T(8,128)(2,1)S(1)}, u32[]{:S(2)}, u32[]{:S(2)}) async-start(bf16[64,4,4096]{2,0,1:T(8,128)(2,1)} %bitcast.22), calls=%async_computation.1 | async-start | bytes 4194304 | tf_op jit(solution)/shard_map/all_to_all | solution.py:46
Sparse Core Ops, SparseCore 0:
  47.1 47.0 reduce-scatter.1
  96.6 50.1 all-gather.2
  148.4 19.9 all-gather.4
where the time goes:
time: 209 us; the launch traced here: 206 us
  waiting for transfers between devices  109 us (52%)
  blocking collectives  46.1 us (22%)
  matrix products  22.9 us (11%)
  between operations  13.7 us (7%)
  other arithmetic  6.19 us (3%)
  starting transfers between devices  4.22 us (2%)
  local copies, waits for them, and re-layouts  4.04 us (2%)
    all_gather x1, waiting for transfers between devices, shards(): spread_keys = lax.all_gather(local_keys, 'dp', axis=1, tiled=True)  49.8 us
    reduce_scatter x1, waiting for transfers between devices, shards(): lax.psum_scatter(jnp.concatenate([gate_part, up_part], axis=1), 'tensor',...  47.1 us
    all_gather x1, blocking collectives, shards(): lax.all_gather(own_rows, 'dp', axis=0, tiled=True)  29.9 us
    unnamed x1, blocking collectives  16.2 us
    dot_general x1, matrix products, shards(): lax.dot_general(row_keys, weighted, (((0,), (0,)), ((), ())), preferred_e...  16 us
    all_to_all x1, waiting for transfers between devices, shards(): lax.all_to_all(spread_keys, 'tensor', split_axis=1, concat_axis=0, tiled=...  11.4 us
    dot_general x1, matrix products, shards(): jnp.dot(packed_rows, up_weight, preferred_element_type=jnp.float32)  4.83 us
  transfers between devices with their start and end apart: 4, of which 3 were waited for; matrix products, arithmetic and copies ran while one was open for 2% of the time, Pallas kernels for 0%

commit v1 on v0

v1 whole, which is shorter than its diff:
```python
import jax
import jax.numpy as jnp
from jax import lax
from jax.experimental import pallas as pl
from jax.experimental.pallas import tpu as pltpu
from jax.sharding import PartitionSpec as P

CAP = 32
LANES = 128
BF, F32 = jnp.bfloat16, jnp.float32
AXES = ("dp", "tensor")
ROWS_OF = (((0,), (0,)), ((), ()))


def pack_rows(token_blocks, weight_blocks):
    member = (weight_blocks > 0).astype(jnp.int32)
    position = jnp.cumsum(member, axis=1) - 1
    slot_index = lax.broadcasted_iota(jnp.int32, (1, CAP, 1), 1)
    picked = (position[:, None, :] == slot_index) & (member[:, None, :] > 0)
    selector = picked.astype(BF)
    packed = jnp.einsum(
        "sct,std->scd", selector, token_blocks, preferred_element_type=F32
    ).astype(BF)
    packed_weight = jnp.einsum(
        "sct,st->sc", selector, weight_blocks, preferred_element_type=F32
    ).astype(BF)
    return (packed.reshape(-1, token_blocks.shape[2]), packed_weight.reshape(-1))


def any_mesh(hidden_states, expert_ids, route_gates, gate_weight, up_weight):
    route_weight = jnp.sum(
        jnp.where(expert_ids == 0, route_gates, jnp.zeros_like(route_gates)), axis=1
    ).astype(BF)
    own_rows, own_weight = pack_rows(hidden_states[None], route_weight[None])
    packed_rows, packed_weight = (
        lax.all_gather(own_rows, "dp", axis=0, tiled=True),
        lax.all_gather(own_weight, "dp", axis=0, tiled=True),
    )
    weight_total = jnp.sum(packed_weight.astype(F32))
    gate_part = jnp.dot(packed_rows, gate_weight, preferred_element_type=F32)
    up_part = jnp.dot(packed_rows, up_weight, preferred_element_type=F32)
    summed = lax.psum_scatter(
        jnp.concatenate([gate_part, up_part], axis=1), "tensor", scatter_dimension=0, tiled=True
    )
    unit_width = gate_weight.shape[1]
    local_keys = (jax.nn.silu(summed[:, :unit_width]) * summed[:, unit_width:]).astype(BF)
    column_keys = lax.all_gather(local_keys, "tensor", axis=0, tiled=True)
    weighted = (packed_weight.astype(F32)[:, None] * column_keys.astype(F32)).astype(BF)
    spread_keys = lax.all_gather(local_keys, "dp", axis=1, tiled=True)
    row_keys = lax.all_to_all(spread_keys, "tensor", split_axis=1, concat_axis=0, tiled=True)
    covariance = lax.dot_general(row_keys, weighted, ROWS_OF, preferred_element_type=F32)
    return covariance / weight_total


def pairs(to):
    number = lambda z, x, y, c: z * 8 + x * 4 + y * 2 + c
    out = []
    for z in range(4):
        for x in range(2):
            for y in range(2):
                for c in range(2):
                    there = to(z, x, y, c)
                    if there is not None:
                        out.append((number(z, x, y, c), number(*there)))
    return out


CORE = pairs(lambda z, x, y, c: (z, x, y, 1 - c))
Y = pairs(lambda z, x, y, c: (z, x, 1 - y, c))
X = pairs(lambda z, x, y, c: (z, 1 - x, y, c))
Z1 = pairs(lambda z, x, y, c: (z ^ 1, x, y, c))
Z2 = pairs(lambda z, x, y, c: (z ^ 2, x, y, c))
XZ1 = pairs(lambda z, x, y, c: (z ^ 1, 1 - x, y, c))
HOME_Z2 = pairs(lambda z, x, y, c: (z ^ 2, x, y, c) if c == z % 2 else None)
HOME_Y = pairs(lambda z, x, y, c: (z, x, 1 - y, c) if c == z % 2 and y == z // 2 else None)
HOME_Z1 = pairs(lambda z, x, y, c: (z ^ 1, x, y, c) if c == z % 2 else None)


def send(value, route):
    return lax.ppermute(value, AXES, route)


def pack_kernel(ids_ref, gates_ref, tokens_ref, out_ref):
    tokens, width = tokens_ref.shape
    weight = jnp.sum(
        jnp.where(ids_ref[...] == 0, gates_ref[...], 0.0), axis=1, keepdims=True
    ).astype(BF)
    member = weight.astype(F32) > 0
    earlier = lax.broadcasted_iota(jnp.int32, (tokens, tokens), 1) <= lax.broadcasted_iota(
        jnp.int32, (tokens, tokens), 0
    )
    spread = jnp.broadcast_to(member.astype(F32), (tokens, LANES)).astype(BF)
    position = jnp.dot(earlier.astype(BF), spread, preferred_element_type=F32) - 1.0
    slot = lax.broadcasted_iota(jnp.int32, (tokens, CAP), 1).astype(F32)
    picked = jnp.where((position[:, :CAP] == slot) & member, 1.0, 0.0).astype(BF)
    out_ref[:, :width] = lax.dot_general(
        picked, tokens_ref[...], ROWS_OF, preferred_element_type=F32
    ).astype(BF)
    weights = jnp.broadcast_to(weight, (tokens, LANES))
    out_ref[:, width:] = lax.dot_general(
        picked, weights, ROWS_OF, preferred_element_type=F32
    ).astype(BF)


def pack(hidden_states, expert_ids, route_gates):
    return pl.pallas_call(
        pack_kernel,
        out_shape=jax.ShapeDtypeStruct((CAP, hidden_states.shape[1] + LANES), BF),
    )(expert_ids, route_gates, hidden_states)


def half(flag, value, width):
    return jnp.where(flag == 0, value[..., :width], value[..., width:])


def fast(hidden_states, expert_ids, route_gates, gate_weight, up_weight):
    depth, units = gate_weight.shape
    dp, tensor = lax.axis_index("dp"), lax.axis_index("tensor")
    z, x, y, core = dp // 2, dp % 2, tensor // 2, tensor % 2
    home, inside = core == z % 2, y == z // 2

    own = pack(hidden_states, expert_ids, route_gates)
    far = send(own, Z2)
    place = (z % 2) * 2 + x

    def chunk(mine):
        beside = {1: send(mine, X), 2: send(mine, Z1), 3: send(mine, XZ1)}
        beside[0] = mine
        rows = []
        for at in range(4):
            differs = place ^ at
            block = beside[0]
            for k in (1, 2, 3):
                block = jnp.where(differs == k, beside[k], block)
            rows.append(block)
        return jnp.concatenate(rows, axis=0)

    def keys_of(tokens):
        rows = tokens[:, :depth]
        parts = jnp.stack(
            [
                jnp.dot(rows, gate_weight, preferred_element_type=F32),
                jnp.dot(rows, up_weight, preferred_element_type=F32),
            ]
        )
        quarter = units // 4
        parts = parts.reshape(2, rows.shape[0], 4, quarter)
        kept = jnp.where(core == 0, parts[:, :, 0::2], parts[:, :, 1::2])
        given = jnp.where(core == 0, parts[:, :, 1::2], parts[:, :, 0::2]).astype(BF)
        summed = kept + send(given, CORE).astype(F32)
        kept = jnp.where(y == 0, summed[:, :, 0], summed[:, :, 1])
        given = jnp.where(y == 0, summed[:, :, 1], summed[:, :, 0]).astype(BF)
        total = kept + send(given, Y).astype(F32)
        return (jax.nn.silu(total[0]) * total[1]).astype(BF)

    def spread(quarter):
        across = send(quarter, Y)
        both = jnp.stack([quarter, across])
        other = send(both, CORE)
        low, high = jnp.where(core == 0, both, other), jnp.where(core == 0, other, both)
        halves = jnp.concatenate([low, high], axis=2)
        mine, others = halves[0], halves[1]
        got = send(mine, HOME_Z2)
        got_across = send(got, HOME_Y)
        mine_s = jnp.where(inside, mine, got)
        others_s = jnp.where(inside, others, got_across)
        own_slice = jnp.concatenate(
            [jnp.where(y == 0, mine, others), jnp.where(y == 0, others, mine)], axis=1
        )
        panel = jnp.concatenate(
            [jnp.where(y == 0, mine_s, others_s), jnp.where(y == 0, others_s, mine_s)], axis=1
        )
        panel = jnp.where(home, panel, send(panel, HOME_Z1))
        return own_slice, panel, send(panel, X)

    tokens = [chunk(own), chunk(far)]
    weights = [each[:, depth : depth + 1].astype(F32) for each in tokens]
    weight_total = jnp.sum(weights[0]) + jnp.sum(weights[1])
    parts = [spread(keys_of(each)) for each in tokens]
    weighted = [(w * p[0].astype(F32)).astype(BF) for w, p in zip(weights, parts)]
    columns = jnp.concatenate(
        [
            jnp.where(inside, weighted[0], weighted[1]),
            jnp.where(inside, weighted[1], weighted[0]),
        ]
    )
    panel_own = jnp.concatenate([p[1] for p in parts])
    panel_other = jnp.concatenate([p[2] for p in parts])
    panel = jnp.concatenate(
        [jnp.where(x == 0, panel_own, panel_other), jnp.where(x == 0, panel_other, panel_own)],
        axis=1,
    )
    covariance = lax.dot_general(panel, columns, ROWS_OF, preferred_element_type=F32)
    return covariance / weight_total


def solution(mesh):
    placed = (P("dp", "tensor"), P("dp", None), P("dp", None), P("tensor", "dp"), P("tensor", "dp"))
    sizes = (mesh.shape["dp"], mesh.shape["tensor"])
    return jax.shard_map(
        fast if sizes == (8, 4) else any_mesh,
        mesh=mesh,
        in_specs=placed,
        out_specs=P("tensor", "dp"),
        check_vma=False,
    )
```

time: 209 us -> 146 us (0.70)
  the two profiles are of different devices: /device:TPU:12 before, /device:TPU:0 now
where the time goes in v1:
time: 146 us; the launch traced here: 145 us
  waiting for transfers between devices  53 us (36%)
  starting transfers between devices  35.7 us (24%)
  matrix products  28.7 us (20%)
  local copies, waits for them, and re-layouts  13.9 us (10%)
  other arithmetic  9.94 us (7%)
  Pallas kernels  2.17 us (1%)
  between operations  1.78 us (1%)
    ppermute x23, waiting for transfers between devices, send(): return lax.ppermute(value, AXES, route)  53 us
    ppermute x23, starting transfers between devices, send(): return lax.ppermute(value, AXES, route)  35.7 us
    dot_general x1, matrix products, fast(): lax.dot_general(panel, columns, ROWS_OF, preferred_element_type=F32)  14.2 us
    dot_general x2, matrix products, keys_of(): jnp.dot(rows, up_weight, preferred_element_type=F32)  8.76 us
    another operation x6, local copies, waits for them, and re-layouts, keys_of(): jnp.stack([jnp.dot(rows, gate_weight, preferred_element_type=F32), jnp.do...  7.85 us
    unnamed x27, local copies, waits for them, and re-layouts  6.03 us
    dot_general x2, matrix products, keys_of(): jnp.dot(rows, gate_weight, preferred_element_type=F32)  5.73 us
  transfers between devices with their start and end apart: 23, of which 16 were waited for; matrix products, arithmetic and copies ran while one was open for 24% of the time, Pallas kernels for 0%

profile of v1, /device:TPU:0, one launch (start us, length us, event | category | flops | bytes accessed | tf_op | source)
XLA Modules:
  0.0 145.2 jit_solution(9412719213052756200)
XLA Ops:
  2.8 2.2 %shard_map.55 = bf16[32,1664]{1,0:T(8,128)(2,1)} custom-call(s32[128,2]{1,0:T(8,128)} %copy.19.ids_ref, f32[128,2]{1,0:T(8,128)} %copy.20.gates_ref, bf16[128,1536]{1,0:T(8,128)(2,1)} %tokens_ref.1), custom_call_target="tpu_custom_call" | custom-call | tf_op jit(solution)/shard_map/pallas_call | solution.py:106
  5.0 2.9 %collective-permute-start.2 = (bf16[32,1664]{1,0:T(8,128)(2,1)}, bf16[32,1664]{1,0:T(8,128)(2,1)S(1)}, u32[]{:S(2)}, u32[]{:S(2)}) collective-permute-start(bf16[32,1664]{1,0:T(8,128)(2,1)} %shard_map.55), channel_id=1, source_target_pairs={{0,4},{1,5},{2,6},{3,7},{4,0},{5,1},{6,2},{7,3},{8,12},{9,13},{10,... | collective-permute-start | bytes 319496 | tf_op jit(solution)/shard_map/ppermute | solution.py:80
  7.9 1.6 %collective-permute-start.1 = (bf16[32,1664]{1,0:T(8,128)(2,1)}, bf16[32,1664]{1,0:T(8,128)(2,1)S(1)}, u32[]{:S(2)}, u32[]{:S(2)}) collective-permute-start(bf16[32,1664]{1,0:T(8,128)(2,1)} %shard_map.55), channel_id=1, source_target_pairs={{0,8},{1,9},{2,10},{3,11},{4,12},{5,13},{6,14},{7,15},{8,0},{9,1},... | collective-permute-start | bytes 319496 | tf_op jit(solution)/shard_map/ppermute | solution.py:80
  9.5 3.0 %collective-permute-start.10 = (bf16[32,1664]{1,0:T(8,128)(2,1)}, bf16[32,1664]{1,0:T(8,128)(2,1)}, u32[]{:S(2)}, u32[]{:S(2)}) collective-permute-start(bf16[32,1664]{1,0:T(8,128)(2,1)} %shard_map.55), channel_id=1, source_target_pairs={{0,16},{1,17},{2,18},{3,19},{4,20},{5,21},{6,22},{7,23},{8,24},{9,... | collective-permute-start | bytes 319496 | tf_op jit(solution)/shard_map/ppermute | solution.py:80
  12.5 3.6 %collective-permute-done.1 = bf16[32,1664]{1,0:T(8,128)(2,1)S(1)} collective-permute-done((bf16[32,1664]{1,0:T(8,128)(2,1)}, bf16[32,1664]{1,0:T(8,128)(2,1)S(1)}, u32[]{:S(2)}, u32[]{:S(2)}) %collective-permute-start.1) | collective-permute-done | bytes 106528 | tf_op jit(solution)/shard_map/ppermute | solution.py:80
  17.5 3.8 %fusion.10 = f32[128,2048]{1,0:T(8,128)S(1)} fusion(bf16[1536,2048]{1,0:T(8,128)(2,1)} %param.9, bf16[128,1664]{1,0:T(8,128)(2,1)S(1)} %pad_maximum_fusion.3), kind=kOutput, calls=%fused_computation.40 | convolution fusion | flops 805306368 | bytes 7733248 | tf_op jit(solution)/shard_map/dot_general | solution.py:143
  22.0 3.8 %fusion.12 = f32[128,2048]{1,0:T(8,128)S(1)} fusion(bf16[1536,2048]{1,0:T(8,128)(2,1)} %param.8, bf16[128,1664]{1,0:T(8,128)(2,1)S(1)} %pad_maximum_fusion.3), kind=kOutput, calls=%fused_computation.42 | convolution fusion | flops 805306368 | bytes 7733248 | tf_op jit(solution)/shard_map/dot_general | solution.py:142
  25.8 1.7 %stack.32 = f32[1,128,4,512]{3,2,1,0:T(4,128)} reshape(f32[128,2048]{1,0:T(8,128)S(1)} %fusion.12) | data formatting | bytes 2097152 | tf_op jit(solution)/shard_map/stack | solution.py:140
  27.4 1.6 %copy_dynamic-update-slice_fusion.3 = f32[2,128,4,512]{3,1,0,2:T(8,128)S(1)} fusion(f32[1,128,4,512]{3,2,1,0:T(4,128)} %stack.32), kind=kLoop, calls=%fused_computation.11 | loop fusion | bytes 2097152
  29.4 2.3 %collective-permute-start.13 = (bf16[32,1664]{1,0:T(8,128)(2,1)}, bf16[32,1664]{1,0:T(8,128)(2,1)S(1)}, u32[]{:S(2)}, u32[]{:S(2)}) collective-permute-start(bf16[32,1664]{1,0:T(8,128)(2,1)} %collective-permute-done.10), channel_id=1, source_target_pairs={{0,4},{1,5},{2,6},{3,7},{4,0},{5,1},{6,2},{7,3},{8,12},{9,13},{10,... | collective-permute-start | bytes 319496 | tf_op jit(solution)/shard_map/ppermute | solution.py:80
  34.1 1.6 %collective-permute-done.13 = bf16[32,1664]{1,0:T(8,128)(2,1)S(1)} collective-permute-done((bf16[32,1664]{1,0:T(8,128)(2,1)}, bf16[32,1664]{1,0:T(8,128)(2,1)S(1)}, u32[]{:S(2)}, u32[]{:S(2)}) %collective-permute-start.13) | collective-permute-done | bytes 106528 | tf_op jit(solution)/shard_map/ppermute | solution.py:80
  38.9 5.0 %fusion.6 = f32[128,2048]{1,0:T(8,128)} fusion(bf16[1536,2048]{1,0:T(8,128)(2,1)} %param.9, bf16[128,1664]{1,0:T(8,128)(2,1)S(1)} %pad_maximum_fusion.4), kind=kOutput, calls=%fused_computation.36 | convolution fusion | flops 805306368 | bytes 7733248 | tf_op jit(solution)/shard_map/dot_general | solution.py:143
  43.9 2.0 %fusion.8 = f32[128,2048]{1,0:T(8,128)} fusion(bf16[1536,2048]{1,0:T(8,128)(2,1)S(1)} %bitcast.61, bf16[128,1664]{1,0:T(8,128)(2,1)S(1)} %pad_maximum_fusion.4), kind=kOutput, calls=%fused_computation.38 | convolution fusion | flops 805306368 | bytes 7733248 | tf_op jit(solution)/shard_map/dot_general | solution.py:142
  45.9 1.9 %stack.38 = f32[1,128,4,512]{3,2,1,0:T(4,128)S(1)} reshape(f32[128,2048]{1,0:T(8,128)} %fusion.6) | data formatting | bytes 2097152 | tf_op jit(solution)/shard_map/stack | solution.py:140
  47.8 2.9 %stack.37 = f32[1,128,4,512]{3,2,1,0:T(4,128)} reshape(f32[128,2048]{1,0:T(8,128)} %fusion.8) | data formatting | bytes 2097152 | tf_op jit(solution)/shard_map/stack | solution.py:140
  50.7 1.6 %copy_dynamic-update-slice_fusion.1 = f32[2,128,4,512]{3,1,0,2:T(8,128)S(1)} fusion(f32[1,128,4,512]{3,2,1,0:T(4,128)} %stack.37), kind=kLoop, calls=%fused_computation.9 | loop fusion | bytes 2097152
  54.2 1.6 %collective-permute-start.4 = (bf16[2,128,512]{2,1,0:T(8,128)(2,1)S(1)}, bf16[2,128,512]{2,1,0:T(8,128)(2,1)S(1)}, u32[]{:S(2)}, u32[]{:S(2)}) collective-permute-start(bf16[2,128,512]{2,1,0:T(8,128)(2,1)S(1)} %fusion.14), channel_id=1, source_target_pairs={{0,2},{1,3},{2,0},{3,1},{4,6},{5,7},{6,4},{7,5},{8,10},{9,11},{10,... | collective-permute-start | bytes 786440 | tf_op jit(solution)/shard_map/ppermute | solution.py:80
  56.7 6.6 %collective-permute-done.4 = bf16[2,128,512]{2,1,0:T(8,128)(2,1)S(1)} collective-permute-done((bf16[2,128,512]{2,1,0:T(8,128)(2,1)S(1)}, bf16[2,128,512]{2,1,0:T(8,128)(2,1)S(1)}, u32[]{:S(2)}, u32[]{:S(2)}) %collective-permute-start.4) | collective-permute-done | bytes 262176 | tf_op jit(solution)/shard_map/ppermute | solution.py:80
  63.6 1.6 %collective-permute-start.5 = (bf16[128,512]{1,0:T(8,128)(2,1)S(1)}, bf16[128,512]{1,0:T(8,128)(2,1)S(1)}, u32[]{:S(2)}, u32[]{:S(2)}) collective-permute-start(bf16[128,512]{1,0:T(8,128)(2,1)S(1)} %fusion.26), channel_id=1, source_target_pairs={{0,2},{1,3},{2,0},{3,1},{4,6},{5,7},{6,4},{7,5},{8,10},{9,11},{10,... | collective-permute-start | bytes 393224 | tf_op jit(solution)/shard_map/ppermute | solution.py:80
  65.2 3.7 %collective-permute-done.15 = bf16[2,128,512]{2,1,0:T(8,128)(2,1)S(1)} collective-permute-done((bf16[2,128,512]{2,1,0:T(8,128)(2,1)S(1)}, bf16[2,128,512]{2,1,0:T(8,128)(2,1)S(1)}, u32[]{:S(2)}, u32[]{:S(2)}) %collective-permute-start.15) | collective-permute-done | bytes 262176 | tf_op jit(solution)/shard_map/ppermute | solution.py:80
  69.2 1.6 %collective-permute-start.16 = (bf16[128,512]{1,0:T(8,128)(2,1)S(1)}, bf16[128,512]{1,0:T(8,128)(2,1)S(1)}, u32[]{:S(2)}, u32[]{:S(2)}) collective-permute-start(bf16[128,512]{1,0:T(8,128)(2,1)S(1)} %fusion.22), channel_id=1, source_target_pairs={{0,2},{1,3},{2,0},{3,1},{4,6},{5,7},{6,4},{7,5},{8,10},{9,11},{10,... | collective-permute-start | bytes 393224 | tf_op jit(solution)/shard_map/ppermute | solution.py:80
  71.7 2.5 %collective-permute-done.16 = bf16[128,512]{1,0:T(8,128)(2,1)S(1)} collective-permute-done((bf16[128,512]{1,0:T(8,128)(2,1)S(1)}, bf16[128,512]{1,0:T(8,128)(2,1)S(1)}, u32[]{:S(2)}, u32[]{:S(2)}) %collective-permute-start.16) | collective-permute-done | bytes 131104 | tf_op jit(solution)/shard_map/ppermute | solution.py:80
  74.5 5.3 %collective-permute-start.7 = (bf16[128,1024]{1,0:T(8,128)(2,1)S(1)}, bf16[128,1024]{1,0:T(8,128)(2,1)S(1)}, u32[]{:S(2)}, u32[]{:S(2)}) collective-permute-start(bf16[128,1024]{1,0:T(8,128)(2,1)S(1)} %get-tuple-element.14), channel_id=1, source_target_pairs={{0,16},{2,18},{4,20},{6,22},{9,25},{11,27},{13,29},{15,31},{16,0},... | collective-permute-start | bytes 786440 | tf_op jit(solution)/shard_map/ppermute | solution.py:80
  80.0 1.9 %collective-permute-start.18 = (bf16[128,1024]{1,0:T(8,128)(2,1)S(1)}, bf16[128,1024]{1,0:T(8,128)(2,1)}, u32[]{:S(2)}, u32[]{:S(2)}) collective-permute-start(bf16[128,1024]{1,0:T(8,128)(2,1)S(1)} %get-tuple-element.11), channel_id=1, source_target_pairs={{0,16},{2,18},{4,20},{6,22},{9,25},{11,27},{13,29},{15,31},{16,0},... | collective-permute-start | bytes 786440 | tf_op jit(solution)/shard_map/ppermute | solution.py:80
  81.9 7.9 %collective-permute-done.7 = bf16[128,1024]{1,0:T(8,128)(2,1)S(1)} collective-permute-done((bf16[128,1024]{1,0:T(8,128)(2,1)S(1)}, bf16[128,1024]{1,0:T(8,128)(2,1)S(1)}, u32[]{:S(2)}, u32[]{:S(2)}) %collective-permute-start.7) | collective-permute-done | bytes 262176 | tf_op jit(solution)/shard_map/ppermute | solution.py:80
  89.8 3.6 %collective-permute-start.8 = (bf16[128,1024]{1,0:T(8,128)(2,1)S(1)}, bf16[128,1024]{1,0:T(8,128)(2,1)S(1)}, u32[]{:S(2)}, u32[]{:S(2)}) collective-permute-start(bf16[128,1024]{1,0:T(8,128)(2,1)S(1)} %collective-permute-done.7), channel_id=1, source_target_pairs={{0,2},{4,6},{9,11},{13,15},{18,16},{22,20},{27,25},{31,29}} | collective-permute-start | bytes 786440 | tf_op jit(solution)/shard_map/ppermute | solution.py:80
  93.4 2.7 %collective-permute-start.19 = (bf16[128,1024]{1,0:T(8,128)(2,1)}, bf16[128,1024]{1,0:T(8,128)(2,1)S(1)}, u32[]{:S(2)}, u32[]{:S(2)}) collective-permute-start(bf16[128,1024]{1,0:T(8,128)(2,1)} %collective-permute-done.18), channel_id=1, source_target_pairs={{0,2},{4,6},{9,11},{13,15},{18,16},{22,20},{27,25},{31,29}} | collective-permute-start | bytes 786440 | tf_op jit(solution)/shard_map/ppermute | solution.py:80
  98.0 2.1 %collective-permute-start.9 = (bf16[128,2048]{1,0:T(8,128)(2,1)}, bf16[128,2048]{1,0:T(8,128)(2,1)}, u32[]{:S(2)}, u32[]{:S(2)}) collective-permute-start(bf16[128,2048]{1,0:T(8,128)(2,1)} %pad_maximum_fusion.1), channel_id=1, source_target_pairs={{0,8},{2,10},{4,12},{6,14},{9,1},{11,3},{13,5},{15,7},{16,24},{18,... | collective-permute-start | bytes 1572872 | tf_op jit(solution)/shard_map/ppermute | solution.py:80
  107.4 4.5 %collective-permute-done.20 = bf16[128,2048]{1,0:T(8,128)(2,1)S(1)} collective-permute-done((bf16[128,2048]{1,0:T(8,128)(2,1)}, bf16[128,2048]{1,0:T(8,128)(2,1)S(1)}, u32[]{:S(2)}, u32[]{:S(2)}) %collective-permute-start.20) | collective-permute-done | bytes 524320 | tf_op jit(solution)/shard_map/ppermute | solution.py:80
  113.3 8.1 %collective-permute-done.21 = bf16[128,2048]{1,0:T(8,128)(2,1)S(1)} collective-permute-done((bf16[128,2048]{1,0:T(8,128)(2,1)S(1)}, bf16[128,2048]{1,0:T(8,128)(2,1)S(1)}, u32[]{:S(2)}, u32[]{:S(2)}) %collective-permute-start.21) | collective-permute-done | bytes 524320 | tf_op jit(solution)/shard_map/ppermute | solution.py:80
  121.4 9.1 %collective-permute-done.22 = bf16[128,2048]{1,0:T(8,128)(2,1)S(1)} collective-permute-done((bf16[128,2048]{1,0:T(8,128)(2,1)S(1)}, bf16[128,2048]{1,0:T(8,128)(2,1)S(1)}, u32[]{:S(2)}, u32[]{:S(2)}) %collective-permute-start.22) | collective-permute-done | bytes 524320 | tf_op jit(solution)/shard_map/ppermute | solution.py:80
  131.0 14.2 %broadcast_divide_fusion = f32[4096,2048]{1,0:T(8,128)} fusion(f32[]{:T(128)S(6)} %add.57, bf16[256,2048]{1,0:T(8,128)(2,1)S(1)} %get-tuple-element.16, bf16[256,2048]{1,0:T(8,128)(2,1)S(1)} %get-tuple-element.15, bf16[128,2048]{1,0:T(8,128)(2,1)S(1)} %get-tuple-element.18, bf16[128,2048]{1,0:T(8,128)(2,1)S(1)} %get-tuple-element.17), kind=kOutput, calls=%fused_computation | convolution fusion | flops 4309647360 | bytes 36700164 | tf_op jit(solution)/shard_map/dot_general | solution.py:193
  (86 shorter events, 25.1 us)
Async XLA Ops:
  5.0 7.5 %collective-permute-start.2 = (bf16[32,1664]{1,0:T(8,128)(2,1)}, bf16[32,1664]{1,0:T(8,128)(2,1)S(1)}, u32[]{:S(2)}, u32[]{:S(2)}) collective-permute-start(bf16[32,1664]{1,0:T(8,128)(2,1)} %shard_map.55), channel_id=1, source_target_pairs={{0,4},{1,5},{2,6},{3,7},{4,0},{5,1},{6,2},{7,3},{8,12},{9,13},{10,... | collective-permute-start | bytes 319496 | tf_op jit(solution)/shard_map/ppermute | solution.py:80
  7.9 8.2 %collective-permute-start.1 = (bf16[32,1664]{1,0:T(8,128)(2,1)}, bf16[32,1664]{1,0:T(8,128)(2,1)S(1)}, u32[]{:S(2)}, u32[]{:S(2)}) collective-permute-start(bf16[32,1664]{1,0:T(8,128)(2,1)} %shard_map.55), channel_id=1, source_target_pairs={{0,8},{1,9},{2,10},{3,11},{4,12},{5,13},{6,14},{7,15},{8,0},{9,1},... | collective-permute-start | bytes 319496 | tf_op jit(solution)/shard_map/ppermute | solution.py:80
  9.5 7.0 %collective-permute-start = (bf16[32,1664]{1,0:T(8,128)(2,1)}, bf16[32,1664]{1,0:T(8,128)(2,1)S(1)}, u32[]{:S(2)}, u32[]{:S(2)}) collective-permute-start(bf16[32,1664]{1,0:T(8,128)(2,1)} %shard_map.55), channel_id=1, source_target_pairs={{0,12},{1,13},{2,14},{3,15},{4,8},{5,9},{6,10},{7,11},{8,4},{9,5},... | collective-permute-start | bytes 319496 | tf_op jit(solution)/shard_map/ppermute | solution.py:80
  9.5 19.8 %collective-permute-start.10 = (bf16[32,1664]{1,0:T(8,128)(2,1)}, bf16[32,1664]{1,0:T(8,128)(2,1)}, u32[]{:S(2)}, u32[]{:S(2)}) collective-permute-start(bf16[32,1664]{1,0:T(8,128)(2,1)} %shard_map.55), channel_id=1, source_target_pairs={{0,16},{1,17},{2,18},{3,19},{4,20},{5,21},{6,22},{7,23},{8,24},{9,... | collective-permute-start | bytes 319496 | tf_op jit(solution)/shard_map/ppermute | solution.py:80
  29.0 14.9 %slice-start = ((s8[6291456]{0:T(1024)(128)(4,1)}), s8[4194304]{0:T(1024)(128)(4,1)S(1)}, s32[]{:S(2)}) async-start(s8[6291456]{0:T(1024)(128)(4,1)} %bitcast.60), calls=%async_computation | async-start | bytes 8388608
  29.4 6.4 %collective-permute-start.13 = (bf16[32,1664]{1,0:T(8,128)(2,1)}, bf16[32,1664]{1,0:T(8,128)(2,1)S(1)}, u32[]{:S(2)}, u32[]{:S(2)}) collective-permute-start(bf16[32,1664]{1,0:T(8,128)(2,1)} %collective-permute-done.10), channel_id=1, source_target_pairs={{0,4},{1,5},{2,6},{3,7},{4,0},{5,1},{6,2},{7,3},{8,12},{9,13},{10,... | collective-permute-start | bytes 319496 | tf_op jit(solution)/shard_map/ppermute | solution.py:80
  31.7 4.9 %collective-permute-start.12 = (bf16[32,1664]{1,0:T(8,128)(2,1)}, bf16[32,1664]{1,0:T(8,128)(2,1)S(1)}, u32[]{:S(2)}, u32[]{:S(2)}) collective-permute-start(bf16[32,1664]{1,0:T(8,128)(2,1)} %collective-permute-done.10), channel_id=1, source_target_pairs={{0,8},{1,9},{2,10},{3,11},{4,12},{5,13},{6,14},{7,15},{8,0},{9,1},... | collective-permute-start | bytes 319496 | tf_op jit(solution)/shard_map/ppermute | solution.py:80
  32.0 5.8 %collective-permute-start.11 = (bf16[32,1664]{1,0:T(8,128)(2,1)}, bf16[32,1664]{1,0:T(8,128)(2,1)S(1)}, u32[]{:S(2)}, u32[]{:S(2)}) collective-permute-start(bf16[32,1664]{1,0:T(8,128)(2,1)} %collective-permute-done.10), channel_id=1, source_target_pairs={{0,12},{1,13},{2,14},{3,15},{4,8},{5,9},{6,10},{7,11},{8,4},{9,5},... | collective-permute-start | bytes 319496 | tf_op jit(solution)/shard_map/ppermute | solution.py:80
  34.1 18.7 %collective-permute-start.3 = (bf16[2,128,2,512]{3,1,0,2:T(8,128)(2,1)}, bf16[2,128,2,512]{3,1,0,2:T(8,128)(2,1)}, u32[]{:S(2)}, u32[]{:S(2)}) collective-permute-start(bf16[2,128,2,512]{3,1,0,2:T(8,128)(2,1)} %select_convert_fusion.1), channel_id=1, source_target_pairs={{0,1},{1,0},{2,3},{3,2},{4,5},{5,4},{6,7},{7,6},{8,9},{9,8},{10,11... | collective-permute-start | bytes 1572872 | tf_op jit(solution)/shard_map/ppermute | solution.py:80
  38.8 5.1 %copy-start.2 = (bf16[32,1664]{1,0:T(8,128)(2,1)}, bf16[32,1664]{1,0:T(8,128)(2,1)S(1)}, u32[]{:S(2)}) copy-start(bf16[32,1664]{1,0:T(8,128)(2,1)S(1)} %get-tuple-element.29) | copy-start | bytes 319492
  38.8 5.1 %copy-start.4 = (bf16[32,1664]{1,0:T(8,128)(2,1)}, bf16[32,1664]{1,0:T(8,128)(2,1)S(1)}, u32[]{:S(2)}) copy-start(bf16[32,1664]{1,0:T(8,128)(2,1)S(1)} %get-tuple-element.30) | copy-start | bytes 319492
  38.8 5.1 %copy-start.6 = (bf16[32,1664]{1,0:T(8,128)(2,1)}, bf16[32,1664]{1,0:T(8,128)(2,1)S(1)}, u32[]{:S(2)}) copy-start(bf16[32,1664]{1,0:T(8,128)(2,1)S(1)} %get-tuple-element.31) | copy-start | bytes 319492
  38.8 5.1 %copy-start.8 = (bf16[32,1664]{1,0:T(8,128)(2,1)}, bf16[32,1664]{1,0:T(8,128)(2,1)S(1)}, u32[]{:S(2)}) copy-start(bf16[32,1664]{1,0:T(8,128)(2,1)S(1)} %get-tuple-element.32) | copy-start | bytes 319492
  52.7 3.0 %collective-permute-start.14 = (bf16[2,128,2,512]{3,1,0,2:T(8,128)(2,1)S(1)}, bf16[2,128,2,512]{3,1,0,2:T(8,128)(2,1)S(1)}, u32[]{:S(2)}, u32[]{:S(2)}) collective-permute-start(bf16[2,128,2,512]{3,1,0,2:T(8,128)(2,1)S(1)} %select_convert_fusion), channel_id=1, source_target_pairs={{0,1},{1,0},{2,3},{3,2},{4,5},{5,4},{6,7},{7,6},{8,9},{9,8},{10,11... | collective-permute-start | bytes 1572872 | tf_op jit(solution)/shard_map/ppermute | solution.py:80
  54.2 9.2 %collective-permute-start.4 = (bf16[2,128,512]{2,1,0:T(8,128)(2,1)S(1)}, bf16[2,128,512]{2,1,0:T(8,128)(2,1)S(1)}, u32[]{:S(2)}, u32[]{:S(2)}) collective-permute-start(bf16[2,128,512]{2,1,0:T(8,128)(2,1)S(1)} %fusion.14), channel_id=1, source_target_pairs={{0,2},{1,3},{2,0},{3,1},{4,6},{5,7},{6,4},{7,5},{8,10},{9,11},{10,... | collective-permute-start | bytes 786440 | tf_op jit(solution)/shard_map/ppermute | solution.py:80
  56.1 12.8 %collective-permute-start.15 = (bf16[2,128,512]{2,1,0:T(8,128)(2,1)S(1)}, bf16[2,128,512]{2,1,0:T(8,128)(2,1)S(1)}, u32[]{:S(2)}, u32[]{:S(2)}) collective-permute-start(bf16[2,128,512]{2,1,0:T(8,128)(2,1)S(1)} %fusion.15), channel_id=1, source_target_pairs={{0,2},{1,3},{2,0},{3,1},{4,6},{5,7},{6,4},{7,5},{8,10},{9,11},{10,... | collective-permute-start | bytes 786440 | tf_op jit(solution)/shard_map/ppermute | solution.py:80
  63.6 7.9 %collective-permute-start.5 = (bf16[128,512]{1,0:T(8,128)(2,1)S(1)}, bf16[128,512]{1,0:T(8,128)(2,1)S(1)}, u32[]{:S(2)}, u32[]{:S(2)}) collective-permute-start(bf16[128,512]{1,0:T(8,128)(2,1)S(1)} %fusion.26), channel_id=1, source_target_pairs={{0,2},{1,3},{2,0},{3,1},{4,6},{5,7},{6,4},{7,5},{8,10},{9,11},{10,... | collective-permute-start | bytes 393224 | tf_op jit(solution)/shard_map/ppermute | solution.py:80
  69.2 5.0 %collective-permute-start.16 = (bf16[128,512]{1,0:T(8,128)(2,1)S(1)}, bf16[128,512]{1,0:T(8,128)(2,1)S(1)}, u32[]{:S(2)}, u32[]{:S(2)}) collective-permute-start(bf16[128,512]{1,0:T(8,128)(2,1)S(1)} %fusion.22), channel_id=1, source_target_pairs={{0,2},{1,3},{2,0},{3,1},{4,6},{5,7},{6,4},{7,5},{8,10},{9,11},{10,... | collective-permute-start | bytes 393224 | tf_op jit(solution)/shard_map/ppermute | solution.py:80
  71.5 2.8 %collective-permute-start.6 = (bf16[2,128,512]{2,1,0:T(8,128)(2,1)S(1)}, bf16[2,128,512]{2,1,0:T(8,128)(2,1)S(1)}, u32[]{:S(2)}, u32[]{:S(2)}) collective-permute-start(bf16[2,128,512]{2,1,0:T(8,128)(2,1)S(1)} %pad_maximum_fusion.7), channel_id=1, source_target_pairs={{0,1},{1,0},{2,3},{3,2},{4,5},{5,4},{6,7},{7,6},{8,9},{9,8},{10,11... | collective-permute-start | bytes 786440 | tf_op jit(solution)/shard_map/ppermute | solution.py:80
  74.3 5.6 %collective-permute-start.17 = (bf16[2,128,512]{2,1,0:T(8,128)(2,1)S(1)}, bf16[2,128,512]{2,1,0:T(8,128)(2,1)S(1)}, u32[]{:S(2)}, u32[]{:S(2)}) collective-permute-start(bf16[2,128,512]{2,1,0:T(8,128)(2,1)S(1)} %pad_maximum_fusion.8), channel_id=1, source_target_pairs={{0,1},{1,0},{2,3},{3,2},{4,5},{5,4},{6,7},{7,6},{8,9},{9,8},{10,11... | collective-permute-start | bytes 786440 | tf_op jit(solution)/shard_map/ppermute | solution.py:80
  74.5 15.3 %collective-permute-start.7 = (bf16[128,1024]{1,0:T(8,128)(2,1)S(1)}, bf16[128,1024]{1,0:T(8,128)(2,1)S(1)}, u32[]{:S(2)}, u32[]{:S(2)}) collective-permute-start(bf16[128,1024]{1,0:T(8,128)(2,1)S(1)} %get-tuple-element.14), channel_id=1, source_target_pairs={{0,16},{2,18},{4,20},{6,22},{9,25},{11,27},{13,29},{15,31},{16,0},... | collective-permute-start | bytes 786440 | tf_op jit(solution)/shard_map/ppermute | solution.py:80
  80.0 13.4 %collective-permute-start.18 = (bf16[128,1024]{1,0:T(8,128)(2,1)S(1)}, bf16[128,1024]{1,0:T(8,128)(2,1)}, u32[]{:S(2)}, u32[]{:S(2)}) collective-permute-start(bf16[128,1024]{1,0:T(8,128)(2,1)S(1)} %get-tuple-element.11), channel_id=1, source_target_pairs={{0,16},{2,18},{4,20},{6,22},{9,25},{11,27},{13,29},{15,31},{16,0},... | collective-permute-start | bytes 786440 | tf_op jit(solution)/shard_map/ppermute | solution.py:80
  89.8 7.3 %collective-permute-start.8 = (bf16[128,1024]{1,0:T(8,128)(2,1)S(1)}, bf16[128,1024]{1,0:T(8,128)(2,1)S(1)}, u32[]{:S(2)}, u32[]{:S(2)}) collective-permute-start(bf16[128,1024]{1,0:T(8,128)(2,1)S(1)} %collective-permute-done.7), channel_id=1, source_target_pairs={{0,2},{4,6},{9,11},{13,15},{18,16},{22,20},{27,25},{31,29}} | collective-permute-start | bytes 786440 | tf_op jit(solution)/shard_map/ppermute | solution.py:80
  93.4 6.9 %collective-permute-start.19 = (bf16[128,1024]{1,0:T(8,128)(2,1)}, bf16[128,1024]{1,0:T(8,128)(2,1)S(1)}, u32[]{:S(2)}, u32[]{:S(2)}) collective-permute-start(bf16[128,1024]{1,0:T(8,128)(2,1)} %collective-permute-done.18), channel_id=1, source_target_pairs={{0,2},{4,6},{9,11},{13,15},{18,16},{22,20},{27,25},{31,29}} | collective-permute-start | bytes 786440 | tf_op jit(solution)/shard_map/ppermute | solution.py:80
  97.1 5.4 %copy-start.1 = (bf16[32,1664]{1,0:T(8,128)(2,1)S(1)}, bf16[32,1664]{1,0:T(8,128)(2,1)}, u32[]{:S(2)}) copy-start(bf16[32,1664]{1,0:T(8,128)(2,1)} %copy-done) | copy-start | bytes 319492
  97.2 5.4 %copy-start.3 = (bf16[32,1664]{1,0:T(8,128)(2,1)S(1)}, bf16[32,1664]{1,0:T(8,128)(2,1)}, u32[]{:S(2)}) copy-start(bf16[32,1664]{1,0:T(8,128)(2,1)} %copy-done.2) | copy-start | bytes 319492
  97.2 5.4 %copy-start.5 = (bf16[32,1664]{1,0:T(8,128)(2,1)S(1)}, bf16[32,1664]{1,0:T(8,128)(2,1)}, u32[]{:S(2)}) copy-start(bf16[32,1664]{1,0:T(8,128)(2,1)} %copy-done.4) | copy-start | bytes 319492
  97.2 5.4 %copy-start.7 = (bf16[32,1664]{1,0:T(8,128)(2,1)S(1)}, bf16[32,1664]{1,0:T(8,128)(2,1)}, u32[]{:S(2)}) copy-start(bf16[32,1664]{1,0:T(8,128)(2,1)} %copy-done.6) | copy-start | bytes 319492
  98.0 8.3 %collective-permute-start.9 = (bf16[128,2048]{1,0:T(8,128)(2,1)}, bf16[128,2048]{1,0:T(8,128)(2,1)}, u32[]{:S(2)}, u32[]{:S(2)}) collective-permute-start(bf16[128,2048]{1,0:T(8,128)(2,1)} %pad_maximum_fusion.1), channel_id=1, source_target_pairs={{0,8},{2,10},{4,12},{6,14},{9,1},{11,3},{13,5},{15,7},{16,24},{18,... | collective-permute-start | bytes 1572872 | tf_op jit(solution)/shard_map/ppermute | solution.py:80
  101.2 10.7 %collective-permute-start.20 = (bf16[128,2048]{1,0:T(8,128)(2,1)}, bf16[128,2048]{1,0:T(8,128)(2,1)S(1)}, u32[]{:S(2)}, u32[]{:S(2)}) collective-permute-start(bf16[128,2048]{1,0:T(8,128)(2,1)} %pad_maximum_fusion.2), channel_id=1, source_target_pairs={{0,8},{2,10},{4,12},{6,14},{9,1},{11,3},{13,5},{15,7},{16,24},{18,... | collective-permute-start | bytes 1572872 | tf_op jit(solution)/shard_map/ppermute | solution.py:80
  106.4 14.9 %collective-permute-start.21 = (bf16[128,2048]{1,0:T(8,128)(2,1)S(1)}, bf16[128,2048]{1,0:T(8,128)(2,1)S(1)}, u32[]{:S(2)}, u32[]{:S(2)}) collective-permute-start(bf16[128,2048]{1,0:T(8,128)(2,1)S(1)} %broadcast_select_fusion.5), channel_id=1, source_target_pairs={{0,4},{1,5},{2,6},{3,7},{4,0},{5,1},{6,2},{7,3},{8,12},{9,13},{10,... | collective-permute-start | bytes 1572872 | tf_op jit(solution)/shard_map/ppermute | solution.py:80
  112.1 18.4 %collective-permute-start.22 = (bf16[128,2048]{1,0:T(8,128)(2,1)S(1)}, bf16[128,2048]{1,0:T(8,128)(2,1)S(1)}, u32[]{:S(2)}, u32[]{:S(2)}) collective-permute-start(bf16[128,2048]{1,0:T(8,128)(2,1)S(1)} %broadcast_select_fusion.4), channel_id=1, source_target_pairs={{0,4},{1,5},{2,6},{3,7},{4,0},{5,1},{6,2},{7,3},{8,12},{9,13},{10,... | collective-permute-start | bytes 1572872 | tf_op jit(solution)/shard_map/ppermute | solution.py:80
  (2 other events, 8.9 us)

commit v2 on v1

v2 whole, which is shorter than its diff:
```python
import jax
import jax.numpy as jnp
from jax import lax
from jax.experimental import pallas as pl
from jax.experimental.pallas import tpu as pltpu
from jax.sharding import PartitionSpec as P

CAP = 32
LANES = 128
BF, F32 = jnp.bfloat16, jnp.float32
AXES = ("dp", "tensor")
ROWS_OF = (((0,), (0,)), ((), ()))


def pack_rows(token_blocks, weight_blocks):
    member = (weight_blocks > 0).astype(jnp.int32)
    position = jnp.cumsum(member, axis=1) - 1
    slot_index = lax.broadcasted_iota(jnp.int32, (1, CAP, 1), 1)
    picked = (position[:, None, :] == slot_index) & (member[:, None, :] > 0)
    selector = picked.astype(BF)
    packed = jnp.einsum(
        "sct,std->scd", selector, token_blocks, preferred_element_type=F32
    ).astype(BF)
    packed_weight = jnp.einsum(
        "sct,st->sc", selector, weight_blocks, preferred_element_type=F32
    ).astype(BF)
    return (packed.reshape(-1, token_blocks.shape[2]), packed_weight.reshape(-1))


def any_mesh(hidden_states, expert_ids, route_gates, gate_weight, up_weight):
    route_weight = jnp.sum(
        jnp.where(expert_ids == 0, route_gates, jnp.zeros_like(route_gates)), axis=1
    ).astype(BF)
    own_rows, own_weight = pack_rows(hidden_states[None], route_weight[None])
    packed_rows, packed_weight = (
        lax.all_gather(own_rows, "dp", axis=0, tiled=True),
        lax.all_gather(own_weight, "dp", axis=0, tiled=True),
    )
    weight_total = jnp.sum(packed_weight.astype(F32))
    gate_part = jnp.dot(packed_rows, gate_weight, preferred_element_type=F32)
    up_part = jnp.dot(packed_rows, up_weight, preferred_element_type=F32)
    summed = lax.psum_scatter(
        jnp.concatenate([gate_part, up_part], axis=1), "tensor", scatter_dimension=0, tiled=True
    )
    unit_width = gate_weight.shape[1]
    local_keys = (jax.nn.silu(summed[:, :unit_width]) * summed[:, unit_width:]).astype(BF)
    column_keys = lax.all_gather(local_keys, "tensor", axis=0, tiled=True)
    weighted = (packed_weight.astype(F32)[:, None] * column_keys.astype(F32)).astype(BF)
    spread_keys = lax.all_gather(local_keys, "dp", axis=1, tiled=True)
    row_keys = lax.all_to_all(spread_keys, "tensor", split_axis=1, concat_axis=0, tiled=True)
    covariance = lax.dot_general(row_keys, weighted, ROWS_OF, preferred_element_type=F32)
    return covariance / weight_total


def pairs(to):
    number = lambda z, x, y, c: z * 8 + x * 4 + y * 2 + c
    out = []
    for z in range(4):
        for x in range(2):
            for y in range(2):
                for c in range(2):
                    there = to(z, x, y, c)
                    if there is not None:
                        out.append((number(z, x, y, c), number(*there)))
    return out


def inside(z, y):
    return z // 2 == y


CORE = pairs(lambda z, x, y, c: (z, x, y, 1 - c))
Y = pairs(lambda z, x, y, c: (z, x, 1 - y, c))
X = pairs(lambda z, x, y, c: (z, 1 - x, y, c))
Z1 = pairs(lambda z, x, y, c: (z ^ 1, x, y, c))
Z2 = pairs(lambda z, x, y, c: (z ^ 2, x, y, c))
XZ1 = pairs(lambda z, x, y, c: (z ^ 1, 1 - x, y, c))
FAR = pairs(lambda z, x, y, c: (z ^ 2, x, y, c) if inside(z, y) else None)
FAR_Y = pairs(lambda z, x, y, c: (z ^ 2, x, 1 - y, c) if not inside(z, y) else None)
HOME_X = pairs(lambda z, x, y, c: (z, 1 - x, y, c) if c == z % 2 else None)
HOME_Z1 = pairs(lambda z, x, y, c: (z ^ 1, x, y, c) if c == z % 2 else None)
AWAY_X = pairs(lambda z, x, y, c: (z, 1 - x, y, c) if c != z % 2 else None)


def send(value, route):
    return lax.ppermute(value, AXES, route)


def pack_kernel(ids_ref, gates_ref, tokens_ref, out_ref):
    tokens, width = tokens_ref.shape
    weight = jnp.sum(jnp.where(ids_ref[...] == 0, gates_ref[...], 0.0), axis=0, keepdims=True)
    weight = weight.astype(BF).astype(F32)
    member = jnp.where(weight > 0, 1.0, 0.0)
    earlier = lax.broadcasted_iota(jnp.int32, (tokens, tokens), 0) <= lax.broadcasted_iota(
        jnp.int32, (tokens, tokens), 1
    )
    position = jnp.dot(
        jnp.broadcast_to(member, (8, tokens)).astype(BF),
        jnp.where(earlier, 1.0, 0.0).astype(BF),
        preferred_element_type=F32,
    )[:1]
    slot = lax.broadcasted_iota(jnp.int32, (CAP, tokens), 0).astype(F32)
    picked = jnp.where((position - 1.0 == slot) & (member > 0), 1.0, 0.0)
    out_ref[:, :width] = jnp.dot(
        picked.astype(BF), tokens_ref[...], preferred_element_type=F32
    ).astype(BF)
    weights = jnp.sum(picked * weight, axis=1, keepdims=True)
    out_ref[:, width:] = jnp.broadcast_to(weights, (CAP, LANES)).astype(BF)


def pack(hidden_states, expert_ids, route_gates):
    return pl.pallas_call(
        pack_kernel,
        out_shape=jax.ShapeDtypeStruct((CAP, hidden_states.shape[1] + LANES), BF),
    )(expert_ids.T, route_gates.T, hidden_states)


TILE = 256


def project_kernel(at_ref, *refs):
    blocks, (gate_ref, up_ref, out_ref, rows_ref) = refs[:4], refs[4:]
    depth, width = gate_ref.shape
    inner = pl.program_id(1)

    @pl.when((pl.program_id(0) == 0) & (inner == 0))
    def _():
        for k, block in enumerate(blocks):
            start = pl.multiple_of((at_ref[0] ^ k) * CAP, CAP)
            rows_ref[pl.ds(start, CAP), :] = block[:, :depth]

    rows = rows_ref[...]
    half = out_ref.shape[2] // 2
    here = pl.multiple_of(inner * width, LANES)
    there = pl.multiple_of(half + inner * width, LANES)
    out_ref[0, :, pl.ds(here, width)] = jnp.dot(rows, gate_ref[...], preferred_element_type=F32)
    out_ref[0, :, pl.ds(there, width)] = jnp.dot(rows, up_ref[...], preferred_element_type=F32)


def project(at, blocks, gate_weight, up_weight):
    depth, units = gate_weight.shape
    quarter = units // 4
    tiles = quarter // TILE
    rows = 4 * CAP
    weight_spec = pl.BlockSpec((depth, TILE), lambda i, j, at: (0, at[1 + i] * tiles + j))
    return pl.pallas_call(
        project_kernel,
        grid_spec=pltpu.PrefetchScalarGridSpec(
            num_scalar_prefetch=1,
            grid=(2, tiles),
            in_specs=[pl.BlockSpec(b.shape, lambda i, j, at: (0, 0)) for b in blocks]
            + [weight_spec, weight_spec],
            out_specs=pl.BlockSpec((1, rows, 2 * quarter), lambda i, j, at: (i, 0, 0)),
            scratch_shapes=[pltpu.VMEM((rows, depth), BF)],
        ),
        out_shape=jax.ShapeDtypeStruct((2, rows, 2 * quarter), F32),
        cost_estimate=pl.CostEstimate(
            flops=2 * rows * depth * units, bytes_accessed=2 * depth * units, transcendentals=0
        ),
    )(at, *blocks, gate_weight, up_weight)


def covariance_kernel(at_ref, scale_ref, first_ref, second_ref, columns_ref, *refs):
    out_ref = refs[-1]
    panel = jnp.concatenate([first_ref[...], second_ref[...]], axis=0)
    out_ref[...] = (
        lax.dot_general(panel, columns_ref[...], ROWS_OF, preferred_element_type=F32)
        * scale_ref[0]
    )


PANEL_TILE = 256


def covariance_part(at, scale, panel, columns, out_rows, into):
    rows, units = panel[0].shape
    steps = units // PANEL_TILE
    panel_spec = pl.BlockSpec((rows, PANEL_TILE), lambda i, at: (0, i))
    in_specs = [
        pl.BlockSpec(memory_space=pltpu.SMEM),
        panel_spec,
        panel_spec,
        pl.BlockSpec(columns.shape, lambda i, at: (0, 0)),
    ]
    args = [at, scale, panel[0], panel[1], columns]
    aliases = {}
    if into is not None:
        in_specs.append(pl.BlockSpec(memory_space=pl.ANY))
        args.append(into)
        aliases = {5: 0}
    width = columns.shape[1]
    return pl.pallas_call(
        covariance_kernel,
        grid_spec=pltpu.PrefetchScalarGridSpec(
            num_scalar_prefetch=1,
            grid=(steps,),
            in_specs=in_specs,
            out_specs=pl.BlockSpec((PANEL_TILE, width), lambda i, at: (at[0] * steps + i, 0)),
        ),
        out_shape=jax.ShapeDtypeStruct((out_rows, width), F32),
        input_output_aliases=aliases,
        cost_estimate=pl.CostEstimate(
            flops=4 * rows * units * width, bytes_accessed=4 * units * width, transcendentals=0
        ),
    )(*args)


def fast(hidden_states, expert_ids, route_gates, gate_weight, up_weight):
    depth, units = gate_weight.shape
    quarter = units // 4
    dp, tensor = lax.axis_index("dp"), lax.axis_index("tensor")
    z, x, y, core = dp // 2, dp % 2, tensor // 2, tensor % 2
    is_home, is_inside = core == z % 2, y == z // 2
    place = (z % 2) * 2 + x
    given_at = jnp.stack([place, (1 - y) * 2 + 1 - core, y * 2 + 1 - core]).astype(jnp.int32)
    kept_at = jnp.stack([place, (1 - y) * 2 + core, y * 2 + core]).astype(jnp.int32)

    def beside(mine):
        return [mine, send(mine, X), send(mine, Z1), send(mine, XZ1)]

    def in_place(blocks):
        rows = []
        for at in range(4):
            block = blocks[0]
            for k in (1, 2, 3):
                block = jnp.where(place ^ at == k, blocks[k], block)
            rows.append(block)
        return jnp.concatenate(rows, axis=0)

    def keys_of(blocks):
        given = project(given_at, blocks, gate_weight, up_weight)
        got = send(given, CORE)
        kept = project(kept_at, blocks, gate_weight, up_weight)
        across = send((kept[0] + got[0]).astype(BF), Y)
        total = kept[1] + got[1] + across.astype(F32)
        return (jax.nn.silu(total[:, :quarter]) * total[:, quarter:]).astype(BF)

    def slice_of(own, other):
        low, high = jnp.where(core == 0, own, other), jnp.where(core == 0, other, own)
        pair = jnp.concatenate([low, high], axis=2)
        return jnp.concatenate(
            [jnp.where(y == 0, pair[0], pair[1]), jnp.where(y == 0, pair[1], pair[0])], axis=1
        )

    def spread(keys):
        far = jnp.stack([send(keys, FAR), send(keys, FAR_Y)])
        near = jnp.stack([keys, send(keys, Y)])
        own_slice = slice_of(near, send(near, CORE))
        far_slice = slice_of(far, send(far, CORE))
        panel = jnp.where(is_inside, own_slice, far_slice)
        along_z, along_x = send(panel, HOME_Z1), send(panel, HOME_X)
        first = jnp.where(is_home, panel, along_z)
        left = send(along_z[:, : units // 2], AWAY_X)
        right = send(along_x[:, units // 2 :], HOME_Z1)
        second = jnp.where(is_home, along_x, jnp.concatenate([left, right], axis=1))
        return own_slice, first, second

    own = pack(hidden_states, expert_ids, route_gates)
    blocks = [beside(own), beside(send(own, Z2))]
    weights = [
        in_place([b[:, depth:] for b in each])[:, :1].astype(F32) for each in blocks
    ]
    scale = (1.0 / (jnp.sum(weights[0]) + jnp.sum(weights[1]))).reshape(1)
    parts = [spread(keys_of(each)) for each in blocks]
    weighted = [(w * p[0].astype(F32)).astype(BF) for w, p in zip(weights, parts)]
    columns = jnp.concatenate(
        [
            jnp.where(is_inside, weighted[0], weighted[1]),
            jnp.where(is_inside, weighted[1], weighted[0]),
        ]
    )
    out_rows = 2 * units
    half_at = jnp.stack([x]).astype(jnp.int32)
    out = covariance_part(half_at, scale, [p[1] for p in parts], columns, out_rows, None)
    return covariance_part(1 - half_at, scale, [p[2] for p in parts], columns, out_rows, out)


def solution(mesh):
    placed = (P("dp", "tensor"), P("dp", None), P("dp", None), P("tensor", "dp"), P("tensor", "dp"))
    sizes = (mesh.shape["dp"], mesh.shape["tensor"])
    return jax.shard_map(
        fast if sizes == (8, 4) else any_mesh,
        mesh=mesh,
        in_specs=placed,
        out_specs=P("tensor", "dp"),
        check_vma=False,
    )
```

time: 146 us -> 139 us (0.952)
  the two profiles are of different devices: /device:TPU:0 before, /device:TPU:16 now
where the time goes in v2:
time: 139 us; the launch traced here: 138 us
  starting transfers between devices  46.4 us (33%)
  Pallas kernels  45 us (32%)
  waiting for transfers between devices  26.9 us (19%)
  other arithmetic  14.5 us (10%)
  local copies, waits for them, and re-layouts  3.27 us (2%)
  between operations  1.62 us (1%)
    ppermute x29, starting transfers between devices, send(): return lax.ppermute(value, AXES, route)  46.4 us
    ppermute x29, waiting for transfers between devices, send(): return lax.ppermute(value, AXES, route)  26.9 us
    pallas_call x4, Pallas kernels, project(): pl.pallas_call(project_kernel, grid_spec=pltpu.PrefetchScalarGridSpec(num...  24.1 us
    pallas_call x2, Pallas kernels, covariance_part(): pl.pallas_call(covariance_kernel, grid_spec=pltpu.PrefetchScalarGridSpec(...  18.9 us
    select_n x2, other arithmetic, spread(): second = jnp.where(is_home, along_x, jnp.concatenate([left, right], axis=1))  3.84 us
    select_n x4, other arithmetic, in_place(): block = jnp.where(place ^ at == k, blocks[k], block)  3.11 us
  transfers between devices with their start and end apart: 29, of which 10 were waited for; matrix products, arithmetic and copies ran while one was open for 10% of the time, Pallas kernels for 24%

profile of v2, /device:TPU:16, one launch (start us, length us, event | category | flops | bytes accessed | tf_op | source)
XLA Modules:
  0.0 137.7 jit_solution(8853823553267802036)
XLA Ops:
  0.0 2.0 %shard_map.55.refs_0_ = bf16[32,1664]{1,0:T(8,128)(2,1)} custom-call(s32[2,128]{1,0:T(2,128)} %bitcast.59, f32[2,128]{1,0:T(2,128)} %bitcast.60, bf16[128,1536]{1,0:T(8,128)(2,1)} %tokens_ref.1), custom_call_target="tpu_custom_call" | custom-call | tf_op jit(solution)/shard_map/pallas_call | solution.py:112
  2.0 1.8 %collective-permute-start.2 = (bf16[32,1664]{1,0:T(8,128)(2,1)}, bf16[32,1664]{1,0:T(8,128)(2,1)S(1)}, u32[]{:S(2)}, u32[]{:S(2)}) collective-permute-start(bf16[32,1664]{1,0:T(8,128)(2,1)} %shard_map.55.refs_0_), channel_id=1, source_target_pairs={{0,4},{1,5},{2,6},{3,7},{4,0},{5,1},{6,2},{7,3},{8,12},{9,13},{10,... | collective-permute-start | bytes 319496 | tf_op jit(solution)/shard_map/ppermute | solution.py:86
  3.8 1.6 %collective-permute-start.1 = (bf16[32,1664]{1,0:T(8,128)(2,1)}, bf16[32,1664]{1,0:T(8,128)(2,1)S(1)}, u32[]{:S(2)}, u32[]{:S(2)}) collective-permute-start(bf16[32,1664]{1,0:T(8,128)(2,1)} %shard_map.55.refs_0_), channel_id=1, source_target_pairs={{0,8},{1,9},{2,10},{3,11},{4,12},{5,13},{6,14},{7,15},{8,0},{9,1},... | collective-permute-start | bytes 319496 | tf_op jit(solution)/shard_map/ppermute | solution.py:86
  6.9 3.9 %collective-permute-done.1.refs_2_ = bf16[32,1664]{1,0:T(8,128)(2,1)S(1)} collective-permute-done((bf16[32,1664]{1,0:T(8,128)(2,1)}, bf16[32,1664]{1,0:T(8,128)(2,1)S(1)}, u32[]{:S(2)}, u32[]{:S(2)}) %collective-permute-start.1) | collective-permute-done | bytes 106528 | tf_op jit(solution)/shard_map/ppermute | solution.py:86
  10.8 1.6 %collective-permute-done.refs_3_ = bf16[32,1664]{1,0:T(8,128)(2,1)S(1)} collective-permute-done((bf16[32,1664]{1,0:T(8,128)(2,1)}, bf16[32,1664]{1,0:T(8,128)(2,1)S(1)}, u32[]{:S(2)}, u32[]{:S(2)}) %collective-permute-start) | collective-permute-done | bytes 106528 | tf_op jit(solution)/shard_map/ppermute | solution.py:86
  13.0 6.0 %shard_map.57 = f32[2,128,1024]{2,1,0:T(8,128)} custom-call(s32[3]{0:T(128)} %pad_add_fusion.1.at_ref, bf16[32,1664]{1,0:T(8,128)(2,1)} %shard_map.55.refs_0_, bf16[32,1664]{1,0:T(8,128)(2,1)} %copy-done.3, bf16[32,1664]{1,0:T(8,128)(2,1)} %copy-done.4, bf16[32,1664]{1,0:T(8,128)(2,1)} %copy-done.5, bf16[1536,2048]{1,0:T(8,128)(2,1)} %refs_4_.7, ...), custom_call_target="tpu_custom_call" | custom-call | flops 805306368 | bytes 6291456 | tf_op jit(solution)/shard_map/pallas_call | solution.py:146
  19.6 2.9 %collective-permute-start.5 = (bf16[32,1664]{1,0:T(8,128)(2,1)S(1)}, bf16[32,1664]{1,0:T(8,128)(2,1)S(1)}, u32[]{:S(2)}, u32[]{:S(2)}) collective-permute-start(bf16[32,1664]{1,0:T(8,128)(2,1)S(1)} %collective-permute-done.3.refs_0_), channel_id=1, source_target_pairs={{0,8},{1,9},{2,10},{3,11},{4,12},{5,13},{6,14},{7,15},{8,0},{9,1},... | collective-permute-start | bytes 319496 | tf_op jit(solution)/shard_map/ppermute | solution.py:86
  24.4 1.8 %collective-permute-done.5.refs_2_ = bf16[32,1664]{1,0:T(8,128)(2,1)S(1)} collective-permute-done((bf16[32,1664]{1,0:T(8,128)(2,1)S(1)}, bf16[32,1664]{1,0:T(8,128)(2,1)S(1)}, u32[]{:S(2)}, u32[]{:S(2)}) %collective-permute-start.5) | collective-permute-done | bytes 106528 | tf_op jit(solution)/shard_map/ppermute | solution.py:86
  26.2 1.9 %collective-permute-done.4.refs_3_ = bf16[32,1664]{1,0:T(8,128)(2,1)S(1)} collective-permute-done((bf16[32,1664]{1,0:T(8,128)(2,1)S(1)}, bf16[32,1664]{1,0:T(8,128)(2,1)S(1)}, u32[]{:S(2)}, u32[]{:S(2)}) %collective-permute-start.4) | collective-permute-done | bytes 106528 | tf_op jit(solution)/shard_map/ppermute | solution.py:86
  28.8 6.0 %shard_map.59 = f32[2,128,1024]{2,1,0:T(8,128)} custom-call(s32[3]{0:T(128)} %pad_add_fusion.1.at_ref, bf16[32,1664]{1,0:T(8,128)(2,1)} %copy-done.2, bf16[32,1664]{1,0:T(8,128)(2,1)} %copy-done.6, bf16[32,1664]{1,0:T(8,128)(2,1)} %copy-done.7, bf16[32,1664]{1,0:T(8,128)(2,1)} %copy-done.8, bf16[1536,2048]{1,0:T(8,128)(2,1)} %refs_4_.7, ...), custom_call_target="tpu_custom_call" | custom-call | flops 805306368 | bytes 6291456 | tf_op jit(solution)/shard_map/pallas_call | solution.py:146
  34.8 6.0 %shard_map.56 = f32[2,128,1024]{2,1,0:T(8,128)} custom-call(s32[3]{0:T(128)} %pad_add_fusion.at_ref, bf16[32,1664]{1,0:T(8,128)(2,1)} %shard_map.55.refs_0_, bf16[32,1664]{1,0:T(8,128)(2,1)} %copy-done.3, bf16[32,1664]{1,0:T(8,128)(2,1)} %copy-done.4, bf16[32,1664]{1,0:T(8,128)(2,1)} %copy-done.5, bf16[1536,2048]{1,0:T(8,128)(2,1)} %refs_4_.7, ...), custom_call_target="tpu_custom_call" | custom-call | flops 805306368 | bytes 6291456 | tf_op jit(solution)/shard_map/pallas_call | solution.py:146
  41.6 6.1 %shard_map.58 = f32[2,128,1024]{2,1,0:T(8,128)} custom-call(s32[3]{0:T(128)} %pad_add_fusion.at_ref, bf16[32,1664]{1,0:T(8,128)(2,1)} %copy-done.2, bf16[32,1664]{1,0:T(8,128)(2,1)} %copy-done.6, bf16[32,1664]{1,0:T(8,128)(2,1)} %copy-done.7, bf16[32,1664]{1,0:T(8,128)(2,1)} %copy-done.8, bf16[1536,2048]{1,0:T(8,128)(2,1)} %refs_4_.7, bf16[1536,2048]{1,0:T(8,128)(2,1)} %refs_5_.7), custom_call_target="tpu_custom_call" | custom-call | flops 805306368 | bytes 6291456 | tf_op jit(solution)/shard_map/pallas_call | solution.py:146
  49.4 1.6 %collective-permute-start.8 = (bf16[128,1024]{1,0:T(8,128)(2,1)S(1)}, bf16[128,1024]{1,0:T(8,128)(2,1)S(1)}, u32[]{:S(2)}, u32[]{:S(2)}) collective-permute-start(bf16[128,1024]{1,0:T(8,128)(2,1)S(1)} %fusion.10), channel_id=1, source_target_pairs={{0,2},{1,3},{2,0},{3,1},{4,6},{5,7},{6,4},{7,5},{8,10},{9,11},{10,... | collective-permute-start | bytes 786440 | tf_op jit(solution)/shard_map/ppermute | solution.py:86
  53.3 5.3 %collective-permute-done.8 = bf16[128,1024]{1,0:T(8,128)(2,1)S(1)} collective-permute-done((bf16[128,1024]{1,0:T(8,128)(2,1)S(1)}, bf16[128,1024]{1,0:T(8,128)(2,1)S(1)}, u32[]{:S(2)}, u32[]{:S(2)}) %collective-permute-start.8) | collective-permute-done | bytes 262176 | tf_op jit(solution)/shard_map/ppermute | solution.py:86
  60.0 3.8 %collective-permute-start.9 = (bf16[128,512]{1,0:T(8,128)(2,1)S(1)}, bf16[128,512]{1,0:T(8,128)(2,1)S(1)}, u32[]{:S(2)}, u32[]{:S(2)}) collective-permute-start(bf16[128,512]{1,0:T(8,128)(2,1)S(1)} %fusion.13), channel_id=1, source_target_pairs={{0,2},{1,3},{2,0},{3,1},{4,6},{5,7},{6,4},{7,5},{8,10},{9,11},{10,... | collective-permute-start | bytes 393224 | tf_op jit(solution)/shard_map/ppermute | solution.py:86
  63.8 3.2 %collective-permute-start.12 = (bf16[128,512]{1,0:T(8,128)(2,1)S(1)}, bf16[128,512]{1,0:T(8,128)(2,1)S(1)}, u32[]{:S(2)}, u32[]{:S(2)}) collective-permute-start(bf16[128,512]{1,0:T(8,128)(2,1)S(1)} %fusion.13), channel_id=1, source_target_pairs={{2,16},{3,17},{6,20},{7,21},{10,24},{11,25},{14,28},{15,29},{16,2}... | collective-permute-start | bytes 393224 | tf_op jit(solution)/shard_map/ppermute | solution.py:86
  67.4 1.3 collective-permute-start.22
  68.7 3.8 %collective-permute-start.20 = (bf16[128,512]{1,0:T(8,128)(2,1)S(1)}, bf16[128,512]{1,0:T(8,128)(2,1)S(1)}, u32[]{:S(2)}, u32[]{:S(2)}) collective-permute-start(bf16[128,512]{1,0:T(8,128)(2,1)S(1)} %fusion.12), channel_id=1, source_target_pairs={{0,2},{1,3},{2,0},{3,1},{4,6},{5,7},{6,4},{7,5},{8,10},{9,11},{10,... | collective-permute-start | bytes 393224 | tf_op jit(solution)/shard_map/ppermute | solution.py:86
  72.5 3.2 %collective-permute-start.23 = (bf16[128,512]{1,0:T(8,128)(2,1)S(1)}, bf16[128,512]{1,0:T(8,128)(2,1)S(1)}, u32[]{:S(2)}, u32[]{:S(2)}) collective-permute-start(bf16[128,512]{1,0:T(8,128)(2,1)S(1)} %fusion.12), channel_id=1, source_target_pairs={{2,16},{3,17},{6,20},{7,21},{10,24},{11,25},{14,28},{15,29},{16,2}... | collective-permute-start | bytes 393224 | tf_op jit(solution)/shard_map/ppermute | solution.py:86
  76.5 4.7 %collective-permute-done.23 = bf16[128,512]{1,0:T(8,128)(2,1)S(1)} collective-permute-done((bf16[128,512]{1,0:T(8,128)(2,1)S(1)}, bf16[128,512]{1,0:T(8,128)(2,1)S(1)}, u32[]{:S(2)}, u32[]{:S(2)}) %collective-permute-start.23) | collective-permute-done | bytes 131104 | tf_op jit(solution)/shard_map/ppermute | solution.py:86
  83.8 5.1 %collective-permute-start.26 = (bf16[128,2048]{1,0:T(8,128)(2,1)S(1)}, bf16[128,2048]{1,0:T(8,128)(2,1)}, u32[]{:S(2)}, u32[]{:S(2)}) collective-permute-start(bf16[128,2048]{1,0:T(8,128)(2,1)S(1)} %get-tuple-element.11), channel_id=1, source_target_pairs={{0,8},{2,10},{4,12},{6,14},{9,1},{11,3},{13,5},{15,7},{16,24},{18,... | collective-permute-start | bytes 1572872 | tf_op jit(solution)/shard_map/ppermute | solution.py:86
  88.9 2.7 %collective-permute-start.25 = (bf16[128,2048]{1,0:T(8,128)(2,1)S(1)}, bf16[128,2048]{1,0:T(8,128)(2,1)S(1)}, u32[]{:S(2)}, u32[]{:S(2)}) collective-permute-start(bf16[128,2048]{1,0:T(8,128)(2,1)S(1)} %get-tuple-element.11), channel_id=1, source_target_pairs={{0,4},{2,6},{4,0},{6,2},{9,13},{11,15},{13,9},{15,11},{16,20},{18,... | collective-permute-start | bytes 1572872 | tf_op jit(solution)/shard_map/ppermute | solution.py:86
  91.6 2.1 %collective-permute-start.15 = (bf16[128,2048]{1,0:T(8,128)(2,1)S(1)}, bf16[128,2048]{1,0:T(8,128)(2,1)}, u32[]{:S(2)}, u32[]{:S(2)}) collective-permute-start(bf16[128,2048]{1,0:T(8,128)(2,1)S(1)} %get-tuple-element.12), channel_id=1, source_target_pairs={{0,8},{2,10},{4,12},{6,14},{9,1},{11,3},{13,5},{15,7},{16,24},{18,... | collective-permute-start | bytes 1572872 | tf_op jit(solution)/shard_map/ppermute | solution.py:86
  93.7 3.2 %collective-permute-start.14 = (bf16[128,2048]{1,0:T(8,128)(2,1)S(1)}, bf16[128,2048]{1,0:T(8,128)(2,1)S(1)}, u32[]{:S(2)}, u32[]{:S(2)}) collective-permute-start(bf16[128,2048]{1,0:T(8,128)(2,1)S(1)} %get-tuple-element.12), channel_id=1, source_target_pairs={{0,4},{2,6},{4,0},{6,2},{9,13},{11,15},{13,9},{15,11},{16,20},{18,... | collective-permute-start | bytes 1572872 | tf_op jit(solution)/shard_map/ppermute | solution.py:86
  100.8 2.8 %collective-permute-start.28 = (bf16[128,1024]{1,0:T(8,128)(2,1)S(1)}, bf16[128,1024]{1,0:T(8,128)(2,1)}, u32[]{:S(2)}, u32[]{:S(2)}) collective-permute-start(bf16[128,1024]{1,0:T(8,128)(2,1)S(1)} %slice.175), channel_id=1, source_target_pairs={{0,8},{2,10},{4,12},{6,14},{9,1},{11,3},{13,5},{15,7},{16,24},{18,... | collective-permute-start | bytes 786440 | tf_op jit(solution)/shard_map/ppermute | solution.py:86
  104.6 1.4 collective-permute-start.16
  106.0 5.2 %collective-permute-done.14 = bf16[128,2048]{1,0:T(8,128)(2,1)S(1)} collective-permute-done((bf16[128,2048]{1,0:T(8,128)(2,1)S(1)}, bf16[128,2048]{1,0:T(8,128)(2,1)S(1)}, u32[]{:S(2)}, u32[]{:S(2)}) %collective-permute-start.14) | collective-permute-done | bytes 524320 | tf_op jit(solution)/shard_map/ppermute | solution.py:86
  111.2 2.0 %collective-permute-start.17 = (bf16[128,1024]{1,0:T(8,128)(2,1)S(1)}, bf16[128,1024]{1,0:T(8,128)(2,1)}, u32[]{:S(2)}, u32[]{:S(2)}) collective-permute-start(bf16[128,1024]{1,0:T(8,128)(2,1)S(1)} %slice.163), channel_id=1, source_target_pairs={{0,8},{2,10},{4,12},{6,14},{9,1},{11,3},{13,5},{15,7},{16,24},{18,... | collective-permute-start | bytes 786440 | tf_op jit(solution)/shard_map/ppermute | solution.py:86
  115.0 9.4 %shard_map.60.refs_0_ = f32[4096,2048]{1,0:T(8,128)} custom-call(s32[1]{0:T(128)} %bitcast.at_ref, f32[1]{0:T(128)} %bitcast.3.scale_ref, bf16[128,2048]{1,0:T(8,128)(2,1)} %broadcast_select_fusion.3.first_ref, bf16[128,2048]{1,0:T(8,128)(2,1)} %broadcast_select_fusion.2.second_ref, bf16[256,2048]{1,0:T(8,128)(2,1)} %pad_maximum_fusion.columns_ref), custom_call_target="tpu_custom_call" | custom-call | flops 2147483648 | bytes 16777216 | tf_op jit(solution)/shard_map/pallas_call | solution.py:192
  124.4 1.9 %maximum_select_fusion.3.second_ref = bf16[128,2048]{1,0:T(8,128)(2,1)} fusion(bf16[128,2048]{1,0:T(8,128)(2,1)S(1)} %collective-permute-done.25, bf16[128,1024]{1,0:T(8,128)(2,1)} %collective-permute-done.28, bf16[128,1024]{1,0:T(8,128)(2,1)S(1)} %collective-permute-done.27, pred[]{:T(512)S(6)} %eq.91), kind=kLoop, calls=%fused_computation.26 | loop fusion | flops 1310720 | bytes 1572865 | tf_op jit(solution)/shard_map/jit(_where)/select_n | solution.py:255
  126.3 2.0 %maximum_select_fusion.1.first_ref = bf16[128,2048]{1,0:T(8,128)(2,1)} fusion(bf16[128,2048]{1,0:T(8,128)(2,1)S(1)} %collective-permute-done.14, bf16[128,1024]{1,0:T(8,128)(2,1)} %collective-permute-done.17, bf16[128,1024]{1,0:T(8,128)(2,1)} %collective-permute-done.16, pred[]{:T(512)S(6)} %eq.91), kind=kLoop, calls=%fused_computation.19 | loop fusion | flops 1310720 | bytes 1572865 | tf_op jit(solution)/shard_map/jit(_where)/select_n | solution.py:255
  128.3 9.5 %shard_map.61 = f32[4096,2048]{1,0:T(8,128)} custom-call(s32[1]{0:T(128)S(6)} %sub.23.at_ref, f32[1]{0:T(128)} %bitcast.3.scale_ref, bf16[128,2048]{1,0:T(8,128)(2,1)} %maximum_select_fusion.1.first_ref, bf16[128,2048]{1,0:T(8,128)(2,1)} %maximum_select_fusion.3.second_ref, ...), custom_call_target="tpu_custom_call", output_to_operand_aliasing={{}: (5, {})} | custom-call | flops 2147483648 | bytes 16777216 | tf_op jit(solution)/shard_map/pallas_call | solution.py:192
  (86 shorter events, 20.6 us)
Async XLA Ops:
  2.0 17.0 %collective-permute-start.3 = (bf16[32,1664]{1,0:T(8,128)(2,1)}, bf16[32,1664]{1,0:T(8,128)(2,1)S(1)}, u32[]{:S(2)}, u32[]{:S(2)}) collective-permute-start(bf16[32,1664]{1,0:T(8,128)(2,1)} %shard_map.55.refs_0_), channel_id=1, source_target_pairs={{0,16},{1,17},{2,18},{3,19},{4,20},{5,21},{6,22},{7,23},{8,24},{9,... | collective-permute-start | bytes 319496 | tf_op jit(solution)/shard_map/ppermute | solution.py:86
  2.0 4.9 %collective-permute-start.2 = (bf16[32,1664]{1,0:T(8,128)(2,1)}, bf16[32,1664]{1,0:T(8,128)(2,1)S(1)}, u32[]{:S(2)}, u32[]{:S(2)}) collective-permute-start(bf16[32,1664]{1,0:T(8,128)(2,1)} %shard_map.55.refs_0_), channel_id=1, source_target_pairs={{0,4},{1,5},{2,6},{3,7},{4,0},{5,1},{6,2},{7,3},{8,12},{9,13},{10,... | collective-permute-start | bytes 319496 | tf_op jit(solution)/shard_map/ppermute | solution.py:86
  3.8 6.9 %collective-permute-start.1 = (bf16[32,1664]{1,0:T(8,128)(2,1)}, bf16[32,1664]{1,0:T(8,128)(2,1)S(1)}, u32[]{:S(2)}, u32[]{:S(2)}) collective-permute-start(bf16[32,1664]{1,0:T(8,128)(2,1)} %shard_map.55.refs_0_), channel_id=1, source_target_pairs={{0,8},{1,9},{2,10},{3,11},{4,12},{5,13},{6,14},{7,15},{8,0},{9,1},... | collective-permute-start | bytes 319496 | tf_op jit(solution)/shard_map/ppermute | solution.py:86
  5.4 6.9 %collective-permute-start = (bf16[32,1664]{1,0:T(8,128)(2,1)}, bf16[32,1664]{1,0:T(8,128)(2,1)S(1)}, u32[]{:S(2)}, u32[]{:S(2)}) collective-permute-start(bf16[32,1664]{1,0:T(8,128)(2,1)} %shard_map.55.refs_0_), channel_id=1, source_target_pairs={{0,12},{1,13},{2,14},{3,15},{4,8},{5,9},{6,10},{7,11},{8,4},{9,5},... | collective-permute-start | bytes 319496 | tf_op jit(solution)/shard_map/ppermute | solution.py:86
  19.0 30.3 %collective-permute-start.7 = (f32[2,128,1024]{2,1,0:T(8,128)}, f32[2,128,1024]{2,1,0:T(8,128)S(1)}, u32[]{:S(2)}, u32[]{:S(2)}) collective-permute-start(f32[2,128,1024]{2,1,0:T(8,128)} %shard_map.57), channel_id=1, source_target_pairs={{0,1},{1,0},{2,3},{3,2},{4,5},{5,4},{6,7},{7,6},{8,9},{9,8},{10,11... | collective-permute-start | bytes 3145736 | tf_op jit(solution)/shard_map/ppermute | solution.py:86
  19.0 9.2 %copy-start.2 = (bf16[32,1664]{1,0:T(8,128)(2,1)}, bf16[32,1664]{1,0:T(8,128)(2,1)S(1)}, u32[]{:S(2)}) copy-start(bf16[32,1664]{1,0:T(8,128)(2,1)S(1)} %collective-permute-done.3.refs_0_) | copy-start | bytes 319492
  19.0 5.4 %collective-permute-start.6 = (bf16[32,1664]{1,0:T(8,128)(2,1)S(1)}, bf16[32,1664]{1,0:T(8,128)(2,1)S(1)}, u32[]{:S(2)}, u32[]{:S(2)}) collective-permute-start(bf16[32,1664]{1,0:T(8,128)(2,1)S(1)} %collective-permute-done.3.refs_0_), channel_id=1, source_target_pairs={{0,4},{1,5},{2,6},{3,7},{4,0},{5,1},{6,2},{7,3},{8,12},{9,13},{10,... | collective-permute-start | bytes 319496 | tf_op jit(solution)/shard_map/ppermute | solution.py:86
  19.6 6.6 %collective-permute-start.5 = (bf16[32,1664]{1,0:T(8,128)(2,1)S(1)}, bf16[32,1664]{1,0:T(8,128)(2,1)S(1)}, u32[]{:S(2)}, u32[]{:S(2)}) collective-permute-start(bf16[32,1664]{1,0:T(8,128)(2,1)S(1)} %collective-permute-done.3.refs_0_), channel_id=1, source_target_pairs={{0,8},{1,9},{2,10},{3,11},{4,12},{5,13},{6,14},{7,15},{8,0},{9,1},... | collective-permute-start | bytes 319496 | tf_op jit(solution)/shard_map/ppermute | solution.py:86
  22.5 5.7 %collective-permute-start.4 = (bf16[32,1664]{1,0:T(8,128)(2,1)S(1)}, bf16[32,1664]{1,0:T(8,128)(2,1)S(1)}, u32[]{:S(2)}, u32[]{:S(2)}) collective-permute-start(bf16[32,1664]{1,0:T(8,128)(2,1)S(1)} %collective-permute-done.3.refs_0_), channel_id=1, source_target_pairs={{0,12},{1,13},{2,14},{3,15},{4,8},{5,9},{6,10},{7,11},{8,4},{9,5},... | collective-permute-start | bytes 319496 | tf_op jit(solution)/shard_map/ppermute | solution.py:86
  34.8 16.8 %collective-permute-start.18 = (f32[2,128,1024]{2,1,0:T(8,128)}, f32[2,128,1024]{2,1,0:T(8,128)S(1)}, u32[]{:S(2)}, u32[]{:S(2)}) collective-permute-start(f32[2,128,1024]{2,1,0:T(8,128)} %shard_map.59), channel_id=1, source_target_pairs={{0,1},{1,0},{2,3},{3,2},{4,5},{5,4},{6,7},{7,6},{8,9},{9,8},{10,11... | collective-permute-start | bytes 3145736 | tf_op jit(solution)/shard_map/ppermute | solution.py:86
  41.6 7.7 %copy-start.1 = (f32[2,128,1024]{2,1,0:T(8,128)S(1)}, f32[2,128,1024]{2,1,0:T(8,128)}, u32[]{:S(2)}) copy-start(f32[2,128,1024]{2,1,0:T(8,128)} %shard_map.56) | copy-start | bytes 3145732
  47.7 19.4 %copy-start = (f32[2,128,1024]{2,1,0:T(8,128)S(1)}, f32[2,128,1024]{2,1,0:T(8,128)}, u32[]{:S(2)}) copy-start(f32[2,128,1024]{2,1,0:T(8,128)} %shard_map.58) | copy-start | bytes 3145732
  49.4 9.2 %collective-permute-start.8 = (bf16[128,1024]{1,0:T(8,128)(2,1)S(1)}, bf16[128,1024]{1,0:T(8,128)(2,1)S(1)}, u32[]{:S(2)}, u32[]{:S(2)}) collective-permute-start(bf16[128,1024]{1,0:T(8,128)(2,1)S(1)} %fusion.10), channel_id=1, source_target_pairs={{0,2},{1,3},{2,0},{3,1},{4,6},{5,7},{6,4},{7,5},{8,10},{9,11},{10,... | collective-permute-start | bytes 786440 | tf_op jit(solution)/shard_map/ppermute | solution.py:86
  52.7 14.4 %collective-permute-start.19 = (bf16[128,1024]{1,0:T(8,128)(2,1)S(1)}, bf16[128,1024]{1,0:T(8,128)(2,1)S(1)}, u32[]{:S(2)}, u32[]{:S(2)}) collective-permute-start(bf16[128,1024]{1,0:T(8,128)(2,1)S(1)} %fusion.11), channel_id=1, source_target_pairs={{0,2},{1,3},{2,0},{3,1},{4,6},{5,7},{6,4},{7,5},{8,10},{9,11},{10,... | collective-permute-start | bytes 786440 | tf_op jit(solution)/shard_map/ppermute | solution.py:86
  58.7 17.0 %collective-permute-start.11 = (bf16[128,512]{1,0:T(8,128)(2,1)S(1)}, bf16[128,512]{1,0:T(8,128)(2,1)S(1)}, u32[]{:S(2)}, u32[]{:S(2)}) collective-permute-start(bf16[128,512]{1,0:T(8,128)(2,1)S(1)} %fusion.13), channel_id=1, source_target_pairs={{0,16},{1,17},{4,20},{5,21},{8,24},{9,25},{12,28},{13,29},{18,2},{... | collective-permute-start | bytes 393224 | tf_op jit(solution)/shard_map/ppermute | solution.py:86
  60.0 12.5 %collective-permute-start.9 = (bf16[128,512]{1,0:T(8,128)(2,1)S(1)}, bf16[128,512]{1,0:T(8,128)(2,1)S(1)}, u32[]{:S(2)}, u32[]{:S(2)}) collective-permute-start(bf16[128,512]{1,0:T(8,128)(2,1)S(1)} %fusion.13), channel_id=1, source_target_pairs={{0,2},{1,3},{2,0},{3,1},{4,6},{5,7},{6,4},{7,5},{8,10},{9,11},{10,... | collective-permute-start | bytes 393224 | tf_op jit(solution)/shard_map/ppermute | solution.py:86
  63.8 11.9 %collective-permute-start.12 = (bf16[128,512]{1,0:T(8,128)(2,1)S(1)}, bf16[128,512]{1,0:T(8,128)(2,1)S(1)}, u32[]{:S(2)}, u32[]{:S(2)}) collective-permute-start(bf16[128,512]{1,0:T(8,128)(2,1)S(1)} %fusion.13), channel_id=1, source_target_pairs={{2,16},{3,17},{6,20},{7,21},{10,24},{11,25},{14,28},{15,29},{16,2}... | collective-permute-start | bytes 393224 | tf_op jit(solution)/shard_map/ppermute | solution.py:86
  67.4 9.1 %collective-permute-start.22 = (bf16[128,512]{1,0:T(8,128)(2,1)S(1)}, bf16[128,512]{1,0:T(8,128)(2,1)S(1)}, u32[]{:S(2)}, u32[]{:S(2)}) collective-permute-start(bf16[128,512]{1,0:T(8,128)(2,1)S(1)} %fusion.12), channel_id=1, source_target_pairs={{0,16},{1,17},{4,20},{5,21},{8,24},{9,25},{12,28},{13,29},{18,2},{... | collective-permute-start | bytes 393224 | tf_op jit(solution)/shard_map/ppermute | solution.py:86
  68.7 7.7 %collective-permute-start.20 = (bf16[128,512]{1,0:T(8,128)(2,1)S(1)}, bf16[128,512]{1,0:T(8,128)(2,1)S(1)}, u32[]{:S(2)}, u32[]{:S(2)}) collective-permute-start(bf16[128,512]{1,0:T(8,128)(2,1)S(1)} %fusion.12), channel_id=1, source_target_pairs={{0,2},{1,3},{2,0},{3,1},{4,6},{5,7},{6,4},{7,5},{8,10},{9,11},{10,... | collective-permute-start | bytes 393224 | tf_op jit(solution)/shard_map/ppermute | solution.py:86
  72.5 8.7 %collective-permute-start.23 = (bf16[128,512]{1,0:T(8,128)(2,1)S(1)}, bf16[128,512]{1,0:T(8,128)(2,1)S(1)}, u32[]{:S(2)}, u32[]{:S(2)}) collective-permute-start(bf16[128,512]{1,0:T(8,128)(2,1)S(1)} %fusion.12), channel_id=1, source_target_pairs={{2,16},{3,17},{6,20},{7,21},{10,24},{11,25},{14,28},{15,29},{16,2}... | collective-permute-start | bytes 393224 | tf_op jit(solution)/shard_map/ppermute | solution.py:86
  75.7 5.6 %collective-permute-start.10 = (bf16[2,128,512]{2,1,0:T(8,128)(2,1)S(1)}, bf16[2,128,512]{2,1,0:T(8,128)(2,1)S(1)}, u32[]{:S(2)}, u32[]{:S(2)}) collective-permute-start(bf16[2,128,512]{2,1,0:T(8,128)(2,1)S(1)} %pad_maximum_fusion.7), channel_id=1, source_target_pairs={{0,1},{1,0},{2,3},{3,2},{4,5},{5,4},{6,7},{7,6},{8,9},{9,8},{10,11... | collective-permute-start | bytes 786440 | tf_op jit(solution)/shard_map/ppermute | solution.py:86
  75.8 5.6 %collective-permute-start.13 = (bf16[2,128,512]{2,1,0:T(8,128)(2,1)S(1)}, bf16[2,128,512]{2,1,0:T(8,128)(2,1)S(1)}, u32[]{:S(2)}, u32[]{:S(2)}) collective-permute-start(bf16[2,128,512]{2,1,0:T(8,128)(2,1)S(1)} %pad_maximum_fusion.8), channel_id=1, source_target_pairs={{0,1},{1,0},{2,3},{3,2},{4,5},{5,4},{6,7},{7,6},{8,9},{9,8},{10,11... | collective-permute-start | bytes 786440 | tf_op jit(solution)/shard_map/ppermute | solution.py:86
  76.4 5.3 %collective-permute-start.21 = (bf16[2,128,512]{2,1,0:T(8,128)(2,1)S(1)}, bf16[2,128,512]{2,1,0:T(8,128)(2,1)S(1)}, u32[]{:S(2)}, u32[]{:S(2)}) collective-permute-start(bf16[2,128,512]{2,1,0:T(8,128)(2,1)S(1)} %pad_maximum_fusion.9), channel_id=1, source_target_pairs={{0,1},{1,0},{2,3},{3,2},{4,5},{5,4},{6,7},{7,6},{8,9},{9,8},{10,11... | collective-permute-start | bytes 786440 | tf_op jit(solution)/shard_map/ppermute | solution.py:86
  81.3 1.6 %collective-permute-start.24 = (bf16[2,128,512]{2,1,0:T(8,128)(2,1)S(1)}, bf16[2,128,512]{2,1,0:T(8,128)(2,1)S(1)}, u32[]{:S(2)}, u32[]{:S(2)}) collective-permute-start(bf16[2,128,512]{2,1,0:T(8,128)(2,1)S(1)} %pad_maximum_fusion.10), channel_id=1, source_target_pairs={{0,1},{1,0},{2,3},{3,2},{4,5},{5,4},{6,7},{7,6},{8,9},{9,8},{10,11... | collective-permute-start | bytes 786440 | tf_op jit(solution)/shard_map/ppermute | solution.py:86
  83.8 15.4 %collective-permute-start.26 = (bf16[128,2048]{1,0:T(8,128)(2,1)S(1)}, bf16[128,2048]{1,0:T(8,128)(2,1)}, u32[]{:S(2)}, u32[]{:S(2)}) collective-permute-start(bf16[128,2048]{1,0:T(8,128)(2,1)S(1)} %get-tuple-element.11), channel_id=1, source_target_pairs={{0,8},{2,10},{4,12},{6,14},{9,1},{11,3},{13,5},{15,7},{16,24},{18,... | collective-permute-start | bytes 1572872 | tf_op jit(solution)/shard_map/ppermute | solution.py:86
  88.9 11.9 %collective-permute-start.25 = (bf16[128,2048]{1,0:T(8,128)(2,1)S(1)}, bf16[128,2048]{1,0:T(8,128)(2,1)S(1)}, u32[]{:S(2)}, u32[]{:S(2)}) collective-permute-start(bf16[128,2048]{1,0:T(8,128)(2,1)S(1)} %get-tuple-element.11), channel_id=1, source_target_pairs={{0,4},{2,6},{4,0},{6,2},{9,13},{11,15},{13,9},{15,11},{16,20},{18,... | collective-permute-start | bytes 1572872 | tf_op jit(solution)/shard_map/ppermute | solution.py:86
  91.6 12.1 %collective-permute-start.15 = (bf16[128,2048]{1,0:T(8,128)(2,1)S(1)}, bf16[128,2048]{1,0:T(8,128)(2,1)}, u32[]{:S(2)}, u32[]{:S(2)}) collective-permute-start(bf16[128,2048]{1,0:T(8,128)(2,1)S(1)} %get-tuple-element.12), channel_id=1, source_target_pairs={{0,8},{2,10},{4,12},{6,14},{9,1},{11,3},{13,5},{15,7},{16,24},{18,... | collective-permute-start | bytes 1572872 | tf_op jit(solution)/shard_map/ppermute | solution.py:86
  93.7 17.5 %collective-permute-start.14 = (bf16[128,2048]{1,0:T(8,128)(2,1)S(1)}, bf16[128,2048]{1,0:T(8,128)(2,1)S(1)}, u32[]{:S(2)}, u32[]{:S(2)}) collective-permute-start(bf16[128,2048]{1,0:T(8,128)(2,1)S(1)} %get-tuple-element.12), channel_id=1, source_target_pairs={{0,4},{2,6},{4,0},{6,2},{9,13},{11,15},{13,9},{15,11},{16,20},{18,... | collective-permute-start | bytes 1572872 | tf_op jit(solution)/shard_map/ppermute | solution.py:86
  100.1 24.3 %collective-permute-start.27 = (bf16[128,1024]{1,0:T(8,128)(2,1)S(1)}, bf16[128,1024]{1,0:T(8,128)(2,1)S(1)}, u32[]{:S(2)}, u32[]{:S(2)}) collective-permute-start(bf16[128,1024]{1,0:T(8,128)(2,1)S(1)} %slice.174), channel_id=1, source_target_pairs={{1,5},{3,7},{5,1},{7,3},{8,12},{10,14},{12,8},{14,10},{17,21},{19,... | collective-permute-start | bytes 786440 | tf_op jit(solution)/shard_map/ppermute | solution.py:86
  100.8 23.6 %collective-permute-start.28 = (bf16[128,1024]{1,0:T(8,128)(2,1)S(1)}, bf16[128,1024]{1,0:T(8,128)(2,1)}, u32[]{:S(2)}, u32[]{:S(2)}) collective-permute-start(bf16[128,1024]{1,0:T(8,128)(2,1)S(1)} %slice.175), channel_id=1, source_target_pairs={{0,8},{2,10},{4,12},{6,14},{9,1},{11,3},{13,5},{15,7},{16,24},{18,... | collective-permute-start | bytes 786440 | tf_op jit(solution)/shard_map/ppermute | solution.py:86
  104.6 21.7 %collective-permute-start.16 = (bf16[128,1024]{1,0:T(8,128)(2,1)S(1)}, bf16[128,1024]{1,0:T(8,128)(2,1)}, u32[]{:S(2)}, u32[]{:S(2)}) collective-permute-start(bf16[128,1024]{1,0:T(8,128)(2,1)S(1)} %slice.162), channel_id=1, source_target_pairs={{1,5},{3,7},{5,1},{7,3},{8,12},{10,14},{12,8},{14,10},{17,21},{19,... | collective-permute-start | bytes 786440 | tf_op jit(solution)/shard_map/ppermute | solution.py:86
  111.2 15.1 %collective-permute-start.17 = (bf16[128,1024]{1,0:T(8,128)(2,1)S(1)}, bf16[128,1024]{1,0:T(8,128)(2,1)}, u32[]{:S(2)}, u32[]{:S(2)}) collective-permute-start(bf16[128,1024]{1,0:T(8,128)(2,1)S(1)} %slice.163), channel_id=1, source_target_pairs={{0,8},{2,10},{4,12},{6,14},{9,1},{11,3},{13,5},{15,7},{16,24},{18,... | collective-permute-start | bytes 786440 | tf_op jit(solution)/shard_map/ppermute | solution.py:86
  (6 other events, 14.0 us)

commit v3 on v0

v3 whole, which is shorter than its diff:
```python
import functools

import jax
import jax.numpy as jnp
from jax import lax
from jax.experimental import pallas as pl
from jax.experimental.pallas import tpu as pltpu
from jax.sharding import PartitionSpec as P

CAP = 32
LANES = 128
BF, F32 = jnp.bfloat16, jnp.float32
AXES = ("dp", "tensor")
ROWS_OF = (((0,), (0,)), ((), ()))


def pack_rows(token_blocks, weight_blocks):
    member = (weight_blocks > 0).astype(jnp.int32)
    position = jnp.cumsum(member, axis=1) - 1
    slot_index = lax.broadcasted_iota(jnp.int32, (1, CAP, 1), 1)
    picked = (position[:, None, :] == slot_index) & (member[:, None, :] > 0)
    selector = picked.astype(BF)
    packed = jnp.einsum(
        "sct,std->scd", selector, token_blocks, preferred_element_type=F32
    ).astype(BF)
    packed_weight = jnp.einsum(
        "sct,st->sc", selector, weight_blocks, preferred_element_type=F32
    ).astype(BF)
    return (packed.reshape(-1, token_blocks.shape[2]), packed_weight.reshape(-1))


def any_mesh(hidden_states, expert_ids, route_gates, gate_weight, up_weight):
    route_weight = jnp.sum(
        jnp.where(expert_ids == 0, route_gates, jnp.zeros_like(route_gates)), axis=1
    ).astype(BF)
    own_rows, own_weight = pack_rows(hidden_states[None], route_weight[None])
    packed_rows, packed_weight = (
        lax.all_gather(own_rows, "dp", axis=0, tiled=True),
        lax.all_gather(own_weight, "dp", axis=0, tiled=True),
    )
    weight_total = jnp.sum(packed_weight.astype(F32))
    gate_part = jnp.dot(packed_rows, gate_weight, preferred_element_type=F32)
    up_part = jnp.dot(packed_rows, up_weight, preferred_element_type=F32)
    summed = lax.psum_scatter(
        jnp.concatenate([gate_part, up_part], axis=1), "tensor", scatter_dimension=0, tiled=True
    )
    unit_width = gate_weight.shape[1]
    local_keys = (jax.nn.silu(summed[:, :unit_width]) * summed[:, unit_width:]).astype(BF)
    column_keys = lax.all_gather(local_keys, "tensor", axis=0, tiled=True)
    weighted = (packed_weight.astype(F32)[:, None] * column_keys.astype(F32)).astype(BF)
    spread_keys = lax.all_gather(local_keys, "dp", axis=1, tiled=True)
    row_keys = lax.all_to_all(spread_keys, "tensor", split_axis=1, concat_axis=0, tiled=True)
    covariance = lax.dot_general(row_keys, weighted, ROWS_OF, preferred_element_type=F32)
    return covariance / weight_total


def pairs(to):
    number = lambda z, x, y, c: z * 8 + x * 4 + y * 2 + c
    out = []
    for z in range(4):
        for x in range(2):
            for y in range(2):
                for c in range(2):
                    there = to(z, x, y, c)
                    if there is not None:
                        out.append((number(z, x, y, c), number(*there)))
    return out


def inside(z, y):
    return z // 2 == y


CORE = pairs(lambda z, x, y, c: (z, x, y, 1 - c))
Y = pairs(lambda z, x, y, c: (z, x, 1 - y, c))
X = pairs(lambda z, x, y, c: (z, 1 - x, y, c))
Z1 = pairs(lambda z, x, y, c: (z ^ 1, x, y, c))
Z2 = pairs(lambda z, x, y, c: (z ^ 2, x, y, c))
XZ1 = pairs(lambda z, x, y, c: (z ^ 1, 1 - x, y, c))
FAR = pairs(lambda z, x, y, c: (z ^ 2, x, y, c) if inside(z, y) else None)
FAR_Y = pairs(lambda z, x, y, c: (z ^ 2, x, 1 - y, c) if not inside(z, y) else None)
SHARE = pairs(lambda z, x, y, c: (z ^ 1, x, y, c) if c == z % 2 else (z, 1 - x, y, 1 - c))
HOME_Z1 = pairs(lambda z, x, y, c: (z ^ 1, x, y, c) if c == z % 2 else None)
AWAY_X = pairs(lambda z, x, y, c: (z, 1 - x, y, c) if c != z % 2 else None)

VM = pl.BlockSpec(memory_space=pltpu.VMEM)
SM = pl.BlockSpec(memory_space=pltpu.SMEM)


def send(value, route):
    return lax.ppermute(value, AXES, route)


def cost(flops, nbytes):
    return pl.CostEstimate(flops=flops, bytes_accessed=nbytes, transcendentals=0)


def limit(mebibytes):
    return pltpu.CompilerParams(vmem_limit_bytes=mebibytes << 20)


def shaped(rows, width, kind):
    return jax.ShapeDtypeStruct((rows, width), kind)


def before(rows):
    down = lax.broadcasted_iota(jnp.int32, (rows, rows), 0)
    return jnp.where(down <= lax.broadcasted_iota(jnp.int32, (rows, rows), 1), 1.0, 0.0).astype(BF)


def pack_kernel(ids_ref, gates_ref, tokens_ref, out_ref):
    tokens, width = tokens_ref.shape
    weight = jnp.sum(jnp.where(ids_ref[...] == 0, gates_ref[...], 0.0), axis=0, keepdims=True)
    weight = weight.astype(BF).astype(F32)
    member = jnp.where(weight > 0, 1.0, 0.0)
    position = jnp.dot(
        jnp.broadcast_to(member, (8, tokens)).astype(BF),
        before(tokens),
        preferred_element_type=F32,
    )[:1]
    slot = lax.broadcasted_iota(jnp.int32, (CAP, tokens), 0).astype(F32)
    picked = jnp.where((position - 1.0 == slot) & (member > 0), 1.0, 0.0)
    out_ref[:, :width] = jnp.dot(
        picked.astype(BF), tokens_ref[...], preferred_element_type=F32
    ).astype(BF)
    weights = jnp.sum(picked * weight, axis=1, keepdims=True)
    out_ref[:, width:] = jnp.broadcast_to(weights, (CAP, LANES)).astype(BF)


def pack(hidden_states, expert_ids, route_gates):
    return pl.pallas_call(
        pack_kernel,
        out_shape=shaped(CAP, hidden_states.shape[1] + LANES, BF),
        compiler_params=limit(4),
    )(expert_ids.T, route_gates.T, hidden_states)


def load_kernel(gate_in, up_in, gate_ref, up_ref, sems):
    copies = [
        pltpu.make_async_copy(gate_in, gate_ref, sems.at[0]),
        pltpu.make_async_copy(up_in, up_ref, sems.at[1]),
    ]
    for copy in copies:
        copy.start()
    for copy in copies:
        copy.wait()


def load(gate_weight, up_weight):
    shape = jax.ShapeDtypeStruct(gate_weight.shape, BF)
    return pl.pallas_call(
        load_kernel,
        in_specs=[pl.BlockSpec(memory_space=pl.ANY)] * 2,
        out_specs=[VM, VM],
        out_shape=[shape, shape],
        scratch_shapes=[pltpu.SemaphoreType.DMA((2,))],
        compiler_params=limit(14),
        cost_estimate=cost(0, 4 * gate_weight.size),
    )(gate_weight, up_weight)


def gather_kernel(at_ref, *refs):
    blocks, (rows_ref, weights_ref, count_ref, all_ref) = refs[:8], refs[8:]
    total, depth = rows_ref.shape
    for k, block in enumerate(blocks):
        start = pl.multiple_of((at_ref[0] ^ k) * CAP, CAP)
        all_ref[pl.ds(start, CAP), :] = block[...]
    weights = all_ref[:, depth:]
    member = jnp.where(weights.astype(F32) > 0, 1.0, 0.0)
    count_ref[0] = jnp.sum(member[:, :1]).astype(jnp.int32)
    member = member.astype(BF)
    position = lax.dot_general(member, before(total), ROWS_OF, preferred_element_type=F32)[:1]
    down = lax.broadcasted_iota(jnp.int32, (total, total), 0)
    across = lax.broadcasted_iota(jnp.int32, (total, total), 1)
    same = jnp.where(down == across, 1.0, 0.0).astype(BF)
    member = lax.dot_general(member, same, ROWS_OF, preferred_element_type=F32)[:1]
    picked = (position - 1.0 == down.astype(F32)) & (member > 0)
    picked = jnp.where(picked, 1.0, 0.0).astype(BF)
    rows_ref[...] = jnp.dot(picked, all_ref[:, :depth], preferred_element_type=F32).astype(BF)
    weights_ref[...] = jnp.dot(picked, weights, preferred_element_type=F32).astype(BF)


def gather(at, blocks):
    rows, width = 8 * CAP, blocks[0].shape[1]
    return pl.pallas_call(
        gather_kernel,
        in_specs=[SM] + [VM] * 8,
        out_specs=[VM, VM, SM],
        out_shape=[
            shaped(rows, width - LANES, BF),
            shaped(rows, LANES, BF),
            jax.ShapeDtypeStruct((1,), jnp.int32),
        ],
        scratch_shapes=[pltpu.VMEM((rows, width), BF)],
        compiler_params=limit(6),
        cost_estimate=cost(1 << 28, 1 << 20),
    )(at, *blocks)


def project_kernel(at_ref, rows_ref, gate_ref, up_ref, *outs):
    rows = rows_ref[...]
    quarter = outs[0].shape[1] // 2
    for i, out_ref in enumerate(outs):
        units = pl.ds(pl.multiple_of(at_ref[i] * quarter, quarter), quarter)
        out_ref[:, :quarter] = jnp.dot(rows, gate_ref[:, units], preferred_element_type=F32)
        out_ref[:, quarter:] = jnp.dot(rows, up_ref[:, units], preferred_element_type=F32)


def project(at, rows, gate_weight, up_weight):
    units = gate_weight.shape[1]
    return pl.pallas_call(
        project_kernel,
        in_specs=[SM, VM, VM, VM],
        out_specs=[VM] * 4,
        out_shape=[shaped(rows.shape[0], units // 2, F32)] * 4,
        compiler_params=limit(4),
        cost_estimate=cost(4 * rows.size * units, 1 << 20),
    )(at, rows, gate_weight, up_weight)


def sum_kernel(kept_ref, got_ref, out_ref):
    out_ref[...] = (kept_ref[: out_ref.shape[0]] + got_ref[...]).astype(BF)


def add_up(kept, got):
    return pl.pallas_call(
        sum_kernel,
        in_specs=[VM, VM],
        out_specs=VM,
        out_shape=jax.ShapeDtypeStruct(got.shape, BF),
        compiler_params=limit(4),
        cost_estimate=cost(1 << 18, 1 << 20),
    )(kept, got)


def keys_kernel(kept_ref, got_ref, across_ref, out_ref):
    rows, width = out_ref.shape
    total = kept_ref[:rows] + got_ref[...] + across_ref[...].astype(F32)
    gate = total[:, :width]
    out_ref[...] = (gate / (1.0 + jnp.exp(-gate)) * total[:, width:]).astype(BF)


def keys_of(kept, got, across):
    rows, width = across.shape
    return pl.pallas_call(
        keys_kernel,
        in_specs=[VM, VM, VM],
        out_specs=VM,
        out_shape=shaped(rows, width // 2, BF),
        compiler_params=limit(6),
        cost_estimate=cost(1 << 18, 1 << 20),
    )(kept, got, across)


def assemble_kernel(at_ref, weights_ref, *refs):
    near, far, (columns_ref, panel_ref) = refs[:4], refs[4:8], refs[8:]
    rows, width = near[0].shape
    weights = weights_ref[:rows, :1].astype(F32)
    y, core, is_inside = at_ref[0], at_ref[1], at_ref[2] == 1
    for k in range(4):
        number = (y ^ (k % 2)) * 2 + (core ^ (k // 2))
        units = pl.ds(pl.multiple_of(number * width, width), width)
        keys = near[k][...]
        columns_ref[:, units] = (weights * keys.astype(F32)).astype(BF)
        panel_ref[:, units] = jnp.where(is_inside, keys, far[k][...])


def assemble(at, weights, near, far):
    rows, width = near[0].shape
    shape = shaped(rows, 4 * width, BF)
    return pl.pallas_call(
        assemble_kernel,
        in_specs=[SM] + [VM] * 9,
        out_specs=[VM, VM],
        out_shape=[shape, shape],
        compiler_params=limit(6),
        cost_estimate=cost(1 << 18, 1 << 20),
    )(at, weights, *near, *far)


SIZES = (160, 192, 224)
TILE = 256
BUFFERS = 4


def covariance_kernel(at_ref, weights_ref, columns_ref, mine_ref, *refs):
    theirs, (out_ref, buffer_ref, sems) = refs[:2], refs[-3:]
    is_home = at_ref[1] == 1
    rows, units = mine_ref.shape
    total = jnp.sum(weights_ref[:, :1].astype(F32), axis=0, keepdims=True)
    scale = 1.0 / total
    steps = units // TILE

    def copy(i):
        start = pl.multiple_of(at_ref[0] * units + i * TILE, TILE)
        slot = i % BUFFERS
        return pltpu.make_async_copy(
            buffer_ref.at[slot], out_ref.at[pl.ds(start, TILE)], sems.at[slot]
        )

    for i in range(steps):
        at = i * TILE
        their_ref = theirs[0]
        part = slice(at, at + TILE)
        if at >= theirs[0].shape[1]:
            their_ref = theirs[1]
            part = slice(at - theirs[0].shape[1], at - theirs[0].shape[1] + TILE)
        panel = jnp.where(is_home, mine_ref[:, at : at + TILE], their_ref[:, part])
        if i >= BUFFERS:
            copy(i - BUFFERS).wait()
        value = lax.dot_general(panel, columns_ref[...], ROWS_OF, preferred_element_type=F32)
        buffer_ref[i % BUFFERS] = value * scale
        copy(i).start()
    for i in range(steps - BUFFERS, steps):
        copy(i).wait()


def covariance_part(at, weights, columns, mine, theirs, out_rows, into):
    rows, units = mine.shape
    width = columns.shape[1]
    if len(theirs) == 1:
        theirs = theirs * 2
    args = [at, weights, columns, mine, *theirs]
    in_specs = [SM] + [VM] * 5
    aliases = {}
    if into is not None:
        args.append(into)
        in_specs.append(pl.BlockSpec(memory_space=pl.ANY))
        aliases = {6: 0}
    return pl.pallas_call(
        covariance_kernel,
        in_specs=in_specs,
        out_specs=pl.BlockSpec(memory_space=pl.ANY),
        out_shape=shaped(out_rows, width, F32),
        scratch_shapes=[
            pltpu.VMEM((BUFFERS, TILE, width), F32),
            pltpu.SemaphoreType.DMA((BUFFERS,)),
        ],
        input_output_aliases=aliases,
        compiler_params=limit(14),
        cost_estimate=cost(2 * rows * units * width, 4 * units * width),
    )(*args)


def numbers(*values):
    return jnp.stack([jnp.asarray(v, jnp.int32) for v in values])


def fast(hidden_states, expert_ids, route_gates, gate_weight, up_weight):
    units = gate_weight.shape[1]
    dp, tensor = lax.axis_index("dp"), lax.axis_index("tensor")
    z, x, y, core = dp // 2, dp % 2, tensor // 2, tensor % 2
    is_home, is_inside = core == z % 2, y == z // 2
    quarters = [(1 - y, 1 - core), (y, 1 - core), (1 - y, core), (y, core)]
    project_at = numbers(*[of_y * 2 + of_core for of_y, of_core in quarters])
    half_at = [numbers(x, is_home), numbers(1 - x, is_home)]
    keys_at = numbers(y, core, is_inside)

    def beside(mine):
        return [mine, send(mine, X), send(mine, Z1), send(mine, XZ1)]

    def rest(rows, weights, given_across, given, kept_across, kept):
        across = add_up(kept_across, send(given_across[:rows], CORE))
        arrived = send(across, Y)
        keys = keys_of(kept, send(given[:rows], CORE), arrived)
        far = [send(keys, FAR)]
        swapped = send(keys, CORE)
        keys, swapped = lax.optimization_barrier((keys, swapped))
        far.append(send(keys, FAR_Y))
        near = [keys, send(keys, Y)]
        near += [swapped, send(near[1], CORE)]
        far += [send(k, CORE) for k in far]
        columns, panel = assemble(keys_at, weights, near, far)
        shared = send(panel, SHARE)
        cut = units * 6 // 8
        last = [send(shared[:, :cut], AWAY_X), send(shared[:, cut:], HOME_Z1)]
        out = covariance_part(half_at[0], weights, columns, panel, [shared], 2 * units, None)
        return covariance_part(half_at[1], weights, columns, shared, last, 2 * units, out)

    own = pack(hidden_states, expert_ids, route_gates)
    far = send(own, Z2)
    far, gate_weight, up_weight = lax.optimization_barrier((far, gate_weight, up_weight))
    gate_weight, up_weight = load(gate_weight, up_weight)
    blocks = beside(own) + beside(far)
    rows, weights, count = gather(numbers(dp), blocks)
    parts = project(project_at, rows, gate_weight, up_weight)
    sizes = [r for r in SIZES if r < rows.shape[0]] + [rows.shape[0]]
    branch = sum((count[0] > r).astype(jnp.int32) for r in sizes[:-1])
    return lax.switch(
        branch, [functools.partial(rest, r) for r in sizes], weights, *parts
    )


def solution(mesh):
    placed = (P("dp", "tensor"), P("dp", None), P("dp", None), P("tensor", "dp"), P("tensor", "dp"))
    sizes = (mesh.shape["dp"], mesh.shape["tensor"])
    return jax.shard_map(
        fast if sizes == (8, 4) else any_mesh,
        mesh=mesh,
        in_specs=placed,
        out_specs=P("tensor", "dp"),
        check_vma=False,
    )
```

time: 209 us -> 94.4 us (0.45)
  the two profiles are of different devices: /device:TPU:12 before, /device:TPU:0 now
where the time goes in v3:
time: 94.4 us; the launch traced here: 94.1 us
  starting transfers between devices  32.9 us (35%)
  waiting for transfers between devices  28.6 us (30%)
  Pallas kernels  21.5 us (23%)
  local copies, waits for them, and re-layouts  8.1 us (9%)
  between operations  2.12 us (2%)
    ppermute x20, starting transfers between devices, send(): return lax.ppermute(value, AXES, route)  32.9 us
    ppermute x20, waiting for transfers between devices, send(): return lax.ppermute(value, AXES, route)  28.6 us
    pallas_call x2, Pallas kernels, covariance_part(): pl.pallas_call(covariance_kernel, in_specs=in_specs, out_specs=pl.BlockSp...  13.8 us
    unnamed x10, local copies, waits for them, and re-layouts  7.92 us
    pallas_call x1, Pallas kernels, project(): pl.pallas_call(project_kernel, in_specs=[SM, VM, VM, VM], out_specs=[VM]...  4.17 us
  transfers between devices with their start and end apart: 20, of which 7 were waited for; matrix products, arithmetic and copies ran while one was open for 0% of the time, Pallas kernels for 8%

profile of v3, /device:TPU:0, one launch (start us, length us, event | category | flops | bytes accessed | tf_op | source)
XLA Modules:
  0.0 94.1 jit_solution(15273519731116464082)
XLA Ops:
  0.0 1.0 %copy-done.2 = bf16[128,1536]{1,0:T(8,128)(2,1)S(1)} copy-done((bf16[128,1536]{1,0:T(8,128)(2,1)S(1)}, bf16[128,1536]{1,0:T(8,128)(2,1)}, u32[]{:S(2)}) %copy-start.2) | copy-done | bytes 393240
  1.0 0.7 copy-done.3
  1.7 0.7 copy-done.4
  2.7 4.1 %collective-permute-start.55 = (bf16[32,1664]{1,0:T(8,128)(2,1)S(1)}, bf16[32,1664]{1,0:T(8,128)(2,1)S(1)}, u32[]{:S(2)}, u32[]{:S(2)}) collective-permute-start(bf16[32,1664]{1,0:T(8,128)(2,1)S(1)} %shard_map.59.refs_0_), channel_id=1, source_target_pairs={{0,16},{1,17},{2,18},{3,19},{4,20},{5,21},{6,22},{7,23},{8,24},{9,... | collective-permute-start | bytes 319496 | tf_op jit(solution)/shard_map/ppermute | solution.py:91
  6.8 2.5 %collective-permute-start.54 = (bf16[32,1664]{1,0:T(8,128)(2,1)S(1)}, bf16[32,1664]{1,0:T(8,128)(2,1)S(1)}, u32[]{:S(2)}, u32[]{:S(2)}) collective-permute-start(bf16[32,1664]{1,0:T(8,128)(2,1)S(1)} %shard_map.59.refs_0_), channel_id=1, source_target_pairs={{0,12},{1,13},{2,14},{3,15},{4,8},{5,9},{6,10},{7,11},{8,4},{9,5},... | collective-permute-start | bytes 319496 | tf_op jit(solution)/shard_map/ppermute | solution.py:91
  9.7 0.5 collective-permute-start.52
  10.4 1.7 %collective-permute-done.55.refs_4_ = bf16[32,1664]{1,0:T(8,128)(2,1)S(1)} collective-permute-done((bf16[32,1664]{1,0:T(8,128)(2,1)S(1)}, bf16[32,1664]{1,0:T(8,128)(2,1)S(1)}, u32[]{:S(2)}, u32[]{:S(2)}) %collective-permute-start.55) | collective-permute-done | bytes 106528 | tf_op jit(solution)/shard_map/ppermute | solution.py:91
  12.1 1.6 %collective-permute-start.58 = (bf16[32,1664]{1,0:T(8,128)(2,1)S(1)}, bf16[32,1664]{1,0:T(8,128)(2,1)S(1)}, u32[]{:S(2)}, u32[]{:S(2)}) collective-permute-start(bf16[32,1664]{1,0:T(8,128)(2,1)S(1)} %collective-permute-done.55.refs_4_), channel_id=1, source_target_pairs={{0,12},{1,13},{2,14},{3,15},{4,8},{5,9},{6,10},{7,11},{8,4},{9,5},... | collective-permute-start | bytes 319496 | tf_op jit(solution)/shard_map/ppermute | solution.py:91
  13.7 1.4 %collective-permute-start.57 = (bf16[32,1664]{1,0:T(8,128)(2,1)S(1)}, bf16[32,1664]{1,0:T(8,128)(2,1)S(1)}, u32[]{:S(2)}, u32[]{:S(2)}) collective-permute-start(bf16[32,1664]{1,0:T(8,128)(2,1)S(1)} %collective-permute-done.55.refs_4_), channel_id=1, source_target_pairs={{0,8},{1,9},{2,10},{3,11},{4,12},{5,13},{6,14},{7,15},{8,0},{9,1},... | collective-permute-start | bytes 319496 | tf_op jit(solution)/shard_map/ppermute | solution.py:91
  15.7 2.8 %copy-done = bf16[1536,2048]{1,0:T(8,128)(2,1)S(1)} copy-done((bf16[1536,2048]{1,0:T(8,128)(2,1)S(1)}, bf16[1536,2048]{1,0:T(8,128)(2,1)}, u32[]{:S(2)}) %copy-start) | copy-done | bytes 6291480
  18.5 2.8 %copy-done.1 = bf16[1536,2048]{1,0:T(8,128)(2,1)S(1)} copy-done((bf16[1536,2048]{1,0:T(8,128)(2,1)S(1)}, bf16[1536,2048]{1,0:T(8,128)(2,1)}, u32[]{:S(2)}) %copy-start.1) | copy-done | bytes 6291480
  21.3 0.9 shard_map.61
  22.2 1.2 %shard_map.60 = (bf16[256,1536]{1,0:T(8,128)(2,1)S(1)}, bf16[256,128]{1,0:T(8,128)(2,1)S(1)}, s32[1]{0:T(128)}) custom-call(s32[1]{0:T(128)} %bitcast.at_ref, bf16[32,1664]{1,0:T(8,128)(2,1)S(1)} %shard_map.59.refs_0_, bf16[32,1664]{1,0:T(8,128)(2,1)S(1)} %collective-permute-done.52.refs_1_, bf16[32,1664]{1,0:T(8,128)(2,1)S(1)} %collective-permute-done.53.refs_2_, ...), custom_call_target="tpu_custom_call" | custom-call | flops 268435456 | bytes 1048576 | tf_op jit(solution)/shard_map/pallas_call | solution.py:185
  25.2 4.2 %shard_map.62 = (f32[256,1024]{1,0:T(8,128)S(1)}, f32[256,1024]{1,0:T(8,128)S(1)}, f32[256,1024]{1,0:T(8,128)S(1)}, f32[256,1024]{1,0:T(8,128)S(1)}) custom-call(s32[4]{0:T(128)S(1)} %pad_add_fusion.at_ref, bf16[256,1536]{1,0:T(8,128)(2,1)S(1)} %get-tuple-element.136.rows_ref, bf16[1536,2048]{1,0:T(8,128)(2,1)S(1)} %get-tuple-element.139.gate_ref, ...), custom_call_target="tpu_custom_call" | custom-call | flops 3221225472 | bytes 1048576 | tf_op jit(solution)/shard_map/pallas_call | solution.py:211
  29.3 64.5 %conditional.1 = (f32[4096,2048]{1,0:T(8,128)}) conditional(s32[]{:T(128)} %bitcast.3, (f32[256,1024]{1,0:T(8,128)S(1)}, f32[256,1024]{1,0:T(8,128)S(1)}, f32[256,1024]{1,0:T(8,128)S(1)}, f32[256,1024]{1,0:T(8,128)S(1)}, s32[3]{0:T(128)S(1)}, /*index=5*/bf16[256,128]{1,0:T(8,128)(2,1)S(1)}, s32[2]{0:T(128)S(1)}, ...), branch_computations={%region_0.1_spmd, %region_1.2_spmd, %region_2.3_spmd, %region_3.4_... | conditional | flops 4295753728 | bytes 65143312 | solution.py:389
  29.6 0.6 collective-permute-start.13
  30.1 1.7 %collective-permute-done.14.got_ref = f32[192,1024]{1,0:T(8,128)S(1)} collective-permute-done((f32[192,1024]{1,0:T(8,128)S(1)}, f32[192,1024]{1,0:T(8,128)S(1)}, u32[]{:S(2)}, u32[]{:S(2)}) %collective-permute-start.14) | collective-permute-done | bytes 786464 | tf_op jit(solution)/shard_map/cond/branch_1_fun/ppermute | solution.py:91
  31.9 1.6 %collective-permute-start.15 = (bf16[192,1024]{1,0:T(8,128)(2,1)S(1)}, bf16[192,1024]{1,0:T(8,128)(2,1)S(1)}, u32[]{:S(2)}, u32[]{:S(2)}) collective-permute-start(bf16[192,1024]{1,0:T(8,128)(2,1)S(1)} %branch_1_fun.5), channel_id=1, source_target_pairs={{0,2},{1,3},{2,0},{3,1},{4,6},{5,7},{6,4},{7,5},{8,10},{9,11},{10,... | collective-permute-start | bytes 1179656 | tf_op jit(solution)/shard_map/cond/branch_1_fun/ppermute | solution.py:91
  33.6 9.6 %collective-permute-done.15.across_ref = bf16[192,1024]{1,0:T(8,128)(2,1)S(1)} collective-permute-done((bf16[192,1024]{1,0:T(8,128)(2,1)S(1)}, bf16[192,1024]{1,0:T(8,128)(2,1)S(1)}, u32[]{:S(2)}, u32[]{:S(2)}) %collective-permute-start.15) | collective-permute-done | bytes 393248 | tf_op jit(solution)/shard_map/cond/branch_1_fun/ppermute | solution.py:91
  43.4 4.0 %collective-permute-start.19 = (bf16[192,512]{1,0:T(8,128)(2,1)S(1)}, bf16[192,512]{1,0:T(8,128)(2,1)S(1)}, u32[]{:S(2)}, u32[]{:S(2)}) collective-permute-start(bf16[192,512]{1,0:T(8,128)(2,1)S(1)} %branch_1_fun.6.refs_0_), channel_id=1, source_target_pairs={{0,16},{1,17},{4,20},{5,21},{8,24},{9,25},{12,28},{13,29},{18,2},{... | collective-permute-start | bytes 589832 | tf_op jit(solution)/shard_map/cond/branch_1_fun/ppermute | solution.py:91
  47.4 0.9 collective-permute-start.20
  48.3 2.3 %collective-permute-start.17 = (bf16[192,512]{1,0:T(8,128)(2,1)S(1)}, bf16[192,512]{1,0:T(8,128)(2,1)S(1)}, u32[]{:S(2)}, u32[]{:S(2)}) collective-permute-start(bf16[192,512]{1,0:T(8,128)(2,1)S(1)} %branch_1_fun.6.refs_0_), channel_id=1, source_target_pairs={{0,2},{1,3},{2,0},{3,1},{4,6},{5,7},{6,4},{7,5},{8,10},{9,11},{10,... | collective-permute-start | bytes 589832 | tf_op jit(solution)/shard_map/cond/branch_1_fun/ppermute | solution.py:91
  50.6 1.7 %collective-permute-done.19.refs_4_ = bf16[192,512]{1,0:T(8,128)(2,1)S(1)} collective-permute-done((bf16[192,512]{1,0:T(8,128)(2,1)S(1)}, bf16[192,512]{1,0:T(8,128)(2,1)S(1)}, u32[]{:S(2)}, u32[]{:S(2)}) %collective-permute-start.19) | collective-permute-done | bytes 196640 | tf_op jit(solution)/shard_map/cond/branch_1_fun/ppermute | solution.py:91
  52.8 2.9 %collective-permute-done.17.refs_1_ = bf16[192,512]{1,0:T(8,128)(2,1)S(1)} collective-permute-done((bf16[192,512]{1,0:T(8,128)(2,1)S(1)}, bf16[192,512]{1,0:T(8,128)(2,1)S(1)}, u32[]{:S(2)}, u32[]{:S(2)}) %collective-permute-start.17) | collective-permute-done | bytes 196640 | tf_op jit(solution)/shard_map/cond/branch_1_fun/ppermute | solution.py:91
  55.7 1.4 %collective-permute-done.18.refs_3_ = bf16[192,512]{1,0:T(8,128)(2,1)S(1)} collective-permute-done((bf16[192,512]{1,0:T(8,128)(2,1)S(1)}, bf16[192,512]{1,0:T(8,128)(2,1)S(1)}, u32[]{:S(2)}, u32[]{:S(2)}) %collective-permute-start.18) | collective-permute-done | bytes 196640 | tf_op jit(solution)/shard_map/cond/branch_1_fun/ppermute | solution.py:91
  57.2 0.8 branch_1_fun.7
  58.0 4.2 %collective-permute-start.23 = (bf16[192,2048]{1,0:T(8,128)(2,1)S(1)}, bf16[192,2048]{1,0:T(8,128)(2,1)S(1)}, u32[]{:S(2)}, u32[]{:S(2)}) collective-permute-start(bf16[192,2048]{1,0:T(8,128)(2,1)S(1)} %get-tuple-element.96.mine_ref), channel_id=1, source_target_pairs={{0,8},{1,4},{2,10},{3,6},{4,12},{5,0},{6,14},{7,2},{8,13},{9,1},{1... | collective-permute-start | bytes 2359304 | tf_op jit(solution)/shard_map/cond/branch_1_fun/ppermute | solution.py:91
  62.2 9.5 %collective-permute-done.23.refs_0_.refs_1_.mine_ref = bf16[192,2048]{1,0:T(8,128)(2,1)S(1)} collective-permute-done((bf16[192,2048]{1,0:T(8,128)(2,1)S(1)}, bf16[192,2048]{1,0:T(8,128)(2,1)S(1)}, u32[]{:S(2)}, u32[]{:S(2)}) %collective-permute-start.23) | collective-permute-done | bytes 786464 | tf_op jit(solution)/shard_map/cond/branch_1_fun/ppermute | solution.py:91
  71.7 0.7 collective-permute-start.24
  72.5 7.0 %collective-permute-start.25 = (bf16[192,512]{1,0:T(8,128)(2,1)S(1)}, bf16[192,512]{1,0:T(8,128)(2,1)S(1)}, u32[]{:S(2)}, u32[]{:S(2)}) collective-permute-start(bf16[192,512]{1,0:T(8,128)(2,1)S(1)} %slice.45), channel_id=1, source_target_pairs={{0,8},{2,10},{4,12},{6,14},{9,1},{11,3},{13,5},{15,7},{16,24},{18,... | collective-permute-start | bytes 589832 | tf_op jit(solution)/shard_map/cond/branch_1_fun/ppermute | solution.py:91
  79.4 6.9 %branch_1_fun.8.refs_2_ = f32[4096,2048]{1,0:T(8,128)} custom-call(s32[2]{0:T(128)S(1)} %get-tuple-element.97.at_ref, bf16[256,128]{1,0:T(8,128)(2,1)S(1)} %get-tuple-element.87.weights_ref, bf16[192,2048]{1,0:T(8,128)(2,1)S(1)} %get-tuple-element.95.columns_ref, bf16[192,2048]{1,0:T(8,128)(2,1)S(1)} %get-tuple-element.96.mine_ref, ...), custom_call_target="tpu_custom_call" | custom-call | flops 1610612736 | bytes 16777216 | tf_op jit(solution)/shard_map/cond/branch_1_fun/pallas_call | solution.py:330
  86.4 6.9 %branch_1_fun.9 = f32[4096,2048]{1,0:T(8,128)} custom-call(s32[2]{0:T(128)S(1)} %get-tuple-element.86.at_ref, bf16[256,128]{1,0:T(8,128)(2,1)S(1)} %get-tuple-element.87.weights_ref, bf16[192,2048]{1,0:T(8,128)(2,1)S(1)} %get-tuple-element.95.columns_ref, ...), custom_call_target="tpu_custom_call", output_to_operand_aliasing={{}: (6, {})} | custom-call | flops 1610612736 | bytes 16777216 | tf_op jit(solution)/shard_map/cond/branch_1_fun/pallas_call | solution.py:330
  (35 shorter events, 2.6 us)
Async XLA Ops:
  0.0 1.0 %copy-start.2 = (bf16[128,1536]{1,0:T(8,128)(2,1)S(1)}, bf16[128,1536]{1,0:T(8,128)(2,1)}, u32[]{:S(2)}) copy-start(bf16[128,1536]{1,0:T(8,128)(2,1)} %tokens_ref.1) | copy-start | bytes 1179652
  1.0 0.7 copy-start.3
  1.7 0.7 copy-start.4
  2.7 9.4 %collective-permute-start.55 = (bf16[32,1664]{1,0:T(8,128)(2,1)S(1)}, bf16[32,1664]{1,0:T(8,128)(2,1)S(1)}, u32[]{:S(2)}, u32[]{:S(2)}) collective-permute-start(bf16[32,1664]{1,0:T(8,128)(2,1)S(1)} %shard_map.59.refs_0_), channel_id=1, source_target_pairs={{0,16},{1,17},{2,18},{3,19},{4,20},{5,21},{6,22},{7,23},{8,24},{9,... | collective-permute-start | bytes 319496 | tf_op jit(solution)/shard_map/ppermute | solution.py:91
  6.8 8.4 %collective-permute-start.54 = (bf16[32,1664]{1,0:T(8,128)(2,1)S(1)}, bf16[32,1664]{1,0:T(8,128)(2,1)S(1)}, u32[]{:S(2)}, u32[]{:S(2)}) collective-permute-start(bf16[32,1664]{1,0:T(8,128)(2,1)S(1)} %shard_map.59.refs_0_), channel_id=1, source_target_pairs={{0,12},{1,13},{2,14},{3,15},{4,8},{5,9},{6,10},{7,11},{8,4},{9,5},... | collective-permute-start | bytes 319496 | tf_op jit(solution)/shard_map/ppermute | solution.py:91
  9.3 12.8 %collective-permute-start.53 = (bf16[32,1664]{1,0:T(8,128)(2,1)S(1)}, bf16[32,1664]{1,0:T(8,128)(2,1)S(1)}, u32[]{:S(2)}, u32[]{:S(2)}) collective-permute-start(bf16[32,1664]{1,0:T(8,128)(2,1)S(1)} %shard_map.59.refs_0_), channel_id=1, source_target_pairs={{0,8},{1,9},{2,10},{3,11},{4,12},{5,13},{6,14},{7,15},{8,0},{9,1},... | collective-permute-start | bytes 319496 | tf_op jit(solution)/shard_map/ppermute | solution.py:91
  9.7 12.4 %collective-permute-start.52 = (bf16[32,1664]{1,0:T(8,128)(2,1)S(1)}, bf16[32,1664]{1,0:T(8,128)(2,1)S(1)}, u32[]{:S(2)}, u32[]{:S(2)}) collective-permute-start(bf16[32,1664]{1,0:T(8,128)(2,1)S(1)} %shard_map.59.refs_0_), channel_id=1, source_target_pairs={{0,4},{1,5},{2,6},{3,7},{4,0},{5,1},{6,2},{7,3},{8,12},{9,13},{10,... | collective-permute-start | bytes 319496 | tf_op jit(solution)/shard_map/ppermute | solution.py:91
  12.1 10.0 %collective-permute-start.58 = (bf16[32,1664]{1,0:T(8,128)(2,1)S(1)}, bf16[32,1664]{1,0:T(8,128)(2,1)S(1)}, u32[]{:S(2)}, u32[]{:S(2)}) collective-permute-start(bf16[32,1664]{1,0:T(8,128)(2,1)S(1)} %collective-permute-done.55.refs_4_), channel_id=1, source_target_pairs={{0,12},{1,13},{2,14},{3,15},{4,8},{5,9},{6,10},{7,11},{8,4},{9,5},... | collective-permute-start | bytes 319496 | tf_op jit(solution)/shard_map/ppermute | solution.py:91
  13.7 8.4 %collective-permute-start.57 = (bf16[32,1664]{1,0:T(8,128)(2,1)S(1)}, bf16[32,1664]{1,0:T(8,128)(2,1)S(1)}, u32[]{:S(2)}, u32[]{:S(2)}) collective-permute-start(bf16[32,1664]{1,0:T(8,128)(2,1)S(1)} %collective-permute-done.55.refs_4_), channel_id=1, source_target_pairs={{0,8},{1,9},{2,10},{3,11},{4,12},{5,13},{6,14},{7,15},{8,0},{9,1},... | collective-permute-start | bytes 319496 | tf_op jit(solution)/shard_map/ppermute | solution.py:91
  15.1 7.0 %collective-permute-start.56 = (bf16[32,1664]{1,0:T(8,128)(2,1)S(1)}, bf16[32,1664]{1,0:T(8,128)(2,1)S(1)}, u32[]{:S(2)}, u32[]{:S(2)}) collective-permute-start(bf16[32,1664]{1,0:T(8,128)(2,1)S(1)} %collective-permute-done.55.refs_4_), channel_id=1, source_target_pairs={{0,4},{1,5},{2,6},{3,7},{4,0},{5,1},{6,2},{7,3},{8,12},{9,13},{10,... | collective-permute-start | bytes 319496 | tf_op jit(solution)/shard_map/ppermute | solution.py:91
  15.7 2.8 %copy-start = (bf16[1536,2048]{1,0:T(8,128)(2,1)S(1)}, bf16[1536,2048]{1,0:T(8,128)(2,1)}, u32[]{:S(2)}) copy-start(bf16[1536,2048]{1,0:T(8,128)(2,1)} %gate_in) | copy-start | bytes 18874372
  18.5 2.8 %copy-start.1 = (bf16[1536,2048]{1,0:T(8,128)(2,1)S(1)}, bf16[1536,2048]{1,0:T(8,128)(2,1)}, u32[]{:S(2)}) copy-start(bf16[1536,2048]{1,0:T(8,128)(2,1)} %up_in) | copy-start | bytes 18874372
  29.4 2.4 %collective-permute-start.14 = (f32[192,1024]{1,0:T(8,128)S(1)}, f32[192,1024]{1,0:T(8,128)S(1)}, u32[]{:S(2)}, u32[]{:S(2)}) collective-permute-start(f32[192,1024]{1,0:T(8,128)S(1)} %slice.33), channel_id=1, source_target_pairs={{0,1},{1,0},{2,3},{3,2},{4,5},{5,4},{6,7},{7,6},{8,9},{9,8},{10,11... | collective-permute-start | bytes 2359304 | tf_op jit(solution)/shard_map/cond/branch_1_fun/ppermute | solution.py:91
  29.6 4.0 %collective-permute-start.13 = (f32[192,1024]{1,0:T(8,128)S(1)}, f32[192,1024]{1,0:T(8,128)S(1)}, u32[]{:S(2)}, u32[]{:S(2)}) collective-permute-start(f32[192,1024]{1,0:T(8,128)S(1)} %slice.32), channel_id=1, source_target_pairs={{0,1},{1,0},{2,3},{3,2},{4,5},{5,4},{6,7},{7,6},{8,9},{9,8},{10,11... | collective-permute-start | bytes 2359304 | tf_op jit(solution)/shard_map/cond/branch_1_fun/ppermute | solution.py:91
  31.9 11.2 %collective-permute-start.15 = (bf16[192,1024]{1,0:T(8,128)(2,1)S(1)}, bf16[192,1024]{1,0:T(8,128)(2,1)S(1)}, u32[]{:S(2)}, u32[]{:S(2)}) collective-permute-start(bf16[192,1024]{1,0:T(8,128)(2,1)S(1)} %branch_1_fun.5), channel_id=1, source_target_pairs={{0,2},{1,3},{2,0},{3,1},{4,6},{5,7},{6,4},{7,5},{8,10},{9,11},{10,... | collective-permute-start | bytes 1179656 | tf_op jit(solution)/shard_map/cond/branch_1_fun/ppermute | solution.py:91
  43.3 4.1 %collective-permute-start.16 = (bf16[192,512]{1,0:T(8,128)(2,1)S(1)}, bf16[192,512]{1,0:T(8,128)(2,1)S(1)}, u32[]{:S(2)}, u32[]{:S(2)}) collective-permute-start(bf16[192,512]{1,0:T(8,128)(2,1)S(1)} %branch_1_fun.6.refs_0_), channel_id=1, source_target_pairs={{0,1},{1,0},{2,3},{3,2},{4,5},{5,4},{6,7},{7,6},{8,9},{9,8},{10,11... | collective-permute-start | bytes 589832 | tf_op jit(solution)/shard_map/cond/branch_1_fun/ppermute | solution.py:91
  43.4 8.9 %collective-permute-start.19 = (bf16[192,512]{1,0:T(8,128)(2,1)S(1)}, bf16[192,512]{1,0:T(8,128)(2,1)S(1)}, u32[]{:S(2)}, u32[]{:S(2)}) collective-permute-start(bf16[192,512]{1,0:T(8,128)(2,1)S(1)} %branch_1_fun.6.refs_0_), channel_id=1, source_target_pairs={{0,16},{1,17},{4,20},{5,21},{8,24},{9,25},{12,28},{13,29},{18,2},{... | collective-permute-start | bytes 589832 | tf_op jit(solution)/shard_map/cond/branch_1_fun/ppermute | solution.py:91
  47.4 4.8 %collective-permute-start.20 = (bf16[192,512]{1,0:T(8,128)(2,1)S(1)}, bf16[192,512]{1,0:T(8,128)(2,1)S(1)}, u32[]{:S(2)}, u32[]{:S(2)}) collective-permute-start(bf16[192,512]{1,0:T(8,128)(2,1)S(1)} %branch_1_fun.6.refs_0_), channel_id=1, source_target_pairs={{2,16},{3,17},{6,20},{7,21},{10,24},{11,25},{14,28},{15,29},{16,2}... | collective-permute-start | bytes 589832 | tf_op jit(solution)/shard_map/cond/branch_1_fun/ppermute | solution.py:91
  48.3 7.4 %collective-permute-start.17 = (bf16[192,512]{1,0:T(8,128)(2,1)S(1)}, bf16[192,512]{1,0:T(8,128)(2,1)S(1)}, u32[]{:S(2)}, u32[]{:S(2)}) collective-permute-start(bf16[192,512]{1,0:T(8,128)(2,1)S(1)} %branch_1_fun.6.refs_0_), channel_id=1, source_target_pairs={{0,2},{1,3},{2,0},{3,1},{4,6},{5,7},{6,4},{7,5},{8,10},{9,11},{10,... | collective-permute-start | bytes 589832 | tf_op jit(solution)/shard_map/cond/branch_1_fun/ppermute | solution.py:91
  52.3 3.5 %collective-permute-start.21 = (bf16[192,512]{1,0:T(8,128)(2,1)S(1)}, bf16[192,512]{1,0:T(8,128)(2,1)S(1)}, u32[]{:S(2)}, u32[]{:S(2)}) collective-permute-start(bf16[192,512]{1,0:T(8,128)(2,1)S(1)} %collective-permute-done.19.refs_4_), channel_id=1, source_target_pairs={{0,1},{1,0},{2,3},{3,2},{4,5},{5,4},{6,7},{7,6},{8,9},{9,8},{10,11... | collective-permute-start | bytes 589832 | tf_op jit(solution)/shard_map/cond/branch_1_fun/ppermute | solution.py:91
  52.3 3.5 %collective-permute-start.22 = (bf16[192,512]{1,0:T(8,128)(2,1)S(1)}, bf16[192,512]{1,0:T(8,128)(2,1)S(1)}, u32[]{:S(2)}, u32[]{:S(2)}) collective-permute-start(bf16[192,512]{1,0:T(8,128)(2,1)S(1)} %collective-permute-done.20.refs_5_), channel_id=1, source_target_pairs={{0,1},{1,0},{2,3},{3,2},{4,5},{5,4},{6,7},{7,6},{8,9},{9,8},{10,11... | collective-permute-start | bytes 589832 | tf_op jit(solution)/shard_map/cond/branch_1_fun/ppermute | solution.py:91
  55.7 1.4 %collective-permute-start.18 = (bf16[192,512]{1,0:T(8,128)(2,1)S(1)}, bf16[192,512]{1,0:T(8,128)(2,1)S(1)}, u32[]{:S(2)}, u32[]{:S(2)}) collective-permute-start(bf16[192,512]{1,0:T(8,128)(2,1)S(1)} %collective-permute-done.17.refs_1_), channel_id=1, source_target_pairs={{0,1},{1,0},{2,3},{3,2},{4,5},{5,4},{6,7},{7,6},{8,9},{9,8},{10,11... | collective-permute-start | bytes 589832 | tf_op jit(solution)/shard_map/cond/branch_1_fun/ppermute | solution.py:91
  58.0 13.7 %collective-permute-start.23 = (bf16[192,2048]{1,0:T(8,128)(2,1)S(1)}, bf16[192,2048]{1,0:T(8,128)(2,1)S(1)}, u32[]{:S(2)}, u32[]{:S(2)}) collective-permute-start(bf16[192,2048]{1,0:T(8,128)(2,1)S(1)} %get-tuple-element.96.mine_ref), channel_id=1, source_target_pairs={{0,8},{1,4},{2,10},{3,6},{4,12},{5,0},{6,14},{7,2},{8,13},{9,1},{1... | collective-permute-start | bytes 2359304 | tf_op jit(solution)/shard_map/cond/branch_1_fun/ppermute | solution.py:91
  71.7 14.6 %collective-permute-start.24 = (bf16[192,1536]{1,0:T(8,128)(2,1)S(1)}, bf16[192,1536]{1,0:T(8,128)(2,1)S(1)}, u32[]{:S(2)}, u32[]{:S(2)}) collective-permute-start(bf16[192,1536]{1,0:T(8,128)(2,1)S(1)} %slice.44), channel_id=1, source_target_pairs={{1,5},{3,7},{5,1},{7,3},{8,12},{10,14},{12,8},{14,10},{17,21},{19,... | collective-permute-start | bytes 1769480 | tf_op jit(solution)/shard_map/cond/branch_1_fun/ppermute | solution.py:91
  72.5 13.9 %collective-permute-start.25 = (bf16[192,512]{1,0:T(8,128)(2,1)S(1)}, bf16[192,512]{1,0:T(8,128)(2,1)S(1)}, u32[]{:S(2)}, u32[]{:S(2)}) collective-permute-start(bf16[192,512]{1,0:T(8,128)(2,1)S(1)} %slice.45), channel_id=1, source_target_pairs={{0,8},{2,10},{4,12},{6,14},{9,1},{11,3},{13,5},{15,7},{16,24},{18,... | collective-permute-start | bytes 589832 | tf_op jit(solution)/shard_map/cond/branch_1_fun/ppermute | solution.py:91

commit v4 on v3

--- a/solution.py
+++ b/solution.py
@@ -80,8 +80,7 @@
 FAR = pairs(lambda z, x, y, c: (z ^ 2, x, y, c) if inside(z, y) else None)
 FAR_Y = pairs(lambda z, x, y, c: (z ^ 2, x, 1 - y, c) if not inside(z, y) else None)
 SHARE = pairs(lambda z, x, y, c: (z ^ 1, x, y, c) if c == z % 2 else (z, 1 - x, y, 1 - c))
-HOME_Z1 = pairs(lambda z, x, y, c: (z ^ 1, x, y, c) if c == z % 2 else None)
-AWAY_X = pairs(lambda z, x, y, c: (z, 1 - x, y, c) if c != z % 2 else None)
+CROSS = pairs(lambda z, x, y, c: (z ^ 1, 1 - x, y, c) if c == z % 2 else None)
 
 VM = pl.BlockSpec(memory_space=pltpu.VMEM)
 SM = pl.BlockSpec(memory_space=pltpu.SMEM)
@@ -131,7 +130,6 @@
     return pl.pallas_call(
         pack_kernel,
         out_shape=shaped(CAP, hidden_states.shape[1] + LANES, BF),
-        compiler_params=limit(4),
     )(expert_ids.T, route_gates.T, hidden_states)
 
 
@@ -159,15 +157,16 @@
     )(gate_weight, up_weight)
 
 
-def gather_kernel(at_ref, *refs):
-    blocks, (rows_ref, weights_ref, count_ref, all_ref) = refs[:8], refs[8:]
+def gather_kernel(sizes, at_ref, *refs):
+    blocks, (rows_ref, weights_ref, branch_ref, all_ref) = refs[:8], refs[8:]
     total, depth = rows_ref.shape
     for k, block in enumerate(blocks):
         start = pl.multiple_of((at_ref[0] ^ k) * CAP, CAP)
         all_ref[pl.ds(start, CAP), :] = block[...]
     weights = all_ref[:, depth:]
     member = jnp.where(weights.astype(F32) > 0, 1.0, 0.0)
-    count_ref[0] = jnp.sum(member[:, :1]).astype(jnp.int32)
+    count = jnp.sum(member[:, :1])
+    branch_ref[0] = sum((count > size).astype(jnp.int32) for size in sizes[:-1])
     member = member.astype(BF)
     position = lax.dot_general(member, before(total), ROWS_OF, preferred_element_type=F32)[:1]
     down = lax.broadcasted_iota(jnp.int32, (total, total), 0)
@@ -180,10 +179,10 @@
     weights_ref[...] = jnp.dot(picked, weights, preferred_element_type=F32).astype(BF)
 
 
-def gather(at, blocks):
+def gather(at, blocks, sizes):
     rows, width = 8 * CAP, blocks[0].shape[1]
     return pl.pallas_call(
-        gather_kernel,
+        functools.partial(gather_kernel, sizes),
         in_specs=[SM] + [VM] * 8,
         out_specs=[VM, VM, SM],
         out_shape=[
@@ -278,55 +277,58 @@
     )(at, weights, *near, *far)
 
 
-SIZES = (160, 192, 224)
+SIZES = (128, 144, 160, 176, 192, 208, 224)
 TILE = 256
 BUFFERS = 4
 
 
-def covariance_kernel(at_ref, weights_ref, columns_ref, mine_ref, *refs):
-    theirs, (out_ref, buffer_ref, sems) = refs[:2], refs[-3:]
-    is_home = at_ref[1] == 1
-    rows, units = mine_ref.shape
-    total = jnp.sum(weights_ref[:, :1].astype(F32), axis=0, keepdims=True)
-    scale = 1.0 / total
+def covariance_kernel(at_ref, weights_ref, columns_ref, panel_ref, *refs):
+    out_ref, buffer_ref, sems = refs[-3:]
+    units = panel_ref.shape[1]
     steps = units // TILE
 
     def copy(i):
         start = pl.multiple_of(at_ref[0] * units + i * TILE, TILE)
-        slot = i % BUFFERS
+        slot = lax.rem(i, BUFFERS)
         return pltpu.make_async_copy(
             buffer_ref.at[slot], out_ref.at[pl.ds(start, TILE)], sems.at[slot]
         )
 
-    for i in range(steps):
-        at = i * TILE
-        their_ref = theirs[0]
-        part = slice(at, at + TILE)
-        if at >= theirs[0].shape[1]:
-            their_ref = theirs[1]
-            part = slice(at - theirs[0].shape[1], at - theirs[0].shape[1] + TILE)
-        panel = jnp.where(is_home, mine_ref[:, at : at + TILE], their_ref[:, part])
-        if i >= BUFFERS:
-            copy(i - BUFFERS).wait()
-        value = lax.dot_general(panel, columns_ref[...], ROWS_OF, preferred_element_type=F32)
-        buffer_ref[i % BUFFERS] = value * scale
-        copy(i).start()
-    for i in range(steps - BUFFERS, steps):
-        copy(i).wait()
-
-
-def covariance_part(at, weights, columns, mine, theirs, out_rows, into):
-    rows, units = mine.shape
+    @pl.when(at_ref[1] == 1)
+    def _():
+        total = jnp.sum(weights_ref[:, :1].astype(F32), axis=0, keepdims=True)
+        scale = 1.0 / total
+
+        def step(i, carry):
+            @pl.when(i >= BUFFERS)
+            def _():
+                copy(i - BUFFERS).wait()
+
+            part = panel_ref[:, pl.ds(pl.multiple_of(i * TILE, TILE), TILE)]
+            value = lax.dot_general(part, columns_ref[...], ROWS_OF, preferred_element_type=F32)
+            buffer_ref[lax.rem(i, BUFFERS)] = value * scale
+            copy(i).start()
+            return carry
+
+        lax.fori_loop(0, steps, step, 0)
+
+        def finish(i, carry):
+            copy(i).wait()
+            return carry
+
+        lax.fori_loop(steps - BUFFERS, steps, finish, 0)
+
+
+def covariance_part(at, weights, columns, panel, out_rows, into):
+    rows, units = panel.shape
     width = columns.shape[1]
-    if len(theirs) == 1:
-        theirs = theirs * 2
-    args = [at, weights, columns, mine, *theirs]
-    in_specs = [SM] + [VM] * 5
+    args = [at, weights, columns, panel]
+    in_specs = [SM, VM, VM, VM]
     aliases = {}
     if into is not None:
         args.append(into)
         in_specs.append(pl.BlockSpec(memory_space=pl.ANY))
-        aliases = {6: 0}
+        aliases = {4: 0}
     return pl.pallas_call(
         covariance_kernel,
         in_specs=in_specs,
@@ -353,7 +355,9 @@
     is_home, is_inside = core == z % 2, y == z // 2
     quarters = [(1 - y, 1 - core), (y, 1 - core), (1 - y, core), (y, core)]
     project_at = numbers(*[of_y * 2 + of_core for of_y, of_core in quarters])
-    half_at = [numbers(x, is_home), numbers(1 - x, is_home)]
+    mine_at = numbers(x, is_home)
+    shared_at = numbers(jnp.where(is_home, 1 - x, x), 1)
+    last_at = numbers(1 - x, core != z % 2)
     keys_at = numbers(y, core, is_inside)
 
     def beside(mine):
@@ -372,22 +376,21 @@
         far += [send(k, CORE) for k in far]
         columns, panel = assemble(keys_at, weights, near, far)
         shared = send(panel, SHARE)
-        cut = units * 6 // 8
-        last = [send(shared[:, :cut], AWAY_X), send(shared[:, cut:], HOME_Z1)]
-        out = covariance_part(half_at[0], weights, columns, panel, [shared], 2 * units, None)
-        return covariance_part(half_at[1], weights, columns, shared, last, 2 * units, out)
+        last = send(panel, CROSS)
+        out = covariance_part(mine_at, weights, columns, panel, 2 * units, None)
+        out = covariance_part(shared_at, weights, columns, shared, 2 * units, out)
+        return covariance_part(last_at, weights, columns, last, 2 * units, out)
 
     own = pack(hidden_states, expert_ids, route_gates)
     far = send(own, Z2)
     far, gate_weight, up_weight = lax.optimization_barrier((far, gate_weight, up_weight))
     gate_weight, up_weight = load(gate_weight, up_weight)
     blocks = beside(own) + beside(far)
-    rows, weights, count = gather(numbers(dp), blocks)
+    sizes = [size for size in SIZES if size < 8 * CAP] + [8 * CAP]
+    rows, weights, branch = gather(numbers(dp), blocks, sizes)
     parts = project(project_at, rows, gate_weight, up_weight)
-    sizes = [r for r in SIZES if r < rows.shape[0]] + [rows.shape[0]]
-    branch = sum((count[0] > r).astype(jnp.int32) for r in sizes[:-1])
     return lax.switch(
-        branch, [functools.partial(rest, r) for r in sizes], weights, *parts
+        branch[0], [functools.partial(rest, size) for size in sizes], weights, *parts
     )
 
 

time: 94.4 us -> 91.6 us (0.970)
  the two profiles are of different devices: /device:TPU:0 before, /device:TPU:12 now
where the time goes in v4:
time: 91.6 us; the launch traced here: 90.9 us
  waiting for transfers between devices  39 us (43%)
  Pallas kernels  23.7 us (26%)
  starting transfers between devices  20 us (22%)
  local copies, waits for them, and re-layouts  6.59 us (7%)
    ppermute x19, waiting for transfers between devices, send(): return lax.ppermute(value, AXES, route)  39 us
    ppermute x19, starting transfers between devices, send(): return lax.ppermute(value, AXES, route)  20 us
    pallas_call x3, Pallas kernels, covariance_part(): pl.pallas_call(covariance_kernel, in_specs=in_specs, out_specs=pl.BlockSp...  14.5 us
    unnamed x6, local copies, waits for them, and re-layouts  6.46 us
    pallas_call x1, Pallas kernels, project(): pl.pallas_call(project_kernel, in_specs=[SM, VM, VM, VM], out_specs=[VM]...  4.16 us
    pallas_call x1, Pallas kernels, pack(): pl.pallas_call(pack_kernel, out_shape=shaped(CAP, hidden_states.shape[1]...  1.99 us
  transfers between devices with their start and end apart: 19, of which 11 were waited for; matrix products, arithmetic and copies ran while one was open for 0% of the time, Pallas kernels for 9%

profile of v4, /device:TPU:12, one launch (start us, length us, event | category | flops | bytes accessed | tf_op | source)
XLA Modules:
  0.0 90.9 jit_solution(10034363175045575656)
XLA Ops:
  0.0 2.0 %shard_map.63.refs_0_ = bf16[32,1664]{1,0:T(8,128)(2,1)} custom-call(s32[2,128]{1,0:T(2,128)} %bitcast.16, f32[2,128]{1,0:T(2,128)} %bitcast.17, bf16[128,1536]{1,0:T(8,128)(2,1)} %tokens_ref.1), custom_call_target="tpu_custom_call" | custom-call | tf_op jit(solution)/shard_map/pallas_call | solution.py:130
  2.0 2.6 %collective-permute-start.99 = (bf16[32,1664]{1,0:T(8,128)(2,1)}, bf16[32,1664]{1,0:T(8,128)(2,1)S(1)}, u32[]{:S(2)}, u32[]{:S(2)}) collective-permute-start(bf16[32,1664]{1,0:T(8,128)(2,1)} %shard_map.63.refs_0_), channel_id=1, source_target_pairs={{0,16},{1,17},{2,18},{3,19},{4,20},{5,21},{6,22},{7,23},{8,24},{9,... | collective-permute-start | bytes 319496 | tf_op jit(solution)/shard_map/ppermute | solution.py:90
  4.6 1.4 %collective-permute-start.98 = (bf16[32,1664]{1,0:T(8,128)(2,1)}, bf16[32,1664]{1,0:T(8,128)(2,1)S(1)}, u32[]{:S(2)}, u32[]{:S(2)}) collective-permute-start(bf16[32,1664]{1,0:T(8,128)(2,1)} %shard_map.63.refs_0_), channel_id=1, source_target_pairs={{0,12},{1,13},{2,14},{3,15},{4,8},{5,9},{6,10},{7,11},{8,4},{9,5},... | collective-permute-start | bytes 319496 | tf_op jit(solution)/shard_map/ppermute | solution.py:90
  6.0 1.6 %collective-permute-start.97 = (bf16[32,1664]{1,0:T(8,128)(2,1)}, bf16[32,1664]{1,0:T(8,128)(2,1)S(1)}, u32[]{:S(2)}, u32[]{:S(2)}) collective-permute-start(bf16[32,1664]{1,0:T(8,128)(2,1)} %shard_map.63.refs_0_), channel_id=1, source_target_pairs={{0,8},{1,9},{2,10},{3,11},{4,12},{5,13},{6,14},{7,15},{8,0},{9,1},... | collective-permute-start | bytes 319496 | tf_op jit(solution)/shard_map/ppermute | solution.py:90
  8.3 1.0 %collective-permute-done.99.refs_4_ = bf16[32,1664]{1,0:T(8,128)(2,1)S(1)} collective-permute-done((bf16[32,1664]{1,0:T(8,128)(2,1)}, bf16[32,1664]{1,0:T(8,128)(2,1)S(1)}, u32[]{:S(2)}, u32[]{:S(2)}) %collective-permute-start.99) | collective-permute-done | bytes 106528 | tf_op jit(solution)/shard_map/ppermute | solution.py:90
  9.3 2.2 %collective-permute-start.102 = (bf16[32,1664]{1,0:T(8,128)(2,1)S(1)}, bf16[32,1664]{1,0:T(8,128)(2,1)S(1)}, u32[]{:S(2)}, u32[]{:S(2)}) collective-permute-start(bf16[32,1664]{1,0:T(8,128)(2,1)S(1)} %collective-permute-done.99.refs_4_), channel_id=1, source_target_pairs={{0,12},{1,13},{2,14},{3,15},{4,8},{5,9},{6,10},{7,11},{8,4},{9,5},... | collective-permute-start | bytes 319496 | tf_op jit(solution)/shard_map/ppermute | solution.py:90
  11.6 0.7 collective-permute-start.101
  12.3 0.6 collective-permute-start.100
  13.0 2.8 %copy-done = bf16[1536,2048]{1,0:T(8,128)(2,1)S(1)} copy-done((bf16[1536,2048]{1,0:T(8,128)(2,1)S(1)}, bf16[1536,2048]{1,0:T(8,128)(2,1)}, u32[]{:S(2)}) %copy-start) | copy-done | bytes 6291480
  15.7 2.8 %copy-done.1 = bf16[1536,2048]{1,0:T(8,128)(2,1)S(1)} copy-done((bf16[1536,2048]{1,0:T(8,128)(2,1)S(1)}, bf16[1536,2048]{1,0:T(8,128)(2,1)}, u32[]{:S(2)}) %copy-start.1) | copy-done | bytes 6291480
  18.5 0.9 shard_map.65
  19.5 0.9 copy-done.2
  20.3 1.2 %shard_map.64 = (bf16[256,1536]{1,0:T(8,128)(2,1)S(1)}, bf16[256,128]{1,0:T(8,128)(2,1)S(1)}, s32[1]{0:T(128)}) custom-call(s32[1]{0:T(128)} %bitcast.at_ref, bf16[32,1664]{1,0:T(8,128)(2,1)S(1)} %copy-done.2, bf16[32,1664]{1,0:T(8,128)(2,1)S(1)} %collective-permute-done.96.refs_1_, bf16[32,1664]{1,0:T(8,128)(2,1)S(1)} %collective-permute-done.97.refs_2_, ...), custom_call_target="tpu_custom_call" | custom-call | flops 268435456 | bytes 1048576 | tf_op jit(solution)/shard_map/pallas_call | solution.py:184
  22.2 4.2 %shard_map.66 = (f32[256,1024]{1,0:T(8,128)S(1)}, f32[256,1024]{1,0:T(8,128)S(1)}, f32[256,1024]{1,0:T(8,128)S(1)}, f32[256,1024]{1,0:T(8,128)S(1)}) custom-call(s32[4]{0:T(128)S(1)} %pad_add_fusion.at_ref, bf16[256,1536]{1,0:T(8,128)(2,1)S(1)} %get-tuple-element.276.rows_ref, bf16[1536,2048]{1,0:T(8,128)(2,1)S(1)} %get-tuple-element.279.gate_ref, ...), custom_call_target="tpu_custom_call" | custom-call | flops 3221225472 | bytes 1048576 | tf_op jit(solution)/shard_map/pallas_call | solution.py:210
  26.3 64.4 %conditional.1 = (f32[4096,2048]{1,0:T(8,128)}) conditional(s32[]{:T(128)} %bitcast.3, (f32[256,1024]{1,0:T(8,128)S(1)}, f32[256,1024]{1,0:T(8,128)S(1)}, f32[256,1024]{1,0:T(8,128)S(1)}, f32[256,1024]{1,0:T(8,128)S(1)}, s32[3]{0:T(128)S(1)}, /*index=5*/bf16[256,128]{1,0:T(8,128)(2,1)S(1)}, s32[2]{0:T(128)S(1)}, ...), branch_computations={%region_0.1_spmd, %region_1.2_spmd, %region_2.3_spmd, %region_3.4_... | conditional | flops 6443237376 | bytes 80085480 | solution.py:392
  27.4 1.7 %collective-permute-done.61.got_ref = f32[208,1024]{1,0:T(8,128)S(1)} collective-permute-done((f32[208,1024]{1,0:T(8,128)S(1)}, f32[208,1024]{1,0:T(8,128)S(1)}, u32[]{:S(2)}, u32[]{:S(2)}) %collective-permute-start.61) | collective-permute-done | bytes 852000 | tf_op jit(solution)/shard_map/cond/branch_5_fun/ppermute | solution.py:90
  29.2 0.6 collective-permute-start.62
  30.3 10.8 %collective-permute-done.62.across_ref = bf16[208,1024]{1,0:T(8,128)(2,1)S(1)} collective-permute-done((bf16[208,1024]{1,0:T(8,128)(2,1)S(1)}, bf16[208,1024]{1,0:T(8,128)(2,1)S(1)}, u32[]{:S(2)}, u32[]{:S(2)}) %collective-permute-start.62) | collective-permute-done | bytes 426016 | tf_op jit(solution)/shard_map/cond/branch_5_fun/ppermute | solution.py:90
  41.4 1.3 %collective-permute-start.66 = (bf16[208,512]{1,0:T(8,128)(2,1)S(1)}, bf16[208,512]{1,0:T(8,128)(2,1)S(1)}, u32[]{:S(2)}, u32[]{:S(2)}) collective-permute-start(bf16[208,512]{1,0:T(8,128)(2,1)S(1)} %branch_5_fun.7.refs_0_), channel_id=1, source_target_pairs={{0,16},{1,17},{4,20},{5,21},{8,24},{9,25},{12,28},{13,29},{18,2},{... | collective-permute-start | bytes 638984 | tf_op jit(solution)/shard_map/cond/branch_5_fun/ppermute | solution.py:90
  42.8 5.1 %collective-permute-start.67 = (bf16[208,512]{1,0:T(8,128)(2,1)S(1)}, bf16[208,512]{1,0:T(8,128)(2,1)S(1)}, u32[]{:S(2)}, u32[]{:S(2)}) collective-permute-start(bf16[208,512]{1,0:T(8,128)(2,1)S(1)} %branch_5_fun.7.refs_0_), channel_id=1, source_target_pairs={{2,16},{3,17},{6,20},{7,21},{10,24},{11,25},{14,28},{15,29},{16,2}... | collective-permute-start | bytes 638984 | tf_op jit(solution)/shard_map/cond/branch_5_fun/ppermute | solution.py:90
  48.0 3.9 %collective-permute-done.66.refs_4_ = bf16[208,512]{1,0:T(8,128)(2,1)S(1)} collective-permute-done((bf16[208,512]{1,0:T(8,128)(2,1)S(1)}, bf16[208,512]{1,0:T(8,128)(2,1)S(1)}, u32[]{:S(2)}, u32[]{:S(2)}) %collective-permute-start.66) | collective-permute-done | bytes 213024 | tf_op jit(solution)/shard_map/cond/branch_5_fun/ppermute | solution.py:90
  52.0 5.1 %collective-permute-done.67.refs_5_ = bf16[208,512]{1,0:T(8,128)(2,1)S(1)} collective-permute-done((bf16[208,512]{1,0:T(8,128)(2,1)S(1)}, bf16[208,512]{1,0:T(8,128)(2,1)S(1)}, u32[]{:S(2)}, u32[]{:S(2)}) %collective-permute-start.67) | collective-permute-done | bytes 213024 | tf_op jit(solution)/shard_map/cond/branch_5_fun/ppermute | solution.py:90
  57.1 1.6 %collective-permute-done.64.refs_1_ = bf16[208,512]{1,0:T(8,128)(2,1)S(1)} collective-permute-done((bf16[208,512]{1,0:T(8,128)(2,1)S(1)}, bf16[208,512]{1,0:T(8,128)(2,1)S(1)}, u32[]{:S(2)}, u32[]{:S(2)}) %collective-permute-start.64) | collective-permute-done | bytes 213024 | tf_op jit(solution)/shard_map/cond/branch_5_fun/ppermute | solution.py:90
  58.7 1.4 %collective-permute-done.65.refs_3_ = bf16[208,512]{1,0:T(8,128)(2,1)S(1)} collective-permute-done((bf16[208,512]{1,0:T(8,128)(2,1)S(1)}, bf16[208,512]{1,0:T(8,128)(2,1)S(1)}, u32[]{:S(2)}, u32[]{:S(2)}) %collective-permute-start.65) | collective-permute-done | bytes 213024 | tf_op jit(solution)/shard_map/cond/branch_5_fun/ppermute | solution.py:90
  60.2 0.8 branch_5_fun.8
  61.0 1.3 %collective-permute-start.71 = (bf16[208,2048]{1,0:T(8,128)(2,1)S(1)}, bf16[208,2048]{1,0:T(8,128)(2,1)S(1)}, u32[]{:S(2)}, u32[]{:S(2)}) collective-permute-start(bf16[208,2048]{1,0:T(8,128)(2,1)S(1)} %get-tuple-element.233.panel_ref), channel_id=1, source_target_pairs={{0,8},{1,4},{2,10},{3,6},{4,12},{5,0},{6,14},{7,2},{8,13},{9,1},{1... | collective-permute-start | bytes 2555912 | tf_op jit(solution)/shard_map/cond/branch_5_fun/ppermute | solution.py:90
  62.3 1.3 %collective-permute-start.70 = (bf16[208,2048]{1,0:T(8,128)(2,1)S(1)}, bf16[208,2048]{1,0:T(8,128)(2,1)S(1)}, u32[]{:S(2)}, u32[]{:S(2)}) collective-permute-start(bf16[208,2048]{1,0:T(8,128)(2,1)S(1)} %get-tuple-element.233.panel_ref), channel_id=1, source_target_pairs={{0,12},{2,14},{4,8},{6,10},{9,5},{11,7},{13,1},{15,3},{16,28},{18,... | collective-permute-start | bytes 2555912 | tf_op jit(solution)/shard_map/cond/branch_5_fun/ppermute | solution.py:90
  63.5 0.6 branch_5_fun.9.refs_0_
  64.1 9.6 %collective-permute-done.71.panel_ref = bf16[208,2048]{1,0:T(8,128)(2,1)S(1)} collective-permute-done((bf16[208,2048]{1,0:T(8,128)(2,1)S(1)}, bf16[208,2048]{1,0:T(8,128)(2,1)S(1)}, u32[]{:S(2)}, u32[]{:S(2)}) %collective-permute-start.71) | collective-permute-done | bytes 852000 | tf_op jit(solution)/shard_map/cond/branch_5_fun/ppermute | solution.py:90
  73.8 6.9 %branch_5_fun.10.refs_0_ = f32[4096,2048]{1,0:T(8,128)} custom-call(s32[2]{0:T(128)S(1)} %get-tuple-element.234.at_ref, bf16[256,128]{1,0:T(8,128)(2,1)S(1)} %get-tuple-element.224.weights_ref, bf16[208,2048]{1,0:T(8,128)(2,1)S(1)} %get-tuple-element.232.columns_ref, ...), custom_call_target="tpu_custom_call", output_to_operand_aliasing={{}: (4, {})} | custom-call | flops 1744830464 | bytes 16777216 | tf_op jit(solution)/shard_map/cond/branch_5_fun/pallas_call | solution.py:332
  80.7 3.1 %collective-permute-done.70.panel_ref = bf16[208,2048]{1,0:T(8,128)(2,1)S(1)} collective-permute-done((bf16[208,2048]{1,0:T(8,128)(2,1)S(1)}, bf16[208,2048]{1,0:T(8,128)(2,1)S(1)}, u32[]{:S(2)}, u32[]{:S(2)}) %collective-permute-start.70) | collective-permute-done | bytes 852000 | tf_op jit(solution)/shard_map/cond/branch_5_fun/ppermute | solution.py:90
  83.8 6.9 %branch_5_fun.11 = f32[4096,2048]{1,0:T(8,128)} custom-call(s32[2]{0:T(128)S(1)} %get-tuple-element.223.at_ref, bf16[256,128]{1,0:T(8,128)(2,1)S(1)} %get-tuple-element.224.weights_ref, bf16[208,2048]{1,0:T(8,128)(2,1)S(1)} %get-tuple-element.232.columns_ref, ...), custom_call_target="tpu_custom_call", output_to_operand_aliasing={{}: (4, {})} | custom-call | flops 1744830464 | bytes 16777216 | tf_op jit(solution)/shard_map/cond/branch_5_fun/pallas_call | solution.py:332
  (29 shorter events, 2.8 us)
Async XLA Ops:
  2.0 7.3 %collective-permute-start.99 = (bf16[32,1664]{1,0:T(8,128)(2,1)}, bf16[32,1664]{1,0:T(8,128)(2,1)S(1)}, u32[]{:S(2)}, u32[]{:S(2)}) collective-permute-start(bf16[32,1664]{1,0:T(8,128)(2,1)} %shard_map.63.refs_0_), channel_id=1, source_target_pairs={{0,16},{1,17},{2,18},{3,19},{4,20},{5,21},{6,22},{7,23},{8,24},{9,... | collective-permute-start | bytes 319496 | tf_op jit(solution)/shard_map/ppermute | solution.py:90
  4.6 7.7 %collective-permute-start.98 = (bf16[32,1664]{1,0:T(8,128)(2,1)}, bf16[32,1664]{1,0:T(8,128)(2,1)S(1)}, u32[]{:S(2)}, u32[]{:S(2)}) collective-permute-start(bf16[32,1664]{1,0:T(8,128)(2,1)} %shard_map.63.refs_0_), channel_id=1, source_target_pairs={{0,12},{1,13},{2,14},{3,15},{4,8},{5,9},{6,10},{7,11},{8,4},{9,5},... | collective-permute-start | bytes 319496 | tf_op jit(solution)/shard_map/ppermute | solution.py:90
  6.0 13.4 %collective-permute-start.97 = (bf16[32,1664]{1,0:T(8,128)(2,1)}, bf16[32,1664]{1,0:T(8,128)(2,1)S(1)}, u32[]{:S(2)}, u32[]{:S(2)}) collective-permute-start(bf16[32,1664]{1,0:T(8,128)(2,1)} %shard_map.63.refs_0_), channel_id=1, source_target_pairs={{0,8},{1,9},{2,10},{3,11},{4,12},{5,13},{6,14},{7,15},{8,0},{9,1},... | collective-permute-start | bytes 319496 | tf_op jit(solution)/shard_map/ppermute | solution.py:90
  7.5 11.9 %collective-permute-start.96 = (bf16[32,1664]{1,0:T(8,128)(2,1)}, bf16[32,1664]{1,0:T(8,128)(2,1)S(1)}, u32[]{:S(2)}, u32[]{:S(2)}) collective-permute-start(bf16[32,1664]{1,0:T(8,128)(2,1)} %shard_map.63.refs_0_), channel_id=1, source_target_pairs={{0,4},{1,5},{2,6},{3,7},{4,0},{5,1},{6,2},{7,3},{8,12},{9,13},{10,... | collective-permute-start | bytes 319496 | tf_op jit(solution)/shard_map/ppermute | solution.py:90
  9.3 10.1 %collective-permute-start.102 = (bf16[32,1664]{1,0:T(8,128)(2,1)S(1)}, bf16[32,1664]{1,0:T(8,128)(2,1)S(1)}, u32[]{:S(2)}, u32[]{:S(2)}) collective-permute-start(bf16[32,1664]{1,0:T(8,128)(2,1)S(1)} %collective-permute-done.99.refs_4_), channel_id=1, source_target_pairs={{0,12},{1,13},{2,14},{3,15},{4,8},{5,9},{6,10},{7,11},{8,4},{9,5},... | collective-permute-start | bytes 319496 | tf_op jit(solution)/shard_map/ppermute | solution.py:90
  11.6 7.9 %collective-permute-start.101 = (bf16[32,1664]{1,0:T(8,128)(2,1)S(1)}, bf16[32,1664]{1,0:T(8,128)(2,1)S(1)}, u32[]{:S(2)}, u32[]{:S(2)}) collective-permute-start(bf16[32,1664]{1,0:T(8,128)(2,1)S(1)} %collective-permute-done.99.refs_4_), channel_id=1, source_target_pairs={{0,8},{1,9},{2,10},{3,11},{4,12},{5,13},{6,14},{7,15},{8,0},{9,1},... | collective-permute-start | bytes 319496 | tf_op jit(solution)/shard_map/ppermute | solution.py:90
  12.3 7.1 %collective-permute-start.100 = (bf16[32,1664]{1,0:T(8,128)(2,1)S(1)}, bf16[32,1664]{1,0:T(8,128)(2,1)S(1)}, u32[]{:S(2)}, u32[]{:S(2)}) collective-permute-start(bf16[32,1664]{1,0:T(8,128)(2,1)S(1)} %collective-permute-done.99.refs_4_), channel_id=1, source_target_pairs={{0,4},{1,5},{2,6},{3,7},{4,0},{5,1},{6,2},{7,3},{8,12},{9,13},{10,... | collective-permute-start | bytes 319496 | tf_op jit(solution)/shard_map/ppermute | solution.py:90
  13.0 2.8 %copy-start = (bf16[1536,2048]{1,0:T(8,128)(2,1)S(1)}, bf16[1536,2048]{1,0:T(8,128)(2,1)}, u32[]{:S(2)}) copy-start(bf16[1536,2048]{1,0:T(8,128)(2,1)} %gate_in) | copy-start | bytes 18874372
  15.7 2.8 %copy-start.1 = (bf16[1536,2048]{1,0:T(8,128)(2,1)S(1)}, bf16[1536,2048]{1,0:T(8,128)(2,1)}, u32[]{:S(2)}) copy-start(bf16[1536,2048]{1,0:T(8,128)(2,1)} %up_in) | copy-start | bytes 18874372
  19.4 0.9 copy-start.2
  26.6 2.4 %collective-permute-start.61 = (f32[208,1024]{1,0:T(8,128)S(1)}, f32[208,1024]{1,0:T(8,128)S(1)}, u32[]{:S(2)}, u32[]{:S(2)}) collective-permute-start(f32[208,1024]{1,0:T(8,128)S(1)} %slice.39), channel_id=1, source_target_pairs={{0,1},{1,0},{2,3},{3,2},{4,5},{5,4},{6,7},{7,6},{8,9},{9,8},{10,11... | collective-permute-start | bytes 2555912 | tf_op jit(solution)/shard_map/cond/branch_5_fun/ppermute | solution.py:90
  26.8 3.5 %collective-permute-start.60 = (f32[208,1024]{1,0:T(8,128)S(1)}, f32[208,1024]{1,0:T(8,128)S(1)}, u32[]{:S(2)}, u32[]{:S(2)}) collective-permute-start(f32[208,1024]{1,0:T(8,128)S(1)} %slice.38), channel_id=1, source_target_pairs={{0,1},{1,0},{2,3},{3,2},{4,5},{5,4},{6,7},{7,6},{8,9},{9,8},{10,11... | collective-permute-start | bytes 2555912 | tf_op jit(solution)/shard_map/cond/branch_5_fun/ppermute | solution.py:90
  29.2 11.9 %collective-permute-start.62 = (bf16[208,1024]{1,0:T(8,128)(2,1)S(1)}, bf16[208,1024]{1,0:T(8,128)(2,1)S(1)}, u32[]{:S(2)}, u32[]{:S(2)}) collective-permute-start(bf16[208,1024]{1,0:T(8,128)(2,1)S(1)} %branch_5_fun.6), channel_id=1, source_target_pairs={{0,2},{1,3},{2,0},{3,1},{4,6},{5,7},{6,4},{7,5},{8,10},{9,11},{10,... | collective-permute-start | bytes 1277960 | tf_op jit(solution)/shard_map/cond/branch_5_fun/ppermute | solution.py:90
  41.3 1.5 %collective-permute-start.63 = (bf16[208,512]{1,0:T(8,128)(2,1)S(1)}, bf16[208,512]{1,0:T(8,128)(2,1)S(1)}, u32[]{:S(2)}, u32[]{:S(2)}) collective-permute-start(bf16[208,512]{1,0:T(8,128)(2,1)S(1)} %branch_5_fun.7.refs_0_), channel_id=1, source_target_pairs={{0,1},{1,0},{2,3},{3,2},{4,5},{5,4},{6,7},{7,6},{8,9},{9,8},{10,11... | collective-permute-start | bytes 638984 | tf_op jit(solution)/shard_map/cond/branch_5_fun/ppermute | solution.py:90
  41.4 10.6 %collective-permute-start.66 = (bf16[208,512]{1,0:T(8,128)(2,1)S(1)}, bf16[208,512]{1,0:T(8,128)(2,1)S(1)}, u32[]{:S(2)}, u32[]{:S(2)}) collective-permute-start(bf16[208,512]{1,0:T(8,128)(2,1)S(1)} %branch_5_fun.7.refs_0_), channel_id=1, source_target_pairs={{0,16},{1,17},{4,20},{5,21},{8,24},{9,25},{12,28},{13,29},{18,2},{... | collective-permute-start | bytes 638984 | tf_op jit(solution)/shard_map/cond/branch_5_fun/ppermute | solution.py:90
  42.8 14.2 %collective-permute-start.67 = (bf16[208,512]{1,0:T(8,128)(2,1)S(1)}, bf16[208,512]{1,0:T(8,128)(2,1)S(1)}, u32[]{:S(2)}, u32[]{:S(2)}) collective-permute-start(bf16[208,512]{1,0:T(8,128)(2,1)S(1)} %branch_5_fun.7.refs_0_), channel_id=1, source_target_pairs={{2,16},{3,17},{6,20},{7,21},{10,24},{11,25},{14,28},{15,29},{16,2}... | collective-permute-start | bytes 638984 | tf_op jit(solution)/shard_map/cond/branch_5_fun/ppermute | solution.py:90
  48.0 10.7 %collective-permute-start.64 = (bf16[208,512]{1,0:T(8,128)(2,1)S(1)}, bf16[208,512]{1,0:T(8,128)(2,1)S(1)}, u32[]{:S(2)}, u32[]{:S(2)}) collective-permute-start(bf16[208,512]{1,0:T(8,128)(2,1)S(1)} %branch_5_fun.7.refs_0_), channel_id=1, source_target_pairs={{0,2},{1,3},{2,0},{3,1},{4,6},{5,7},{6,4},{7,5},{8,10},{9,11},{10,... | collective-permute-start | bytes 638984 | tf_op jit(solution)/shard_map/cond/branch_5_fun/ppermute | solution.py:90
  52.0 6.8 %collective-permute-start.68 = (bf16[208,512]{1,0:T(8,128)(2,1)S(1)}, bf16[208,512]{1,0:T(8,128)(2,1)S(1)}, u32[]{:S(2)}, u32[]{:S(2)}) collective-permute-start(bf16[208,512]{1,0:T(8,128)(2,1)S(1)} %collective-permute-done.66.refs_4_), channel_id=1, source_target_pairs={{0,1},{1,0},{2,3},{3,2},{4,5},{5,4},{6,7},{7,6},{8,9},{9,8},{10,11... | collective-permute-start | bytes 638984 | tf_op jit(solution)/shard_map/cond/branch_5_fun/ppermute | solution.py:90
  57.0 1.7 %collective-permute-start.69 = (bf16[208,512]{1,0:T(8,128)(2,1)S(1)}, bf16[208,512]{1,0:T(8,128)(2,1)S(1)}, u32[]{:S(2)}, u32[]{:S(2)}) collective-permute-start(bf16[208,512]{1,0:T(8,128)(2,1)S(1)} %collective-permute-done.67.refs_5_), channel_id=1, source_target_pairs={{0,1},{1,0},{2,3},{3,2},{4,5},{5,4},{6,7},{7,6},{8,9},{9,8},{10,11... | collective-permute-start | bytes 638984 | tf_op jit(solution)/shard_map/cond/branch_5_fun/ppermute | solution.py:90
  58.7 1.5 %collective-permute-start.65 = (bf16[208,512]{1,0:T(8,128)(2,1)S(1)}, bf16[208,512]{1,0:T(8,128)(2,1)S(1)}, u32[]{:S(2)}, u32[]{:S(2)}) collective-permute-start(bf16[208,512]{1,0:T(8,128)(2,1)S(1)} %collective-permute-done.64.refs_1_), channel_id=1, source_target_pairs={{0,1},{1,0},{2,3},{3,2},{4,5},{5,4},{6,7},{7,6},{8,9},{9,8},{10,11... | collective-permute-start | bytes 638984 | tf_op jit(solution)/shard_map/cond/branch_5_fun/ppermute | solution.py:90
  61.0 12.8 %collective-permute-start.71 = (bf16[208,2048]{1,0:T(8,128)(2,1)S(1)}, bf16[208,2048]{1,0:T(8,128)(2,1)S(1)}, u32[]{:S(2)}, u32[]{:S(2)}) collective-permute-start(bf16[208,2048]{1,0:T(8,128)(2,1)S(1)} %get-tuple-element.233.panel_ref), channel_id=1, source_target_pairs={{0,8},{1,4},{2,10},{3,6},{4,12},{5,0},{6,14},{7,2},{8,13},{9,1},{1... | collective-permute-start | bytes 2555912 | tf_op jit(solution)/shard_map/cond/branch_5_fun/ppermute | solution.py:90
  62.3 21.5 %collective-permute-start.70 = (bf16[208,2048]{1,0:T(8,128)(2,1)S(1)}, bf16[208,2048]{1,0:T(8,128)(2,1)S(1)}, u32[]{:S(2)}, u32[]{:S(2)}) collective-permute-start(bf16[208,2048]{1,0:T(8,128)(2,1)S(1)} %get-tuple-element.233.panel_ref), channel_id=1, source_target_pairs={{0,12},{2,14},{4,8},{6,10},{9,5},{11,7},{13,1},{15,3},{16,28},{18,... | collective-permute-start | bytes 2555912 | tf_op jit(solution)/shard_map/cond/branch_5_fun/ppermute | solution.py:90

commit v5 on v4

--- a/solution.py
+++ b/solution.py
@@ -130,31 +130,26 @@
     return pl.pallas_call(
         pack_kernel,
         out_shape=shaped(CAP, hidden_states.shape[1] + LANES, BF),
+        compiler_params=limit(4),
     )(expert_ids.T, route_gates.T, hidden_states)
 
 
-def load_kernel(gate_in, up_in, gate_ref, up_ref, sems):
-    copies = [
-        pltpu.make_async_copy(gate_in, gate_ref, sems.at[0]),
-        pltpu.make_async_copy(up_in, up_ref, sems.at[1]),
-    ]
-    for copy in copies:
-        copy.start()
-    for copy in copies:
-        copy.wait()
-
-
-def load(gate_weight, up_weight):
-    shape = jax.ShapeDtypeStruct(gate_weight.shape, BF)
+def load_kernel(weight_in, weight_ref, sem):
+    copy = pltpu.make_async_copy(weight_in, weight_ref, sem)
+    copy.start()
+    copy.wait()
+
+
+def load(weight):
     return pl.pallas_call(
         load_kernel,
-        in_specs=[pl.BlockSpec(memory_space=pl.ANY)] * 2,
-        out_specs=[VM, VM],
-        out_shape=[shape, shape],
-        scratch_shapes=[pltpu.SemaphoreType.DMA((2,))],
-        compiler_params=limit(14),
-        cost_estimate=cost(0, 4 * gate_weight.size),
-    )(gate_weight, up_weight)
+        in_specs=[pl.BlockSpec(memory_space=pl.ANY)],
+        out_specs=VM,
+        out_shape=jax.ShapeDtypeStruct(weight.shape, BF),
+        scratch_shapes=[pltpu.SemaphoreType.DMA],
+        compiler_params=limit(44),
+        cost_estimate=cost(0, 2 * weight.size),
+    )(weight)
 
 
 def gather_kernel(sizes, at_ref, *refs):
@@ -382,9 +377,10 @@
         return covariance_part(last_at, weights, columns, last, 2 * units, out)
 
     own = pack(hidden_states, expert_ids, route_gates)
+    gate_weight = load(gate_weight)
     far = send(own, Z2)
-    far, gate_weight, up_weight = lax.optimization_barrier((far, gate_weight, up_weight))
-    gate_weight, up_weight = load(gate_weight, up_weight)
+    far, up_weight = lax.optimization_barrier((far, up_weight))
+    up_weight = load(up_weight)
     blocks = beside(own) + beside(far)
     sizes = [size for size in SIZES if size < 8 * CAP] + [8 * CAP]
     rows, weights, branch = gather(numbers(dp), blocks, sizes)

time: 91.6 us -> 85.2 us (0.930); the launches traced: 90.9 us -> 83.5 us
  waiting for transfers between devices: 39 us -> 34.6 us
  local copies, waits for them, and re-layouts: 6.59 us -> 2.46 us
  Pallas kernels: 23.7 us -> 26.7 us
  starting transfers between devices: 20 us -> 18 us
    pallas_call x1 -> x2, Pallas kernels: 0.86 us -> 5.59 us  [load(): pl.pallas_call(load_kernel, in_specs=[pl.BlockSpec(memory_space=pl.ANY)],...]
    ppermute x19, waiting for transfers between devices: 39 us -> 34.6 us  [send(): return lax.ppermute(value, AXES, route)]
    unnamed x6, local copies, waits for them, and re-layouts: 6.46 us -> 2.35 us
    ppermute x19, starting transfers between devices: 20 us -> 18 us  [send(): return lax.ppermute(value, AXES, route)]
    pallas_call x1, Pallas kernels: 1.99 us -> 0.3 us  [pack(): pl.pallas_call(pack_kernel, out_shape=shaped(CAP, hidden_states.shape[1]...]
  transfers between devices with their start and end apart: 19 -> 19, of which waited for: 11 -> 12; matrix products, arithmetic and copies ran while one was open for 0% -> 0% of each run, Pallas kernels for 9% -> 16%
where the time goes in v5:
time: 85.2 us; the launch traced here: 83.5 us
  waiting for transfers between devices  34.6 us (41%)
  Pallas kernels  26.7 us (31%)
  starting transfers between devices  18 us (21%)
  local copies, waits for them, and re-layouts  2.46 us (3%)
  between operations  0.89 us (1%)
    ppermute x19, waiting for transfers between devices, send(): return lax.ppermute(value, AXES, route)  34.6 us
    ppermute x19, starting transfers between devices, send(): return lax.ppermute(value, AXES, route)  18 us
    pallas_call x3, Pallas kernels, covariance_part(): pl.pallas_call(covariance_kernel, in_specs=in_specs, out_specs=pl.BlockSp...  14.5 us
    pallas_call x2, Pallas kernels, load(): pl.pallas_call(load_kernel, in_specs=[pl.BlockSpec(memory_space=pl.ANY)],...  5.59 us
    pallas_call x1, Pallas kernels, project(): pl.pallas_call(project_kernel, in_specs=[SM, VM, VM, VM], out_specs=[VM]...  4.16 us
    unnamed x6, local copies, waits for them, and re-layouts  2.35 us
  transfers between devices with their start and end apart: 19, of which 12 were waited for; matrix products, arithmetic and copies ran while one was open for 0% of the time, Pallas kernels for 16%

profile of v5, /device:TPU:12, one launch (start us, length us, event | category | flops | bytes accessed | tf_op | source)
XLA Modules:
  0.0 83.5 jit_solution(661326891144992115)
XLA Ops:
  0.0 1.0 %copy-done = bf16[128,1536]{1,0:T(8,128)(2,1)S(1)} copy-done((bf16[128,1536]{1,0:T(8,128)(2,1)S(1)}, bf16[128,1536]{1,0:T(8,128)(2,1)}, u32[]{:S(2)}) %copy-start) | copy-done | bytes 393240
  1.0 0.7 copy-done.1
  1.7 0.7 copy-done.2
  2.7 2.6 %collective-permute-start.99 = (bf16[32,1664]{1,0:T(8,128)(2,1)S(1)}, bf16[32,1664]{1,0:T(8,128)(2,1)S(1)}, u32[]{:S(2)}, u32[]{:S(2)}) collective-permute-start(bf16[32,1664]{1,0:T(8,128)(2,1)S(1)} %shard_map.63.refs_0_), channel_id=1, source_target_pairs={{0,16},{1,17},{2,18},{3,19},{4,20},{5,21},{6,22},{7,23},{8,24},{9,... | collective-permute-start | bytes 319496 | tf_op jit(solution)/shard_map/ppermute | solution.py:90
  5.3 1.4 %collective-permute-start.98 = (bf16[32,1664]{1,0:T(8,128)(2,1)S(1)}, bf16[32,1664]{1,0:T(8,128)(2,1)S(1)}, u32[]{:S(2)}, u32[]{:S(2)}) collective-permute-start(bf16[32,1664]{1,0:T(8,128)(2,1)S(1)} %shard_map.63.refs_0_), channel_id=1, source_target_pairs={{0,12},{1,13},{2,14},{3,15},{4,8},{5,9},{6,10},{7,11},{8,4},{9,5},... | collective-permute-start | bytes 319496 | tf_op jit(solution)/shard_map/ppermute | solution.py:90
  6.7 1.6 %collective-permute-start.97 = (bf16[32,1664]{1,0:T(8,128)(2,1)S(1)}, bf16[32,1664]{1,0:T(8,128)(2,1)S(1)}, u32[]{:S(2)}, u32[]{:S(2)}) collective-permute-start(bf16[32,1664]{1,0:T(8,128)(2,1)S(1)} %shard_map.63.refs_0_), channel_id=1, source_target_pairs={{0,8},{1,9},{2,10},{3,11},{4,12},{5,13},{6,14},{7,15},{8,0},{9,1},... | collective-permute-start | bytes 319496 | tf_op jit(solution)/shard_map/ppermute | solution.py:90
  8.8 2.8 %shard_map.65.gate_ref = bf16[1536,2048]{1,0:T(8,128)(2,1)S(1)} custom-call(bf16[1536,2048]{1,0:T(8,128)(2,1)} %weight_in.1), custom_call_target="tpu_custom_call" | custom-call | bytes 6291456 | tf_op jit(solution)/shard_map/pallas_call | solution.py:144
  11.8 1.4 %collective-permute-start.102 = (bf16[32,1664]{1,0:T(8,128)(2,1)S(1)}, bf16[32,1664]{1,0:T(8,128)(2,1)S(1)}, u32[]{:S(2)}, u32[]{:S(2)}) collective-permute-start(bf16[32,1664]{1,0:T(8,128)(2,1)S(1)} %collective-permute-done.99.refs_4_), channel_id=1, source_target_pairs={{0,12},{1,13},{2,14},{3,15},{4,8},{5,9},{6,10},{7,11},{8,4},{9,5},... | collective-permute-start | bytes 319496 | tf_op jit(solution)/shard_map/ppermute | solution.py:90
  13.2 1.6 %collective-permute-start.101 = (bf16[32,1664]{1,0:T(8,128)(2,1)S(1)}, bf16[32,1664]{1,0:T(8,128)(2,1)S(1)}, u32[]{:S(2)}, u32[]{:S(2)}) collective-permute-start(bf16[32,1664]{1,0:T(8,128)(2,1)S(1)} %collective-permute-done.99.refs_4_), channel_id=1, source_target_pairs={{0,8},{1,9},{2,10},{3,11},{4,12},{5,13},{6,14},{7,15},{8,0},{9,1},... | collective-permute-start | bytes 319496 | tf_op jit(solution)/shard_map/ppermute | solution.py:90
  15.4 2.8 %shard_map.66.up_ref = bf16[1536,2048]{1,0:T(8,128)(2,1)S(1)} custom-call(bf16[1536,2048]{1,0:T(8,128)(2,1)} %weight_in.2), custom_call_target="tpu_custom_call" | custom-call | bytes 6291456 | tf_op jit(solution)/shard_map/pallas_call | solution.py:144
  18.7 0.9 %collective-permute-done.100.refs_5_ = bf16[32,1664]{1,0:T(8,128)(2,1)S(1)} collective-permute-done((bf16[32,1664]{1,0:T(8,128)(2,1)S(1)}, bf16[32,1664]{1,0:T(8,128)(2,1)S(1)}, u32[]{:S(2)}, u32[]{:S(2)}) %collective-permute-start.100) | collective-permute-done | bytes 106528 | tf_op jit(solution)/shard_map/ppermute | solution.py:90
  19.5 1.2 %shard_map.64 = (bf16[256,1536]{1,0:T(8,128)(2,1)S(1)}, bf16[256,128]{1,0:T(8,128)(2,1)S(1)}, s32[1]{0:T(128)}) custom-call(s32[1]{0:T(128)} %bitcast.at_ref, bf16[32,1664]{1,0:T(8,128)(2,1)S(1)} %shard_map.63.refs_0_, bf16[32,1664]{1,0:T(8,128)(2,1)S(1)} %collective-permute-done.96.refs_1_, bf16[32,1664]{1,0:T(8,128)(2,1)S(1)} %collective-permute-done.97.refs_2_, ...), custom_call_target="tpu_custom_call" | custom-call | flops 268435456 | bytes 1048576 | tf_op jit(solution)/shard_map/pallas_call | solution.py:179
  21.3 4.2 %shard_map.67 = (f32[256,1024]{1,0:T(8,128)S(1)}, f32[256,1024]{1,0:T(8,128)S(1)}, f32[256,1024]{1,0:T(8,128)S(1)}, f32[256,1024]{1,0:T(8,128)S(1)}) custom-call(s32[4]{0:T(128)S(1)} %pad_add_fusion.at_ref, bf16[256,1536]{1,0:T(8,128)(2,1)S(1)} %get-tuple-element.273.rows_ref, bf16[1536,2048]{1,0:T(8,128)(2,1)S(1)} %shard_map.65.gate_ref, ...), custom_call_target="tpu_custom_call" | custom-call | flops 3221225472 | bytes 1048576 | tf_op jit(solution)/shard_map/pallas_call | solution.py:205
  25.5 57.9 %conditional.1 = (f32[4096,2048]{1,0:T(8,128)}) conditional(s32[]{:T(128)} %bitcast.3, (f32[256,1024]{1,0:T(8,128)S(1)}, f32[256,1024]{1,0:T(8,128)S(1)}, f32[256,1024]{1,0:T(8,128)S(1)}, f32[256,1024]{1,0:T(8,128)S(1)}, s32[3]{0:T(128)S(1)}, /*index=5*/bf16[256,128]{1,0:T(8,128)(2,1)S(1)}, s32[2]{0:T(128)S(1)}, ...), branch_computations={%region_0.1_spmd, %region_1.2_spmd, %region_2.3_spmd, %region_3.4_... | conditional | flops 6443237376 | bytes 80085480 | solution.py:388
  25.9 0.6 collective-permute-start.36
  26.5 1.5 %collective-permute-done.37.got_ref = f32[176,1024]{1,0:T(8,128)S(1)} collective-permute-done((f32[176,1024]{1,0:T(8,128)S(1)}, f32[176,1024]{1,0:T(8,128)S(1)}, u32[]{:S(2)}, u32[]{:S(2)}) %collective-permute-start.37) | collective-permute-done | bytes 720928 | tf_op jit(solution)/shard_map/cond/branch_3_fun/ppermute | solution.py:90
  28.1 0.6 collective-permute-start.38
  29.0 9.6 %collective-permute-done.38.across_ref = bf16[176,1024]{1,0:T(8,128)(2,1)S(1)} collective-permute-done((bf16[176,1024]{1,0:T(8,128)(2,1)S(1)}, bf16[176,1024]{1,0:T(8,128)(2,1)S(1)}, u32[]{:S(2)}, u32[]{:S(2)}) %collective-permute-start.38) | collective-permute-done | bytes 360480 | tf_op jit(solution)/shard_map/cond/branch_3_fun/ppermute | solution.py:90
  38.9 1.3 %collective-permute-start.42 = (bf16[176,512]{1,0:T(8,128)(2,1)S(1)}, bf16[176,512]{1,0:T(8,128)(2,1)S(1)}, u32[]{:S(2)}, u32[]{:S(2)}) collective-permute-start(bf16[176,512]{1,0:T(8,128)(2,1)S(1)} %branch_3_fun.7.refs_0_), channel_id=1, source_target_pairs={{0,16},{1,17},{4,20},{5,21},{8,24},{9,25},{12,28},{13,29},{18,2},{... | collective-permute-start | bytes 540680 | tf_op jit(solution)/shard_map/cond/branch_3_fun/ppermute | solution.py:90
  40.3 3.6 %collective-permute-start.43 = (bf16[176,512]{1,0:T(8,128)(2,1)S(1)}, bf16[176,512]{1,0:T(8,128)(2,1)S(1)}, u32[]{:S(2)}, u32[]{:S(2)}) collective-permute-start(bf16[176,512]{1,0:T(8,128)(2,1)S(1)} %branch_3_fun.7.refs_0_), channel_id=1, source_target_pairs={{2,16},{3,17},{6,20},{7,21},{10,24},{11,25},{14,28},{15,29},{16,2}... | collective-permute-start | bytes 540680 | tf_op jit(solution)/shard_map/cond/branch_3_fun/ppermute | solution.py:90
  44.0 4.7 %collective-permute-done.42.refs_4_ = bf16[176,512]{1,0:T(8,128)(2,1)S(1)} collective-permute-done((bf16[176,512]{1,0:T(8,128)(2,1)S(1)}, bf16[176,512]{1,0:T(8,128)(2,1)S(1)}, u32[]{:S(2)}, u32[]{:S(2)}) %collective-permute-start.42) | collective-permute-done | bytes 180256 | tf_op jit(solution)/shard_map/cond/branch_3_fun/ppermute | solution.py:90
  48.7 3.1 %collective-permute-done.43.refs_5_ = bf16[176,512]{1,0:T(8,128)(2,1)S(1)} collective-permute-done((bf16[176,512]{1,0:T(8,128)(2,1)S(1)}, bf16[176,512]{1,0:T(8,128)(2,1)S(1)}, u32[]{:S(2)}, u32[]{:S(2)}) %collective-permute-start.43) | collective-permute-done | bytes 180256 | tf_op jit(solution)/shard_map/cond/branch_3_fun/ppermute | solution.py:90
  51.9 2.6 %collective-permute-done.40.refs_1_ = bf16[176,512]{1,0:T(8,128)(2,1)S(1)} collective-permute-done((bf16[176,512]{1,0:T(8,128)(2,1)S(1)}, bf16[176,512]{1,0:T(8,128)(2,1)S(1)}, u32[]{:S(2)}, u32[]{:S(2)}) %collective-permute-start.40) | collective-permute-done | bytes 180256 | tf_op jit(solution)/shard_map/cond/branch_3_fun/ppermute | solution.py:90
  54.5 1.4 %collective-permute-done.41.refs_3_ = bf16[176,512]{1,0:T(8,128)(2,1)S(1)} collective-permute-done((bf16[176,512]{1,0:T(8,128)(2,1)S(1)}, bf16[176,512]{1,0:T(8,128)(2,1)S(1)}, u32[]{:S(2)}, u32[]{:S(2)}) %collective-permute-start.41) | collective-permute-done | bytes 180256 | tf_op jit(solution)/shard_map/cond/branch_3_fun/ppermute | solution.py:90
  55.9 0.8 branch_3_fun.8
  56.7 0.8 collective-permute-start.47
  57.5 1.3 %collective-permute-start.46 = (bf16[176,2048]{1,0:T(8,128)(2,1)S(1)}, bf16[176,2048]{1,0:T(8,128)(2,1)S(1)}, u32[]{:S(2)}, u32[]{:S(2)}) collective-permute-start(bf16[176,2048]{1,0:T(8,128)(2,1)S(1)} %get-tuple-element.207.panel_ref), channel_id=1, source_target_pairs={{0,12},{2,14},{4,8},{6,10},{9,5},{11,7},{13,1},{15,3},{16,28},{18,... | collective-permute-start | bytes 2162696 | tf_op jit(solution)/shard_map/cond/branch_3_fun/ppermute | solution.py:90
  58.8 0.6 branch_3_fun.9.refs_0_
  59.4 8.7 %collective-permute-done.47.panel_ref = bf16[176,2048]{1,0:T(8,128)(2,1)S(1)} collective-permute-done((bf16[176,2048]{1,0:T(8,128)(2,1)S(1)}, bf16[176,2048]{1,0:T(8,128)(2,1)S(1)}, u32[]{:S(2)}, u32[]{:S(2)}) %collective-permute-start.47) | collective-permute-done | bytes 720928 | tf_op jit(solution)/shard_map/cond/branch_3_fun/ppermute | solution.py:90
  68.1 6.9 %branch_3_fun.10.refs_0_ = f32[4096,2048]{1,0:T(8,128)} custom-call(s32[2]{0:T(128)S(1)} %get-tuple-element.208.at_ref, bf16[256,128]{1,0:T(8,128)(2,1)S(1)} %get-tuple-element.198.weights_ref, bf16[176,2048]{1,0:T(8,128)(2,1)S(1)} %get-tuple-element.206.columns_ref, ...), custom_call_target="tpu_custom_call", output_to_operand_aliasing={{}: (4, {})} | custom-call | flops 1476395008 | bytes 16777216 | tf_op jit(solution)/shard_map/cond/branch_3_fun/pallas_call | solution.py:327
  75.0 1.2 %collective-permute-done.46.panel_ref = bf16[176,2048]{1,0:T(8,128)(2,1)S(1)} collective-permute-done((bf16[176,2048]{1,0:T(8,128)(2,1)S(1)}, bf16[176,2048]{1,0:T(8,128)(2,1)S(1)}, u32[]{:S(2)}, u32[]{:S(2)}) %collective-permute-start.46) | collective-permute-done | bytes 720928 | tf_op jit(solution)/shard_map/cond/branch_3_fun/ppermute | solution.py:90
  76.2 6.9 %branch_3_fun.11 = f32[4096,2048]{1,0:T(8,128)} custom-call(s32[2]{0:T(128)S(1)} %get-tuple-element.197.at_ref, bf16[256,128]{1,0:T(8,128)(2,1)S(1)} %get-tuple-element.198.weights_ref, bf16[176,2048]{1,0:T(8,128)(2,1)S(1)} %get-tuple-element.206.columns_ref, ...), custom_call_target="tpu_custom_call", output_to_operand_aliasing={{}: (4, {})} | custom-call | flops 1476395008 | bytes 16777216 | tf_op jit(solution)/shard_map/cond/branch_3_fun/pallas_call | solution.py:327
  (30 shorter events, 3.2 us)
Async XLA Ops:
  0.0 1.0 %copy-start = (bf16[128,1536]{1,0:T(8,128)(2,1)S(1)}, bf16[128,1536]{1,0:T(8,128)(2,1)}, u32[]{:S(2)}) copy-start(bf16[128,1536]{1,0:T(8,128)(2,1)} %tokens_ref.1) | copy-start | bytes 1179652
  1.0 0.7 copy-start.1
  1.7 0.7 copy-start.2
  2.7 9.2 %collective-permute-start.99 = (bf16[32,1664]{1,0:T(8,128)(2,1)S(1)}, bf16[32,1664]{1,0:T(8,128)(2,1)S(1)}, u32[]{:S(2)}, u32[]{:S(2)}) collective-permute-start(bf16[32,1664]{1,0:T(8,128)(2,1)S(1)} %shard_map.63.refs_0_), channel_id=1, source_target_pairs={{0,16},{1,17},{2,18},{3,19},{4,20},{5,21},{6,22},{7,23},{8,24},{9,... | collective-permute-start | bytes 319496 | tf_op jit(solution)/shard_map/ppermute | solution.py:90
  5.3 9.5 %collective-permute-start.98 = (bf16[32,1664]{1,0:T(8,128)(2,1)S(1)}, bf16[32,1664]{1,0:T(8,128)(2,1)S(1)}, u32[]{:S(2)}, u32[]{:S(2)}) collective-permute-start(bf16[32,1664]{1,0:T(8,128)(2,1)S(1)} %shard_map.63.refs_0_), channel_id=1, source_target_pairs={{0,12},{1,13},{2,14},{3,15},{4,8},{5,9},{6,10},{7,11},{8,4},{9,5},... | collective-permute-start | bytes 319496 | tf_op jit(solution)/shard_map/ppermute | solution.py:90
  6.7 11.5 %collective-permute-start.97 = (bf16[32,1664]{1,0:T(8,128)(2,1)S(1)}, bf16[32,1664]{1,0:T(8,128)(2,1)S(1)}, u32[]{:S(2)}, u32[]{:S(2)}) collective-permute-start(bf16[32,1664]{1,0:T(8,128)(2,1)S(1)} %shard_map.63.refs_0_), channel_id=1, source_target_pairs={{0,8},{1,9},{2,10},{3,11},{4,12},{5,13},{6,14},{7,15},{8,0},{9,1},... | collective-permute-start | bytes 319496 | tf_op jit(solution)/shard_map/ppermute | solution.py:90
  8.3 10.0 %collective-permute-start.96 = (bf16[32,1664]{1,0:T(8,128)(2,1)S(1)}, bf16[32,1664]{1,0:T(8,128)(2,1)S(1)}, u32[]{:S(2)}, u32[]{:S(2)}) collective-permute-start(bf16[32,1664]{1,0:T(8,128)(2,1)S(1)} %shard_map.63.refs_0_), channel_id=1, source_target_pairs={{0,4},{1,5},{2,6},{3,7},{4,0},{5,1},{6,2},{7,3},{8,12},{9,13},{10,... | collective-permute-start | bytes 319496 | tf_op jit(solution)/shard_map/ppermute | solution.py:90
  11.8 6.4 %collective-permute-start.102 = (bf16[32,1664]{1,0:T(8,128)(2,1)S(1)}, bf16[32,1664]{1,0:T(8,128)(2,1)S(1)}, u32[]{:S(2)}, u32[]{:S(2)}) collective-permute-start(bf16[32,1664]{1,0:T(8,128)(2,1)S(1)} %collective-permute-done.99.refs_4_), channel_id=1, source_target_pairs={{0,12},{1,13},{2,14},{3,15},{4,8},{5,9},{6,10},{7,11},{8,4},{9,5},... | collective-permute-start | bytes 319496 | tf_op jit(solution)/shard_map/ppermute | solution.py:90
  13.2 5.4 %collective-permute-start.101 = (bf16[32,1664]{1,0:T(8,128)(2,1)S(1)}, bf16[32,1664]{1,0:T(8,128)(2,1)S(1)}, u32[]{:S(2)}, u32[]{:S(2)}) collective-permute-start(bf16[32,1664]{1,0:T(8,128)(2,1)S(1)} %collective-permute-done.99.refs_4_), channel_id=1, source_target_pairs={{0,8},{1,9},{2,10},{3,11},{4,12},{5,13},{6,14},{7,15},{8,0},{9,1},... | collective-permute-start | bytes 319496 | tf_op jit(solution)/shard_map/ppermute | solution.py:90
  14.8 4.7 %collective-permute-start.100 = (bf16[32,1664]{1,0:T(8,128)(2,1)S(1)}, bf16[32,1664]{1,0:T(8,128)(2,1)S(1)}, u32[]{:S(2)}, u32[]{:S(2)}) collective-permute-start(bf16[32,1664]{1,0:T(8,128)(2,1)S(1)} %collective-permute-done.99.refs_4_), channel_id=1, source_target_pairs={{0,4},{1,5},{2,6},{3,7},{4,0},{5,1},{6,2},{7,3},{8,12},{9,13},{10,... | collective-permute-start | bytes 319496 | tf_op jit(solution)/shard_map/ppermute | solution.py:90
  25.8 2.3 %collective-permute-start.37 = (f32[176,1024]{1,0:T(8,128)S(1)}, f32[176,1024]{1,0:T(8,128)S(1)}, u32[]{:S(2)}, u32[]{:S(2)}) collective-permute-start(f32[176,1024]{1,0:T(8,128)S(1)} %slice.35), channel_id=1, source_target_pairs={{0,1},{1,0},{2,3},{3,2},{4,5},{5,4},{6,7},{7,6},{8,9},{9,8},{10,11... | collective-permute-start | bytes 2162696 | tf_op jit(solution)/shard_map/cond/branch_3_fun/ppermute | solution.py:90
  25.9 3.1 %collective-permute-start.36 = (f32[176,1024]{1,0:T(8,128)S(1)}, f32[176,1024]{1,0:T(8,128)S(1)}, u32[]{:S(2)}, u32[]{:S(2)}) collective-permute-start(f32[176,1024]{1,0:T(8,128)S(1)} %slice.34), channel_id=1, source_target_pairs={{0,1},{1,0},{2,3},{3,2},{4,5},{5,4},{6,7},{7,6},{8,9},{9,8},{10,11... | collective-permute-start | bytes 2162696 | tf_op jit(solution)/shard_map/cond/branch_3_fun/ppermute | solution.py:90
  28.1 10.5 %collective-permute-start.38 = (bf16[176,1024]{1,0:T(8,128)(2,1)S(1)}, bf16[176,1024]{1,0:T(8,128)(2,1)S(1)}, u32[]{:S(2)}, u32[]{:S(2)}) collective-permute-start(bf16[176,1024]{1,0:T(8,128)(2,1)S(1)} %branch_3_fun.6), channel_id=1, source_target_pairs={{0,2},{1,3},{2,0},{3,1},{4,6},{5,7},{6,4},{7,5},{8,10},{9,11},{10,... | collective-permute-start | bytes 1081352 | tf_op jit(solution)/shard_map/cond/branch_3_fun/ppermute | solution.py:90
  38.8 1.5 %collective-permute-start.39 = (bf16[176,512]{1,0:T(8,128)(2,1)S(1)}, bf16[176,512]{1,0:T(8,128)(2,1)S(1)}, u32[]{:S(2)}, u32[]{:S(2)}) collective-permute-start(bf16[176,512]{1,0:T(8,128)(2,1)S(1)} %branch_3_fun.7.refs_0_), channel_id=1, source_target_pairs={{0,1},{1,0},{2,3},{3,2},{4,5},{5,4},{6,7},{7,6},{8,9},{9,8},{10,11... | collective-permute-start | bytes 540680 | tf_op jit(solution)/shard_map/cond/branch_3_fun/ppermute | solution.py:90
  38.9 9.8 %collective-permute-start.42 = (bf16[176,512]{1,0:T(8,128)(2,1)S(1)}, bf16[176,512]{1,0:T(8,128)(2,1)S(1)}, u32[]{:S(2)}, u32[]{:S(2)}) collective-permute-start(bf16[176,512]{1,0:T(8,128)(2,1)S(1)} %branch_3_fun.7.refs_0_), channel_id=1, source_target_pairs={{0,16},{1,17},{4,20},{5,21},{8,24},{9,25},{12,28},{13,29},{18,2},{... | collective-permute-start | bytes 540680 | tf_op jit(solution)/shard_map/cond/branch_3_fun/ppermute | solution.py:90
  40.3 11.6 %collective-permute-start.43 = (bf16[176,512]{1,0:T(8,128)(2,1)S(1)}, bf16[176,512]{1,0:T(8,128)(2,1)S(1)}, u32[]{:S(2)}, u32[]{:S(2)}) collective-permute-start(bf16[176,512]{1,0:T(8,128)(2,1)S(1)} %branch_3_fun.7.refs_0_), channel_id=1, source_target_pairs={{2,16},{3,17},{6,20},{7,21},{10,24},{11,25},{14,28},{15,29},{16,2}... | collective-permute-start | bytes 540680 | tf_op jit(solution)/shard_map/cond/branch_3_fun/ppermute | solution.py:90
  44.0 10.5 %collective-permute-start.40 = (bf16[176,512]{1,0:T(8,128)(2,1)S(1)}, bf16[176,512]{1,0:T(8,128)(2,1)S(1)}, u32[]{:S(2)}, u32[]{:S(2)}) collective-permute-start(bf16[176,512]{1,0:T(8,128)(2,1)S(1)} %branch_3_fun.7.refs_0_), channel_id=1, source_target_pairs={{0,2},{1,3},{2,0},{3,1},{4,6},{5,7},{6,4},{7,5},{8,10},{9,11},{10,... | collective-permute-start | bytes 540680 | tf_op jit(solution)/shard_map/cond/branch_3_fun/ppermute | solution.py:90
  48.7 5.8 %collective-permute-start.44 = (bf16[176,512]{1,0:T(8,128)(2,1)S(1)}, bf16[176,512]{1,0:T(8,128)(2,1)S(1)}, u32[]{:S(2)}, u32[]{:S(2)}) collective-permute-start(bf16[176,512]{1,0:T(8,128)(2,1)S(1)} %collective-permute-done.42.refs_4_), channel_id=1, source_target_pairs={{0,1},{1,0},{2,3},{3,2},{4,5},{5,4},{6,7},{7,6},{8,9},{9,8},{10,11... | collective-permute-start | bytes 540680 | tf_op jit(solution)/shard_map/cond/branch_3_fun/ppermute | solution.py:90
  51.9 2.6 %collective-permute-start.45 = (bf16[176,512]{1,0:T(8,128)(2,1)S(1)}, bf16[176,512]{1,0:T(8,128)(2,1)S(1)}, u32[]{:S(2)}, u32[]{:S(2)}) collective-permute-start(bf16[176,512]{1,0:T(8,128)(2,1)S(1)} %collective-permute-done.43.refs_5_), channel_id=1, source_target_pairs={{0,1},{1,0},{2,3},{3,2},{4,5},{5,4},{6,7},{7,6},{8,9},{9,8},{10,11... | collective-permute-start | bytes 540680 | tf_op jit(solution)/shard_map/cond/branch_3_fun/ppermute | solution.py:90
  54.5 1.4 %collective-permute-start.41 = (bf16[176,512]{1,0:T(8,128)(2,1)S(1)}, bf16[176,512]{1,0:T(8,128)(2,1)S(1)}, u32[]{:S(2)}, u32[]{:S(2)}) collective-permute-start(bf16[176,512]{1,0:T(8,128)(2,1)S(1)} %collective-permute-done.40.refs_1_), channel_id=1, source_target_pairs={{0,1},{1,0},{2,3},{3,2},{4,5},{5,4},{6,7},{7,6},{8,9},{9,8},{10,11... | collective-permute-start | bytes 540680 | tf_op jit(solution)/shard_map/cond/branch_3_fun/ppermute | solution.py:90
  56.7 11.3 %collective-permute-start.47 = (bf16[176,2048]{1,0:T(8,128)(2,1)S(1)}, bf16[176,2048]{1,0:T(8,128)(2,1)S(1)}, u32[]{:S(2)}, u32[]{:S(2)}) collective-permute-start(bf16[176,2048]{1,0:T(8,128)(2,1)S(1)} %get-tuple-element.207.panel_ref), channel_id=1, source_target_pairs={{0,8},{1,4},{2,10},{3,6},{4,12},{5,0},{6,14},{7,2},{8,13},{9,1},{1... | collective-permute-start | bytes 2162696 | tf_op jit(solution)/shard_map/cond/branch_3_fun/ppermute | solution.py:90
  57.5 18.7 %collective-permute-start.46 = (bf16[176,2048]{1,0:T(8,128)(2,1)S(1)}, bf16[176,2048]{1,0:T(8,128)(2,1)S(1)}, u32[]{:S(2)}, u32[]{:S(2)}) collective-permute-start(bf16[176,2048]{1,0:T(8,128)(2,1)S(1)} %get-tuple-element.207.panel_ref), channel_id=1, source_target_pairs={{0,12},{2,14},{4,8},{6,10},{9,5},{11,7},{13,1},{15,3},{16,28},{18,... | collective-permute-start | bytes 2162696 | tf_op jit(solution)/shard_map/cond/branch_3_fun/ppermute | solution.py:90
